TPU v7x, 32 devices: a whole 2x2x4 slice. The times are simulated.
32 devices in a mesh: tok: 8 (over z, core), ch: 4 (over y, x).
Axes of the slice: x: 2, y: 2, z: 4, core: 2. Of those that a mesh axis runs over, the one named last changes fastest.
Arguments:
- layer_in: bfloat16 [8192, 2048], P('tok', 'ch'), may hold values from -6 to 6
- positions: int32 [8192], P('tok'), may hold values from 0 to 3071, as said below
- norm_gain: float32 [2048], replicated, may hold values from 0.25 to 1.75
- w_branch: bfloat16 [2048, 2560], P(None, 'ch'), may hold values from -0.125 to 0.125
- w_gelu: bfloat16 [2048, 2560], P(None, 'ch'), may hold values from -0.125 to 0.125
- conv_w: float32 [4, 2560], P(None, 'ch'), may hold values from -3 to 3
- conv_b: float32 [2560], P('ch'), may hold values from -3 to 3
- w_rgate: bfloat16 [16, 160, 160], P('ch'), may hold values from -0.5 to 0.5
- b_rgate: float32 [2560], P('ch'), may hold values from -4 to 4
- w_igate: bfloat16 [16, 160, 160], P('ch'), may hold values from -0.5 to 0.5
- b_igate: float32 [2560], P('ch'), may hold values from -4 to 4
- decay_param: float32 [2560], P('ch'), may hold values from 3.5 to 11
- w_out: bfloat16 [2560, 2048], P('ch'), may hold values from -0.25 to 0.25
- mlp_gain: float32 [2048], replicated, may hold values from 0.25 to 1.75
- w_gate: bfloat16 [2048, 6144], P(None, 'ch'), may hold values from -0.125 to 0.125
- w_up: bfloat16 [2048, 6144], P(None, 'ch'), may hold values from -0.125 to 0.125
- w_down: bfloat16 [6144, 2048], P('ch'), may hold values from -0.15625 to 0.15625
- cotangent: bfloat16 [8192, 2048], P('tok', 'ch'), may hold values from -6 to 6
Outputs:
- layer_out: bfloat16 [8192, 2048], P('tok', 'ch')
- input_grad: float32 [8192, 2048], P('tok', 'ch')
- norm_gain_grad: float32 [2048], P('ch')
- w_branch_grad: float32 [2048, 2560], P('tok', 'ch')
- w_gelu_grad: float32 [2048, 2560], P('tok', 'ch')
- conv_w_grad: float32 [4, 2560], P(None, 'ch')
- conv_b_grad: float32 [2560], P('ch')
- w_rgate_grad: float32 [16, 160, 160], P('ch', 'tok')
- b_rgate_grad: float32 [2560], P('ch')
- w_igate_grad: float32 [16, 160, 160], P('ch', 'tok')
- b_igate_grad: float32 [2560], P('ch')
- decay_grad: float32 [2560], P('ch')
- w_out_grad: float32 [2560, 2048], P('ch', 'tok')
- mlp_gain_grad: float32 [2048], P('ch')
- w_gate_grad: float32 [2048, 6144], P('tok', 'ch')
- w_up_grad: float32 [2048, 6144], P('tok', 'ch')
- w_down_grad: float32 [6144, 2048], P('ch', 'tok')
Inputs may be any that keep to these rules, and one draw needn't show every extreme that they name: positions count 0, 1, 2 and so on along each sequence; the sequences lie end to end from the first token to the last, each has 1024 tokens or more, and the longest reaches the largest position.
All inputs are finite; a program needn't handle non-finite values.
Results may differ from a plain program's by a relative error of at most 0.0093.
Values may be sent and summed in bfloat16 or wider, within the bound.
A program may use at most 256 MiB of HBM per device.

v0:
```python
import jax
import jax.numpy as jnp
from jax import lax
from jax.sharding import PartitionSpec as P


def shifted(block, axis, distance):
    devices = range(lax.axis_size(axis))
    route = [(i - distance, i) for i in devices if i - distance in devices]
    return lax.ppermute(block, axis, route)


def carried_in(part, axis, combine, identity, reverse):
    count = lax.axis_size(axis)
    place = lax.axis_index(axis)
    ahead = count - 1 - place if reverse else place
    gathered = jax.tree.map(lambda a: lax.all_gather(a, axis), part)
    state = jax.tree.map(lambda a, e: jnp.zeros_like(a) + jnp.asarray(e, a.dtype), part, identity)

    def one(step, state):
        source = count - 1 - step if reverse else step
        return combine(
            state, jax.tree.map(lambda a: lax.dynamic_index_in_dim(a, source, 0, False), gathered)
        )

    return lax.fori_loop(0, ahead, one, state)


def rms_norm(values, gain_vec):
    return values * lax.rsqrt(jnp.mean(values * values, axis=-1, keepdims=True) + 1e-06) * gain_vec


def combine(earlier, latter):
    return (earlier[0] * latter[0], latter[0] * earlier[1] + latter[1])


def gate_terms(pre_rate, pre_input, conv_out, decay_param, keep_mask):
    rate_gate = jax.nn.sigmoid(pre_rate)
    input_gate = jax.nn.sigmoid(pre_input)
    log_decay = -8.0 * rate_gate * jax.nn.softplus(-decay_param)
    decay_val = jnp.exp(log_decay)
    norm_scale = jnp.where(keep_mask > 0, jnp.sqrt(-jnp.expm1(2.0 * log_decay)), 1.0)
    return (decay_val * keep_mask, input_gate * conv_out * norm_scale)


def gated_unit(gate_in, up_in):
    return jax.nn.gelu(gate_in) * up_in


def block_product(values, blocks):
    shaped = values.reshape(values.shape[0], blocks.shape[0], blocks.shape[1])
    return jnp.einsum("tnb,nbc->tnc", shaped, blocks, preferred_element_type=jnp.float32).reshape(
        values.shape[0], -1
    )


def block_back(grads_in, blocks):
    shaped = grads_in.reshape(grads_in.shape[0], blocks.shape[0], blocks.shape[2])
    return jnp.einsum("tnc,nbc->tnb", shaped, blocks, preferred_element_type=jnp.float32).reshape(
        grads_in.shape[0], -1
    )


def block_weights(values, grads_in, blocks):
    shaped = values.reshape(values.shape[0], blocks.shape[0], blocks.shape[1])
    grads_shaped = grads_in.reshape(grads_in.shape[0], blocks.shape[0], blocks.shape[2])
    return jnp.einsum("tnb,tnc->nbc", shaped, grads_shaped, preferred_element_type=jnp.float32)


def left_product(first_in, second_in):
    return lax.dot_general(
        first_in, second_in, (((0,), (0,)), ((), ())), preferred_element_type=jnp.float32
    )


def right_product(first_in, second_in):
    return lax.dot_general(
        first_in, second_in, (((1,), (1,)), ((), ())), preferred_element_type=jnp.float32
    )


def local(
    layer_in,
    positions,
    norm_gain,
    w_branch,
    w_gelu,
    conv_w,
    conv_b,
    w_rgate,
    b_rgate,
    w_igate,
    b_igate,
    decay_param,
    w_out,
    mlp_gain,
    w_gate,
    w_up,
    w_down,
    cotangent,
):
    row_count = layer_in.shape[0]
    col_width = layer_in.shape[1]
    column = lax.axis_index("ch") * col_width
    tap_count = conv_w.shape[0]
    keep_mask = (positions > 0).astype(jnp.float32)[:, None]
    tap_masks = [(positions >= offset).astype(jnp.float32)[:, None] for offset in range(tap_count)]
    ones_vec = jnp.ones_like(decay_param)
    zeros_vec = jnp.zeros_like(decay_param)
    full_in = lax.all_gather(layer_in, "ch", axis=1, tiled=True).astype(jnp.float32)
    width_total = full_in.shape[1]
    normed_f, norm_back = jax.vjp(rms_norm, full_in, norm_gain)
    normed = normed_f.astype(jnp.bfloat16)
    rec_in = jnp.dot(normed, w_branch, preferred_element_type=jnp.float32)
    gate_pre = jnp.dot(normed, w_gelu, preferred_element_type=jnp.float32)
    gate_act, gelu_back = jax.vjp(jax.nn.gelu, gate_pre)
    before = shifted(rec_in[row_count - (tap_count - 1) :], "tok", 1)
    extended = jnp.concatenate([before, rec_in], axis=0)
    conv_out = conv_b + jnp.zeros_like(rec_in)
    for offset in range(tap_count):
        start_row = tap_count - 1 - offset
        conv_out = (
            conv_out
            + conv_w[offset] * extended[start_row : start_row + row_count] * tap_masks[offset]
        )
    conv_low = conv_out.astype(jnp.bfloat16)
    pre_rate = block_product(conv_low, w_rgate) + b_rgate
    pre_input = block_product(conv_low, w_igate) + b_igate

    def gate_fn(rate_in, input_in, conv_in, decay_in):
        return gate_terms(rate_in, input_in, conv_in, decay_in, keep_mask)

    (step_decay, gated_in), gate_back = jax.vjp(gate_fn, pre_rate, pre_input, conv_out, decay_param)
    products, partial_state = lax.associative_scan(combine, (step_decay, gated_in), axis=0)
    state_in = carried_in(
        (products[-1], partial_state[-1]), "tok", combine, (ones_vec, zeros_vec), False
    )[1]
    lru_state = partial_state + products * state_in
    previous = jnp.concatenate([state_in[None], lru_state[:-1]], axis=0)
    branch = (lru_state * gate_act).astype(jnp.bfloat16)
    block_out = lax.psum(jnp.dot(branch, w_out, preferred_element_type=jnp.float32), "ch")
    middle = full_in + block_out
    normed_mid_f, mid_pullback = jax.vjp(rms_norm, middle, mlp_gain)
    normed_mid = normed_mid_f.astype(jnp.bfloat16)
    gate_val = jnp.dot(normed_mid, w_gate, preferred_element_type=jnp.float32)
    up_val = jnp.dot(normed_mid, w_up, preferred_element_type=jnp.float32)
    hidden_f, unit_back = jax.vjp(gated_unit, gate_val, up_val)
    hidden = hidden_f.astype(jnp.bfloat16)
    mlp_out = lax.psum_scatter(
        jnp.dot(hidden, w_down, preferred_element_type=jnp.float32),
        "ch",
        scatter_dimension=1,
        tiled=True,
    )
    own_middle = lax.dynamic_slice_in_dim(middle, column, col_width, 1)
    layer_out = (own_middle + mlp_out).astype(jnp.bfloat16)
    grad_rows = lax.all_gather(cotangent, "ch", axis=1, tiled=True)
    grad_wdown = left_product(hidden, grad_rows)
    grad_hidden = right_product(grad_rows, w_down)
    grad_gate_f, grad_up_f = unit_back(grad_hidden)
    grad_gate = grad_gate_f.astype(jnp.bfloat16)
    grad_up = grad_up_f.astype(jnp.bfloat16)
    grad_wgate = left_product(normed_mid, grad_gate)
    grad_wup = left_product(normed_mid, grad_up)
    grad_normed_mid = lax.psum(
        right_product(grad_gate, w_gate) + right_product(grad_up, w_up), "ch"
    )
    grad_middle, grad_mlp_gain = mid_pullback(grad_normed_mid)
    grad_middle = grad_middle + grad_rows.astype(jnp.float32)
    own_mlp_gain = lax.dynamic_slice_in_dim(grad_mlp_gain, column, col_width, 0)
    grad_block = grad_middle.astype(jnp.bfloat16)
    grad_wout = left_product(branch, grad_block)
    grad_branch = right_product(grad_block, w_out)
    grad_state = grad_branch * gate_act
    (grad_gate_pre_f,) = gelu_back(grad_branch * lru_state)
    following = jnp.concatenate([step_decay[1:], jnp.ones_like(step_decay[:1])], axis=0)
    reach_prod, partial_grad = lax.associative_scan(
        combine, (following, grad_state), reverse=True, axis=0
    )
    send_pair = (step_decay[0] * reach_prod[0], step_decay[0] * partial_grad[0])
    incoming = carried_in(send_pair, "tok", combine, (ones_vec, zeros_vec), True)[1]
    carried = partial_grad + reach_prod * incoming
    grad_rate_f, grad_input_f, grad_conv_gate, grad_decay = gate_back((carried * previous, carried))
    grad_rate = grad_rate_f.astype(jnp.bfloat16)
    grad_input = grad_input_f.astype(jnp.bfloat16)
    grad_brate = jnp.sum(grad_rate.astype(jnp.float32), axis=0)
    grad_binput = jnp.sum(grad_input.astype(jnp.float32), axis=0)
    grad_wrate = block_weights(conv_low, grad_rate, w_rgate)
    grad_winput = block_weights(conv_low, grad_input, w_igate)
    grad_conv = grad_conv_gate + block_back(grad_rate, w_rgate) + block_back(grad_input, w_igate)
    grad_convb = jnp.sum(grad_conv, axis=0)
    masked = [grad_conv * tap_masks[offset] for offset in range(tap_count)]
    grad_convw = jnp.stack(
        [
            jnp.sum(
                masked[offset]
                * extended[tap_count - 1 - offset : tap_count - 1 - offset + row_count],
                axis=0,
            )
            for offset in range(tap_count)
        ]
    )
    edge_rows = jnp.stack([masked[offset][: tap_count - 1] for offset in range(1, tap_count)])
    next_rows = shifted(edge_rows, "tok", -1)
    grad_rec_f = conv_w[0] * grad_conv
    for offset in range(1, tap_count):
        joined = jnp.concatenate([masked[offset], next_rows[offset - 1]], axis=0)
        grad_rec_f = grad_rec_f + conv_w[offset] * joined[offset : offset + row_count]
    grad_rec = grad_rec_f.astype(jnp.bfloat16)
    grad_gate_pre = grad_gate_pre_f.astype(jnp.bfloat16)
    grad_wbranch = left_product(normed, grad_rec)
    grad_wgelu = left_product(normed, grad_gate_pre)
    partial_normed = right_product(grad_rec, w_branch) + right_product(grad_gate_pre, w_gelu)
    own_grad_middle = lax.dynamic_slice_in_dim(grad_middle, column, col_width, 1)
    row_term = jnp.sum(partial_normed * norm_gain * full_in, axis=1)
    spread_term = jnp.broadcast_to(row_term[:, None], (row_count, lax.axis_size("ch")))
    own_normed, row_stat = (
        lax.psum_scatter(partial_normed, "ch", scatter_dimension=1, tiled=True),
        lax.psum_scatter(spread_term, "ch", scatter_dimension=1, tiled=True),
    )
    scale_in = lax.rsqrt(jnp.mean(full_in * full_in, axis=1, keepdims=True) + 1e-06)
    own_in = layer_in.astype(jnp.float32)
    own_gain = lax.dynamic_slice_in_dim(norm_gain, column, col_width, 0)
    cubed = scale_in * scale_in * scale_in
    input_grad = (
        own_grad_middle
        + scale_in * own_gain * own_normed
        - cubed * own_in * (row_stat / width_total)
    )
    own_norm_gain = jnp.sum(own_normed * own_in * scale_in, axis=0)
    small_sums = lax.psum(
        (grad_convw, grad_convb, grad_brate, grad_binput, grad_decay, own_norm_gain, own_mlp_gain),
        "tok",
    )
    every_sum = (
        lax.psum_scatter(grad_wbranch, "tok", scatter_dimension=0, tiled=True),
        lax.psum_scatter(grad_wgelu, "tok", scatter_dimension=0, tiled=True),
        lax.psum_scatter(grad_wrate, "tok", scatter_dimension=1, tiled=True),
        lax.psum_scatter(grad_winput, "tok", scatter_dimension=1, tiled=True),
        lax.psum_scatter(grad_wout, "tok", scatter_dimension=1, tiled=True),
        lax.psum_scatter(grad_wgate, "tok", scatter_dimension=0, tiled=True),
        lax.psum_scatter(grad_wup, "tok", scatter_dimension=0, tiled=True),
        lax.psum_scatter(grad_wdown, "tok", scatter_dimension=1, tiled=True),
    )
    return (
        layer_out,
        input_grad,
        small_sums[5],
        every_sum[0],
        every_sum[1],
        small_sums[0],
        small_sums[1],
        every_sum[2],
        small_sums[2],
        every_sum[3],
        small_sums[3],
        small_sums[4],
        every_sum[4],
        small_sums[6],
        every_sum[5],
        every_sum[6],
        every_sum[7],
    )


def solution(mesh):
    placed = (
        P("tok", "ch"),
        P("tok"),
        P(),
        P(None, "ch"),
        P(None, "ch"),
        P(None, "ch"),
        P("ch"),
        P("ch", None, None),
        P("ch"),
        P("ch", None, None),
        P("ch"),
        P("ch"),
        P("ch", None),
        P(),
        P(None, "ch"),
        P(None, "ch"),
        P("ch", None),
        P("tok", "ch"),
    )
    return jax.shard_map(
        local,
        mesh=mesh,
        in_specs=placed,
        out_specs=(
            P("tok", "ch"),
            P("tok", "ch"),
            P("ch"),
            P("tok", "ch"),
            P("tok", "ch"),
            P(None, "ch"),
            P("ch"),
            P("ch", "tok", None),
            P("ch"),
            P("ch", "tok", None),
            P("ch"),
            P("ch"),
            P("ch", "tok"),
            P("ch"),
            P("tok", "ch"),
            P("tok", "ch"),
            P("ch", "tok"),
        ),
        check_vma=False,
    )
```

profile of v0, /device:TPU:0, one launch (start us, length us, event | category | flops | bytes accessed | tf_op | source)
XLA Modules:
  0.0 1949.6 jit_solution(8693740519804002635)
XLA Ops:
  9.4 55.7 %all-gather.7.cloned.1.call-done = bf16[1024,2048]{1,0:T(8,128)(2,1)} async-done(((bf16[1024,512]{1,0:T(8,128)(2,1)}), bf16[1024,2048]{1,0:T(8,128)(2,1)}) %all-gather.7.cloned.1.call-update) | async-done | bytes 4194320 | tf_op jit(solution)/shard_map/all_gather | solution.py:110
  78.9 7.9 fusion.92
  110.6 7.0 slice.760
  117.6 7.0 slice.690
  124.6 7.0 slice.689
  132.3 7.0 slice.692
  139.3 7.0 slice.688
  201.1 7.0 slice.687
  261.4 9.1 pad.285
  278.5 9.1 pad.284
  288.4 16.3 all-gather
  304.7 9.1 pad.265
  316.2 9.3 pad.264
  326.3 13.8 all-gather.1
  340.1 11.8 multiply_convert_fusion.3
  359.3 171.6 %all-reduce.91.cloned.1.call-done = f32[1024,2048]{1,0:T(8,128)} async-done(((f32[1024,2048]{1,0:T(8,128)}), f32[1024,2048]{1,0:T(8,128)}) %all-reduce.91.cloned.1.call-update) | async-done | bytes 8388624 | tf_op jit(solution)/shard_map/psum | solution.py:141
  540.2 12.2 fusion.109
  552.4 10.5 fusion.108
  562.9 23.3 %all-gather.9.cloned.1.call-done = bf16[1024,2048]{1,0:T(8,128)(2,1)} async-done(((bf16[1024,512]{1,0:T(8,128)(2,1)}), bf16[1024,2048]{1,0:T(8,128)(2,1)}) %all-gather.9.cloned.1.call-update) | async-done | bytes 4194320 | tf_op jit(solution)/shard_map/all_gather | solution.py:157
  586.2 18.0 multiply_convert_fusion.1
  604.2 11.1 fusion.111
  615.3 10.9 convolution_add_fusion.1
  629.8 7.2 slice.793
  637.1 7.1 slice.786
  644.1 7.0 slice.784
  651.2 10.7 slice.794
  661.9 11.0 slice.785
  672.9 10.7 slice.787
  683.6 114.9 %all-reduce.93.cloned.1.call-done = f32[1024,2048]{1,0:T(8,128)} async-done(((f32[1024,2048]{1,0:T(8,128)}), f32[1024,2048]{1,0:T(8,128)}) %all-reduce.93.cloned.1.call-update) | async-done | bytes 8388624 | tf_op jit(solution)/shard_map/psum | solution.py:165
  798.5 7.7 multiply_reduce_fusion
  812.7 11.5 fusion.18
  825.7 7.0 slice.862
  832.6 7.0 slice.790
  839.6 7.0 slice.788
  846.6 10.7 slice.789
  857.3 10.7 slice.791
  921.1 11.1 slice.863
  988.8 9.0 pad.304
  997.9 9.2 pad.324
  1007.0 9.3 pad.325
  1016.3 9.2 pad.305
  1032.7 20.8 %rev.8 = f32[1024,640]{1,0:T(8,128)} reverse(f32[1024,640]{1,0:T(8,128)} %add.690), dimensions={0} | reverse | bytes 5242880 | tf_op jit(solution)/shard_map/rev | solution.py:177
  1053.5 20.9 %rev.9 = f32[1024,640]{1,0:T(8,128)} reverse(f32[1024,640]{1,0:T(8,128)} %add.700), dimensions={0} | reverse | bytes 5242880 | tf_op jit(solution)/shard_map/rev | solution.py:177
  1074.3 13.8 all-gather.3
  1088.2 13.8 all-gather.2
  1102.5 10.5 multiply_reduce_fusion.3
  1127.1 12.1 fusion.110
  1153.5 9.4 fusion.87
  1177.8 9.1 fusion.40
  1187.6 8.8 fusion.79
  1196.4 8.7 fusion.81
  1205.4 12.4 fusion.117
  1217.8 12.8 fusion.116
  1230.6 12.5 fusion.115
  1246.5 16.8 all-reduce.82
  1267.1 9.2 reduce-scatter.9.cloned.1.call-done
  1279.8 86.2 %reduce-scatter.11.cloned.1.call-done = f32[1024,512]{1,0:T(8,128)} async-done(((f32[1024,2048]{1,0:T(8,128)}), f32[1024,512]{1,0:T(8,128)}) %reduce-scatter.11.cloned.1.call-update) | async-done | bytes 2097168 | tf_op jit(solution)/shard_map/reduce_scatter | solution.py:218
  1370.0 30.7 %all-reduce.85 = (f32[512]{0:T(512)}, f32[4,640]{1,0:T(4,128)}, f32[640]{0:T(1024)}, f32[640]{0:T(1024)}, f32[640]{0:T(1024)}, /*index=5*/f32[640]{0:T(1024)}, f32[512]{0:T(512)}) all-reduce(f32[512]{0:T(512)S(1)} %get-tuple-element.253, f32[4,640]{1,0:T(4,128)S(1)} %pad_maximum_fusion.36, ...), channel_id=1, replica_groups=mesh['tok'=8,'ch'=4] {'tok'}, use_global_device_ids=true, to_apply=%region_14.15 | all-reduce | flops 6144 | bytes 49152 | tf_op jit(solution)/shard_map/psum | solution.py:231
  1400.6 28.7 %reduce-scatter.17.cloned.1.call-done = f32[640,256]{1,0:T(8,128)} async-done(((f32[640,2048]{1,0:T(8,128)}), f32[640,256]{1,0:T(8,128)}) %reduce-scatter.17.cloned.1.call-update) | async-done | bytes 655376 | tf_op jit(solution)/shard_map/reduce_scatter | solution.py:240
  1429.3 61.1 %reduce-scatter.15.cloned.1.call-done = f32[256,640]{1,0:T(8,128)} async-done(((f32[2048,640]{1,0:T(8,128)}), f32[256,640]{1,0:T(8,128)}) %reduce-scatter.15.cloned.1.call-update) | async-done | bytes 655376 | tf_op jit(solution)/shard_map/reduce_scatter | solution.py:237
  1490.5 61.0 %reduce-scatter.13.cloned.1.call-done = f32[256,640]{1,0:T(8,128)} async-done(((f32[2048,640]{1,0:T(8,128)}), f32[256,640]{1,0:T(8,128)}) %reduce-scatter.13.cloned.1.call-update) | async-done | bytes 655376 | tf_op jit(solution)/shard_map/reduce_scatter | solution.py:236
  1551.5 130.5 %reduce-scatter.23.cloned.1.call-done = f32[1536,256]{1,0:T(8,128)} async-done(((f32[1536,2048]{1,0:T(8,128)}), f32[1536,256]{1,0:T(8,128)}) %reduce-scatter.23.cloned.1.call-update) | async-done | bytes 1572880 | tf_op jit(solution)/shard_map/reduce_scatter | solution.py:243
  1682.0 130.3 %reduce-scatter.21.cloned.1.call-done = f32[256,1536]{1,0:T(8,128)} async-done(((f32[2048,1536]{1,0:T(8,128)}), f32[256,1536]{1,0:T(8,128)}) %reduce-scatter.21.cloned.1.call-update) | async-done | bytes 1572880 | tf_op jit(solution)/shard_map/reduce_scatter | solution.py:242
  1812.3 130.5 %reduce-scatter.19.cloned.1.call-done = f32[256,1536]{1,0:T(8,128)} async-done(((f32[2048,1536]{1,0:T(8,128)}), f32[256,1536]{1,0:T(8,128)}) %reduce-scatter.19.cloned.1.call-update) | async-done | bytes 1572880 | tf_op jit(solution)/shard_map/reduce_scatter | solution.py:241
  (594 shorter events, 363.0 us)
Async XLA Ops:
  7.2 332.9 %copy-start = (bf16[2048,640]{1,0:T(8,128)(2,1)S(1)}, bf16[2048,640]{1,0:T(8,128)(2,1)}, u32[]{:S(2)}) copy-start(bf16[2048,640]{1,0:T(8,128)(2,1)} %param.26) | copy-start | bytes 7864324
  7.2 61.8 %copy-start.46 = (f32[2048]{0:T(1024)S(1)}, f32[2048]{0:T(1024)}, u32[]{:S(2)}) copy-start(f32[2048]{0:T(1024)} %param.24) | copy-start | bytes 24580
  7.2 58.0 %all-gather.7.cloned.1.call-start = ((), (), s32[]{:S(2)}) async-start(), calls=%async_computation.8 | async-start | bytes 5242880 | tf_op jit(solution)/shard_map/all_gather | solution.py:110
  7.9 523.0 %all-reduce.91.cloned.1.call-start = ((), (), s32[]{:S(2)}) async-start(), calls=%async_computation.9 | async-start | bytes 16777216 | tf_op jit(solution)/shard_map/psum | solution.py:141
  8.7 93.9 %copy-start.52 = (f32[640]{0:T(1024)}, f32[640]{0:T(1024)S(1)}, u32[]{:S(2)}) copy-start(f32[640]{0:T(1024)S(1)} %broadcast_multiply_fusion.3) | copy-start | bytes 7684
  9.4 68.9 %copy-start.66 = (f32[1024]{0:T(1024)}, f32[1024]{0:T(1024)S(1)}, u32[]{:S(2)}) copy-start(f32[1024]{0:T(1024)S(1)} %get-tuple-element.351) | copy-start | bytes 12292
  9.4 68.9 %copy-start.68 = (f32[1024]{0:T(1024)}, f32[1024]{0:T(1024)S(1)}, u32[]{:S(2)}) copy-start(f32[1024]{0:T(1024)S(1)} %get-tuple-element.352) | copy-start | bytes 12292
  9.4 68.9 %copy-start.70 = (f32[1024]{0:T(1024)}, f32[1024]{0:T(1024)S(1)}, u32[]{:S(2)}) copy-start(f32[1024]{0:T(1024)S(1)} %get-tuple-element.353) | copy-start | bytes 12292
  9.4 68.9 %copy-start.72 = (f32[1024]{0:T(1024)}, f32[1024]{0:T(1024)S(1)}, u32[]{:S(2)}) copy-start(f32[1024]{0:T(1024)S(1)} %get-tuple-element.355) | copy-start | bytes 12292
  9.4 93.1 %copy-start.50 = (f32[1024]{0:T(1024)}, f32[1024]{0:T(1024)S(1)}, u32[]{:S(2)}) copy-start(f32[1024]{0:T(1024)S(1)} %get-tuple-element.354) | copy-start | bytes 12292
  9.4 93.1 %copy-start.83 = (pred[1024]{0:T(1024)(128)(4,1)}, pred[1024]{0:T(1024)(128)(4,1)S(1)}, u32[]{:S(2)}) copy-start(pred[1024]{0:T(1024)(128)(4,1)S(1)} %get-tuple-element.350) | copy-start | bytes 3076
  69.0 271.1 %copy-start.75 = (f32[1024]{0:T(1024)}, f32[1024]{0:T(1024)S(1)}, u32[]{:S(2)}) copy-start(f32[1024]{0:T(1024)S(1)} %get-tuple-element.349) | copy-start | bytes 12292
  69.0 8.6 copy-start.78
  69.0 9.9 copy-start.85
  75.7 2.5 collective-permute-start
  217.4 7.2 copy-start.79
  219.8 5.6 copy-start.80
  235.4 4.4 copy-start.21
  235.4 4.4 copy-start.23
  235.4 4.4 copy-start.25
  235.4 4.4 copy-start.35
  235.4 4.4 copy-start.37
  340.1 12.9 copy-start.86
  358.5 227.7 %all-gather.9.cloned.1.call-start = ((), (), s32[]{:S(2)}) async-start(), calls=%async_computation.11 | async-start | bytes 5242880 | tf_op jit(solution)/shard_map/all_gather | solution.py:157
  359.3 177.6 %copy-start.45 = (f32[2048]{0:T(1024)S(1)}, f32[2048]{0:T(1024)}, u32[]{:S(2)}) copy-start(f32[2048]{0:T(1024)} %param.35) | copy-start | bytes 24580
  359.3 439.2 %all-reduce.93.cloned.1.call-start = ((), (), s32[]{:S(2)}) async-start(), calls=%async_computation.12 | async-start | bytes 16777216 | tf_op jit(solution)/shard_map/psum | solution.py:165
  540.2 12.2 copy-start.29
  604.2 11.1 copy-start.90
  604.2 11.1 copy-start.91
  626.2 637.8 %all-reduce.95.cloned.1.call-start = ((), (), s32[]{:S(2)}) async-start(), calls=%async_computation.20 | async-start | bytes 2621440
  798.5 8.2 copy-start.6
  798.5 9.4 copy-start.30
  807.9 4.8 copy-start.34
  812.7 11.5 copy-start.4
  939.5 7.2 copy-start.81
  941.9 5.6 copy-start.82
  957.5 4.4 copy-start.22
  957.5 4.4 copy-start.24
  957.5 4.4 copy-start.26
  957.5 4.4 copy-start.36
  957.5 4.4 copy-start.38
  1025.5 4.4 copy-start.16
  1025.5 4.5 copy-start.17
  1053.4 49.0 %copy-start.51 = (f32[1024]{0:T(1024)S(1)}, f32[1024]{0:T(1024)}, u32[]{:S(2)}) copy-start(f32[1024]{0:T(1024)} %copy-done.50) | copy-start | bytes 12292
  1053.4 49.0 %copy-start.53 = (f32[640]{0:T(1024)S(1)}, f32[640]{0:T(1024)}, u32[]{:S(2)}) copy-start(f32[640]{0:T(1024)} %copy-done.52) | copy-start | bytes 7684
  1053.4 49.0 %copy-start.55 = (f32[640]{0:T(1024)S(1)}, f32[640]{0:T(1024)}, u32[]{:S(2)}) copy-start(f32[640]{0:T(1024)} %param.30) | copy-start | bytes 7684
  1053.4 49.0 %copy-start.65 = (f32[640]{0:T(1024)S(1)}, f32[640]{0:T(1024)}, u32[]{:S(2)}) copy-start(f32[640]{0:T(1024)} %param.32) | copy-start | bytes 7684
  1053.4 49.0 %copy-start.84 = (pred[1024]{0:T(1024)(128)(4,1)S(1)}, pred[1024]{0:T(1024)(128)(4,1)}, u32[]{:S(2)}) copy-start(pred[1024]{0:T(1024)(128)(4,1)} %copy-done.83) | copy-start | bytes 3076
  1102.5 10.5 copy-start.77
  1102.5 10.5 copy-start.5
  1127.0 149.3 %reduce-scatter.9.cloned.1.call-start = ((), (), s32[]{:S(2)}) async-start(), calls=%async_computation.10 | async-start | bytes 10485760 | tf_op jit(solution)/shard_map/reduce_scatter | solution.py:149
  1139.2 226.8 %reduce-scatter.11.cloned.1.call-start = ((), (), s32[]{:S(2)}) async-start(), calls=%async_computation.13 | async-start | bytes 10485760 | tf_op jit(solution)/shard_map/reduce_scatter | solution.py:218
  1153.5 12.6 copy-start.57
  1153.5 12.6 copy-start.59
  1153.5 12.6 copy-start.61
  1153.5 12.6 copy-start.63
  1163.0 3.1 collective-permute-start.1
  1177.6 251.7 %reduce-scatter.17.cloned.1.call-start = ((), (), s32[]{:S(2)}) async-start(), calls=%async_computation.16 | async-start | bytes 5898240 | tf_op jit(solution)/shard_map/reduce_scatter | solution.py:240
  1186.9 303.5 %reduce-scatter.15.cloned.1.call-start = ((), (), s32[]{:S(2)}) async-start(), calls=%async_computation.15 | async-start | bytes 5898240 | tf_op jit(solution)/shard_map/reduce_scatter | solution.py:237
  1196.4 355.1 %reduce-scatter.13.cloned.1.call-start = ((), (), s32[]{:S(2)}) async-start(), calls=%async_computation.14 | async-start | bytes 5898240 | tf_op jit(solution)/shard_map/reduce_scatter | solution.py:236
  1205.1 476.9 %reduce-scatter.23.cloned.1.call-start = ((), (), s32[]{:S(2)}) async-start(), calls=%async_computation.19 | async-start | bytes 14155776 | tf_op jit(solution)/shard_map/reduce_scatter | solution.py:243
  1217.7 594.6 %reduce-scatter.21.cloned.1.call-start = ((), (), s32[]{:S(2)}) async-start(), calls=%async_computation.18 | async-start | bytes 14155776 | tf_op jit(solution)/shard_map/reduce_scatter | solution.py:242
  1230.6 712.2 %reduce-scatter.19.cloned.1.call-start = ((), (), s32[]{:S(2)}) async-start(), calls=%async_computation.17 | async-start | bytes 14155776 | tf_op jit(solution)/shard_map/reduce_scatter | solution.py:241
  1267.1 98.9 %copy-start.74 = (f32[1024]{0:T(1024)S(1)}, f32[1024]{0:T(1024)}, u32[]{:S(2)}) copy-start(f32[1024]{0:T(1024)} %get-tuple-element.348) | copy-start | bytes 12292
  (43 other events, 97.5 us)
Sparse Core Ops, SparseCore 0:
  9.9 55.2 all-gather.6
  358.7 172.2 all-reduce.90
  532.9 53.2 all-gather.8
  626.3 172.0 all-reduce.92
  1127.1 60.2 all-reduce.94
  1190.4 85.8 reduce-scatter.8
  1279.6 86.2 reduce-scatter.10
  1368.9 60.4 reduce-scatter.16
  1432.2 58.2 reduce-scatter.14
  1493.2 58.2 reduce-scatter.12
  1554.4 127.5 reduce-scatter.22
  1684.7 127.5 reduce-scatter.20
  1815.2 127.5 reduce-scatter.18
where the time goes:
time: 1970 us; the launch traced here: 1950 us
  waiting for transfers between devices  1010 us (51%)
  local copies, waits for them, and re-layouts  470 us (24%)
  matrix products  200 us (10%)
  other arithmetic  147 us (7%)
  blocking collectives  105 us (5%)
    psum x1, waiting for transfers between devices, local(): lax.psum(jnp.dot(branch, w_out, preferred_element_type=jnp.float32), 'ch')  172 us
    slice x73, local copies, waits for them, and re-layouts, local(): lax.associative_scan(combine, (following, grad_state), reverse=True, axis=0)  150 us
    reduce_scatter x1, waiting for transfers between devices, local(): lax.psum_scatter(grad_wdown, 'tok', scatter_dimension=1, tiled=True)  130 us
    reduce_scatter x1, waiting for transfers between devices, local(): lax.psum_scatter(grad_wgate, 'tok', scatter_dimension=0, tiled=True)  130 us
    reduce_scatter x1, waiting for transfers between devices, local(): lax.psum_scatter(grad_wup, 'tok', scatter_dimension=0, tiled=True)  130 us
    psum x1, waiting for transfers between devices, local(): lax.psum(right_product(grad_gate, w_gate) + right_product(grad_up, w_up),...  115 us
    slice x68, local copies, waits for them, and re-layouts, local(): lax.associative_scan(combine, (step_decay, gated_in), axis=0)  87.3 us
    reduce_scatter x1, waiting for transfers between devices, local(): lax.psum_scatter(partial_normed, 'ch', scatter_dimension=1, tiled=True)  86.2 us
  transfers between devices with their start and end apart: 15, of which 14 were waited for; matrix products, arithmetic and copies ran while one was open for 11% of the time, Pallas kernels for 0%

commit v1 on v0

v1 whole, which is shorter than its diff:
```python
import functools

import jax
import jax.numpy as jnp
from jax import lax
from jax.experimental import pallas as pl
from jax.experimental.pallas import tpu as pltpu
from jax.sharding import PartitionSpec as P

MESH = pl.DeviceIdType.MESH
F32 = jnp.float32
BF16 = jnp.bfloat16
SEGS = 8
GELU_A = 0.7978845608028654
GELU_B = 0.044715


def low_bit(mask):
    return (mask & -mask).bit_length() - 1


def high_bit(mask):
    return mask.bit_length() - 1


def gelu_parts(x):
    inner = jnp.tanh(GELU_A * (x + GELU_B * x * x * x))
    act = 0.5 * x * (1.0 + inner)
    slope = 0.5 * (1.0 + inner) + 0.5 * x * (1.0 - inner * inner) * GELU_A * (
        1.0 + 3.0 * GELU_B * x * x
    )
    return act, slope


def gelu_value(x):
    return 0.5 * x * (1.0 + jnp.tanh(GELU_A * (x + GELU_B * x * x * x)))


def minus_expm1(y, exp_y):
    series = 1.0 + y * (1.0 / 7.0)
    for k in (6, 5, 4, 3, 2):
        series = 1.0 + y * (1.0 / k) * series
    return jnp.where(y > -0.35, -y * series, 1.0 - exp_y)


def nt_dot(a, b):
    return lax.dot_general(a, b, (((1,), (1,)), ((), ())), preferred_element_type=F32)


def tn_dot(a, b):
    return lax.dot_general(a, b, (((0,), (0,)), ((), ())), preferred_element_type=F32)


def lane_tiles(chans):
    return [(j, min(128, chans - 128 * j)) for j in range(-(-chans // 128))]


def put_tiles(ref, span, value):
    for j, lanes in lane_tiles(value.shape[1]):
        ref[j, span, :lanes] = value[:, 128 * j : 128 * j + lanes]


def get_tiles(ref, span, chans):
    return jnp.concatenate(
        [ref[j, span, :lanes] for j, lanes in lane_tiles(chans)], axis=1
    )


def join_tiles(parts, chans):
    return jnp.concatenate(
        [part[:, :lanes] for part, (_, lanes) in zip(parts, lane_tiles(chans), strict=True)],
        axis=1,
    )


def whole_vmem(count):
    return [pl.BlockSpec(memory_space=pltpu.VMEM)] * count


def greet(targets):
    barrier = pltpu.get_barrier_semaphore()
    for target in targets:
        pl.semaphore_signal(barrier, inc=1, device_id=target, device_id_type=MESH)
    pl.semaphore_wait(barrier, len(targets))


def gather_kernel(n, chunks, x, out, send, recv, send_f, recv_f, here):
    tok, me = lax.axis_index("tok"), lax.axis_index("ch")
    bits = n.bit_length() - 1
    rows, width = x.shape
    size, half = rows // chunks, width // 2
    greet([(tok, me ^ (1 << b)) for b in range(bits)])

    def place(owner, part, c):
        span = pl.ds(c * size, size)
        if part is None:
            return out.at[span, pl.ds(pl.multiple_of(owner * width, 128), width)]
        return out.at[span, pl.ds(pl.multiple_of(owner * width + part * half, 128), half)]

    own = pltpu.make_async_copy(
        x, out.at[:, pl.ds(pl.multiple_of(me * width, 128), width)], here
    )
    own.start()
    started = []
    for c in range(chunks):
        for b in range(bits):
            copy = pltpu.make_async_remote_copy(
                x.at[pl.ds(c * size, size)],
                place(me, None, c),
                send.at[b, c],
                recv.at[b, c],
                (tok, me ^ (1 << b)),
                MESH,
            )
            copy.start()
            started.append(copy)
    for c in range(chunks):
        for count in range(1, bits):
            for mask in [m for m in range(1, n) if m.bit_count() == count]:
                if count == 1:
                    b = low_bit(mask)
                    pltpu.make_async_remote_copy(
                        x.at[pl.ds(c * size, size)],
                        place(me ^ mask, None, c),
                        send.at[b, c],
                        recv.at[b, c],
                        (tok, me ^ (1 << b)),
                        MESH,
                    ).wait_recv()
                for part in range(2):
                    nexts = (
                        range(high_bit(mask) + 1, bits) if part == 0 else range(low_bit(mask))
                    )
                    block = place(me ^ mask, part, c)
                    if count > 1:
                        pltpu.make_async_remote_copy(
                            block, block, send_f.at[part, mask, c], recv_f.at[part, mask, c],
                            (tok, me ^ 1), MESH,
                        ).wait_recv()
                    for b in nexts:
                        got = mask | (1 << b)
                        copy = pltpu.make_async_remote_copy(
                            block,
                            block,
                            send_f.at[part, got, c],
                            recv_f.at[part, got, c],
                            (tok, me ^ (1 << b)),
                            MESH,
                        )
                        copy.start()
                        started.append(copy)
    for c in range(chunks):
        mask = n - 1
        for part in range(2):
            block = place(me ^ mask, part, c)
            pltpu.make_async_remote_copy(
                block, block, send_f.at[part, mask, c], recv_f.at[part, mask, c],
                (tok, me ^ 1), MESH,
            ).wait_recv()
    for copy in started:
        copy.wait_send()
    own.wait()


def gather_columns(x, ident, chunks=4):
    n = lax.axis_size("ch")
    bits = n.bit_length() - 1
    rows, width = x.shape
    return pl.pallas_call(
        functools.partial(gather_kernel, n, chunks),
        out_shape=jax.ShapeDtypeStruct((rows, n * width), x.dtype),
        in_specs=[pl.BlockSpec(memory_space=pl.ANY)],
        out_specs=pl.BlockSpec(memory_space=pl.ANY),
        scratch_shapes=[
            pltpu.SemaphoreType.DMA((bits, chunks)),
            pltpu.SemaphoreType.DMA((bits, chunks)),
            pltpu.SemaphoreType.DMA((2, n, chunks)),
            pltpu.SemaphoreType.DMA((2, n, chunks)),
            pltpu.SemaphoreType.DMA,
        ],
        compiler_params=pltpu.CompilerParams(collective_id=ident, has_side_effects=True),
    )(x)


def tok_targets():
    count = lax.axis_size("tok")
    tok, ch = lax.axis_index("tok"), lax.axis_index("ch")
    return [(lax.rem(tok + o, count), ch) for o in range(1, count)]


def share_rows(buffer, send, recv):
    tok = lax.axis_index("tok")
    copies = []
    for o, target in enumerate(tok_targets()):
        copy = pltpu.make_async_remote_copy(
            buffer.at[tok], buffer.at[tok], send.at[o], recv.at[o], target, MESH
        )
        copy.start()
        copies.append(copy)
    count = lax.axis_size("tok")
    for o in range(count - 1):
        source = lax.rem(tok + count - 1 - o, count)
        pltpu.make_async_remote_copy(
            buffer.at[source], buffer.at[source], send.at[o], recv.at[o], tok_targets()[o], MESH
        ).wait_recv()
    return copies


def recur_fwd_kernel(
    rec, gpre, pos, cw, cb, wr, br, wi, bi, sp,
    ext, conv, rate, igate, lru, branch,
    low, a_s, h_s, halo, seg, ends, halo_send, halo_recv, send, recv,
):
    rows, chans = rec.shape
    taps = cw.shape[0]
    tok, ch = lax.axis_index("tok"), lax.axis_index("ch")
    count = lax.axis_size("tok")
    greet(tok_targets())
    halo_copy = pltpu.make_async_remote_copy(
        rec.at[pl.ds(rows - 8, 8)], halo, halo_send, halo_recv,
        (lax.rem(tok + 1, count), ch), MESH,
    )
    halo_copy.start()

    step = 16

    def spread(i, _):
        ext[pl.ds(8 + i * step, step), :] = rec[pl.ds(i * step, step), :]
        return 0

    lax.fori_loop(0, rows // step, spread, 0, unroll=4)
    halo_copy.wait()
    ext[0:8, :] = jnp.where(tok > 0, halo[...], 0.0)

    def conv_rows(i, _):
        window = ext[pl.ds(i * step, step + 8), :]
        at = pos[pl.ds(i * step, step), :]
        total = cb[...] + cw[0:1, :] * window[8 : 8 + step]
        for k in range(1, taps):
            total = total + jnp.where(at >= k, cw[k : k + 1, :] * window[8 - k : 8 - k + step], 0.0)
        conv[pl.ds(i * step, step), :] = total
        low[pl.ds(i * step, step), :] = total.astype(BF16)
        return 0

    lax.fori_loop(0, rows // step, conv_rows, 0, unroll=2)

    big = min(256, rows)

    def products(i, _):
        span = pl.ds(i * big, big)
        rate[span, :] = jnp.dot(low[span, :], wr[...], preferred_element_type=F32) + br[...]
        igate[span, :] = jnp.dot(low[span, :], wi[...], preferred_element_type=F32) + bi[...]
        return 0

    lax.fori_loop(0, rows // big, products, 0)

    def gates(i, _):
        span = pl.ds(i * step, step)
        at = pos[span, :]
        r = jax.nn.sigmoid(rate[span, :])
        g = jax.nn.sigmoid(igate[span, :])
        rate[span, :] = r
        igate[span, :] = g
        log_decay = -8.0 * r * sp[...]
        decay = jnp.exp(log_decay)
        mult = jnp.sqrt(minus_expm1(2.0 * log_decay, decay * decay))
        mult = jnp.where(at > 0, mult, 1.0)
        put_tiles(a_s, span, jnp.where(at > 0, decay, 0.0))
        put_tiles(h_s, span, g * conv[span, :] * mult)
        return 0

    lax.fori_loop(0, rows // step, gates, 0, unroll=2)

    length = rows // SEGS

    def scan(t, carry):
        span = pl.ds(t, SEGS, stride=length)
        after = []
        for j, (h, p) in enumerate(carry):
            a = a_s[j, span, :]
            h = a * h + h_s[j, span, :]
            p = a * p
            h_s[j, span, :] = h
            a_s[j, span, :] = p
            after.append((h, p))
        return tuple(after)

    nothing = tuple(
        (jnp.zeros((SEGS, 128), F32), jnp.ones((SEGS, 128), F32)) for _ in lane_tiles(chans)
    )
    found = lax.fori_loop(0, length, scan, nothing, unroll=8)
    h_end = join_tiles([h for h, _ in found], chans)
    p_end = join_tiles([p for _, p in found], chans)
    total_h, total_p = jnp.zeros((1, chans), F32), jnp.ones((1, chans), F32)
    for s in range(SEGS):
        total_h = p_end[s : s + 1] * total_h + h_end[s : s + 1]
        total_p = p_end[s : s + 1] * total_p
    ends[tok, 0:1, :] = total_h
    ends[tok, 1:2, :] = total_p
    sends = share_rows(ends, send, recv)
    state = jnp.zeros((1, chans), F32)
    for source in range(count - 1):
        after = ends[source, 1:2, :] * state + ends[source, 0:1, :]
        state = jnp.where(source < tok, after, state)
    lru[0:8, :] = jnp.broadcast_to(state, (8, chans))
    for s in range(SEGS):
        seg[s : s + 1, :] = state
        state = p_end[s : s + 1] * state + h_end[s : s + 1]

    per = length // step

    def finish(i, _):
        span = pl.ds(i * step, step)
        entering = seg[pl.ds(i // per, 1), :]
        value = get_tiles(h_s, span, chans) + get_tiles(a_s, span, chans) * entering
        lru[pl.ds(8 + i * step, step), :] = value
        branch[span, :] = (value * gelu_value(gpre[span, :])).astype(BF16)
        return 0

    lax.fori_loop(0, rows // step, finish, 0, unroll=2)
    for copy in sends:
        copy.wait_send()


def recur_fwd(rec, gpre, pos, cw, cb, wr, br, wi, bi, sp, ident):
    rows, chans = rec.shape
    count = lax.axis_size("tok")
    grid = jax.ShapeDtypeStruct((rows, chans), F32)
    tall = jax.ShapeDtypeStruct((rows + 8, chans), F32)
    return pl.pallas_call(
        recur_fwd_kernel,
        out_shape=[tall, grid, grid, grid, tall, jax.ShapeDtypeStruct((rows, chans), BF16)],
        in_specs=whole_vmem(10),
        out_specs=whole_vmem(6),
        scratch_shapes=[
            pltpu.VMEM((rows, chans), BF16),
            pltpu.VMEM((len(lane_tiles(chans)), rows, 128), F32),
            pltpu.VMEM((len(lane_tiles(chans)), rows, 128), F32),
            pltpu.VMEM((8, chans), F32),
            pltpu.VMEM((SEGS, chans), F32),
            pltpu.VMEM((count, 8, chans), F32),
            pltpu.SemaphoreType.DMA,
            pltpu.SemaphoreType.DMA,
            pltpu.SemaphoreType.DMA((count - 1,)),
            pltpu.SemaphoreType.DMA((count - 1,)),
        ],
        compiler_params=pltpu.CompilerParams(
            collective_id=ident, has_side_effects=True, vmem_limit_bytes=56 << 20
        ),
    )(rec, gpre, pos, cw, cb, wr, br, wi, bi, sp)


def recur_bwd_kernel(
    gb, gpre, ext, conv, rate, igate, lru, pos, cw, wr, wi, sp, sg,
    grec, ggp, grate, ginput, sums, row_term,
    g_s, a_s, gc, seg, ends, edge, landed, acc, edge_send, edge_recv, send, recv,
):
    rows, chans = gb.shape
    taps = cw.shape[0]
    tok, ch = lax.axis_index("tok"), lax.axis_index("ch")
    count = lax.axis_size("tok")
    greet(tok_targets())
    step = 16
    length = rows // SEGS
    per = length // step

    def begin(i, _):
        span = pl.ds(i * step, step)
        act, slope = gelu_parts(gpre[span, :])
        grad = gb[span, :]
        put_tiles(g_s, span, grad * act)
        ggp[span, :] = (grad * lru[pl.ds(8 + i * step, step), :] * slope).astype(BF16)
        at = pos[span, :]
        put_tiles(a_s, span, jnp.where(at > 0, jnp.exp(-8.0 * rate[span, :] * sp[...]), 0.0))
        return 0

    lax.fori_loop(0, rows // step, begin, 0, unroll=2)

    def scan(t, carry):
        span = pl.ds(length - 1 - t, SEGS, stride=length)
        after = []
        for j, (v, q) in enumerate(carry):
            a = a_s[j, span, :]
            c = g_s[j, span, :] + v
            g_s[j, span, :] = c
            a_s[j, span, :] = q
            after.append((a * c, a * q))
        return tuple(after)

    nothing = tuple(
        (jnp.zeros((SEGS, 128), F32), jnp.ones((SEGS, 128), F32)) for _ in lane_tiles(chans)
    )
    found = lax.fori_loop(0, length, scan, nothing, unroll=8)
    v_end = join_tiles([v for v, _ in found], chans)
    q_end = join_tiles([q for _, q in found], chans)
    total_v, total_q = jnp.zeros((1, chans), F32), jnp.ones((1, chans), F32)
    for s in reversed(range(SEGS)):
        total_v = q_end[s : s + 1] * total_v + v_end[s : s + 1]
        total_q = q_end[s : s + 1] * total_q
    ends[tok, 0:1, :] = total_v
    ends[tok, 1:2, :] = total_q
    sends = share_rows(ends, send, recv)
    state = jnp.zeros((1, chans), F32)
    for source in reversed(range(1, count)):
        after = ends[source, 1:2, :] * state + ends[source, 0:1, :]
        state = jnp.where(source > tok, after, state)
    for s in reversed(range(SEGS)):
        seg[s : s + 1, :] = state
        state = q_end[s : s + 1] * state + v_end[s : s + 1]

    acc[...] = jnp.zeros_like(acc)

    def folded(x):
        return jnp.sum(x.reshape(-1, 8, chans), axis=0)

    def middle(i, _):
        span = pl.ds(i * step, step)
        carried = get_tiles(g_s, span, chans)
        carried = carried + get_tiles(a_s, span, chans) * seg[pl.ds(i // per, 1), :]
        before = lru[pl.ds(i * step, step + 8), :][7 : 7 + step]
        keep = pos[span, :] > 0
        r, g, out = rate[span, :], igate[span, :], conv[span, :]
        log_decay = -8.0 * r * sp[...]
        decay = jnp.exp(log_decay)
        square = decay * decay
        mult = jnp.where(keep, jnp.sqrt(minus_expm1(2.0 * log_decay, square)), 1.0)
        scaled = carried * g
        grad_log = jnp.where(
            keep, decay * carried * before - scaled * out * square / mult, 0.0
        )
        slope = 8.0 * r * grad_log
        grad_rate = (-slope * sp[...] * (1.0 - r)).astype(BF16)
        grad_input = (scaled * out * mult * (1.0 - g)).astype(BF16)
        grate[span, :] = grad_rate
        ginput[span, :] = grad_input
        gc[span, :] = scaled * mult
        acc[0] += folded(slope * sg[...])
        acc[1] += folded(grad_rate.astype(F32))
        acc[2] += folded(grad_input.astype(F32))
        return 0

    lax.fori_loop(0, rows // step, middle, 0)
    big = min(256, rows)

    def products(i, _):
        span = pl.ds(i * big, big)
        gc[span, :] += nt_dot(grate[span, :], wr[...]) + nt_dot(ginput[span, :], wi[...])
        return 0

    lax.fori_loop(0, rows // big, products, 0)
    gc[pl.ds(rows, 8), :] = jnp.zeros((8, chans), F32)

    first = gc[0:8, :]
    first_at = pos[0:8, :]
    total = jnp.zeros((8, chans), F32)
    for k in range(1, taps):
        masked = jnp.where(first_at >= k, cw[k : k + 1, :] * first, 0.0)
        total = total + jnp.concatenate([jnp.zeros((8, chans), F32), masked], axis=0)[k : k + 8]
    edge[...] = total
    edge_copy = pltpu.make_async_remote_copy(
        edge, landed, edge_send, edge_recv, (lax.rem(tok + count - 1, count), ch), MESH
    )
    edge_copy.start()

    def last(i, _):
        span = pl.ds(i * step, step)
        window = gc[pl.ds(i * step, step + 8), :]
        at = pos[pl.ds(i * step, step + 8), :]
        source = ext[pl.ds(i * step, step + 8), :]
        here = window[:step]
        total = cw[0:1, :] * here
        acc[3] += folded(here)
        acc[4] += folded(here * source[8 : 8 + step])
        for k in range(1, taps):
            masked = jnp.where(at >= k, window, 0.0)
            total = total + cw[k : k + 1, :] * masked[k : k + step]
            acc[4 + k] += folded(masked[:step] * source[8 - k : 8 - k + step])
        grec[span, :] = total.astype(BF16)
        return 0

    lax.fori_loop(0, rows // step, last, 0)
    edge_copy.wait()
    tail = jnp.concatenate([jnp.zeros((8, chans), F32), landed[...]], axis=0)
    span = pl.ds(rows - 16, 16)
    window = gc[pl.ds(rows - 16, 24), :]
    at = pos[pl.ds(rows - 16, 24), :]
    total = cw[0:1, :] * window[:16] + jnp.where(tok < count - 1, tail, 0.0)
    for k in range(1, taps):
        masked = jnp.where(at >= k, window, 0.0)
        total = total + cw[k : k + 1, :] * masked[k : k + 16]
    grec[span, :] = total.astype(BF16)

    def stat(i, _):
        span = pl.ds(i * step, step)
        both = grec[span, :].astype(F32) * ext[pl.ds(8 + i * step, step), :]
        both = both + ggp[span, :].astype(F32) * gpre[span, :]
        row_term[span, :] = jnp.sum(both, axis=1, keepdims=True)
        return 0

    lax.fori_loop(0, rows // step, stat, 0, unroll=2)
    for k in range(8):
        sums[k : k + 1, :] = jnp.sum(acc[k], axis=0, keepdims=True)
    for copy in sends:
        copy.wait_send()


def recur_bwd(gb, gpre, ext, conv, rate, igate, lru, pos, cw, wr, wi, sp, sg, ident):
    rows, chans = gb.shape
    count = lax.axis_size("tok")
    half = jax.ShapeDtypeStruct((rows, chans), BF16)
    return pl.pallas_call(
        recur_bwd_kernel,
        out_shape=[
            half, half, half, half,
            jax.ShapeDtypeStruct((8, chans), F32),
            jax.ShapeDtypeStruct((rows, 1), F32),
        ],
        in_specs=whole_vmem(13),
        out_specs=whole_vmem(6),
        scratch_shapes=[
            pltpu.VMEM((len(lane_tiles(chans)), rows, 128), F32),
            pltpu.VMEM((len(lane_tiles(chans)), rows, 128), F32),
            pltpu.VMEM((rows + 8, chans), F32),
            pltpu.VMEM((SEGS, chans), F32),
            pltpu.VMEM((count, 8, chans), F32),
            pltpu.VMEM((8, chans), F32),
            pltpu.VMEM((8, chans), F32),
            pltpu.VMEM((8, 8, chans), F32),
            pltpu.SemaphoreType.DMA,
            pltpu.SemaphoreType.DMA,
            pltpu.SemaphoreType.DMA((count - 1,)),
            pltpu.SemaphoreType.DMA((count - 1,)),
        ],
        compiler_params=pltpu.CompilerParams(
            collective_id=ident, has_side_effects=True, vmem_limit_bytes=60 << 20
        ),
    )(gb, gpre, ext, conv, rate, igate, lru, pos, cw, wr, wi, sp, sg)


class Exchange:
    def __init__(self, n, rows, width, chunks, gather):
        self.n, self.rows, self.width, self.chunks, self.gather = n, rows, width, chunks, gather
        self.bits = n.bit_length() - 1
        self.half = width // 2
        self.size = rows // chunks
        self.keeps = [(part, m) for part in range(2) for m in range(n) if self.incoming(part, m)]

    def scratch(self):
        n, rows, half, chunks = self.n, self.rows, self.half, self.chunks
        shapes = [
            pltpu.VMEM((2, n, rows, half), BF16),
            pltpu.VMEM((2, n, rows, half), BF16),
            pltpu.VMEM((len(self.keeps), rows, half), F32),
            pltpu.SemaphoreType.DMA((2, n, chunks)),
            pltpu.SemaphoreType.DMA((2, n, chunks)),
        ]
        if self.gather:
            shapes += [
                pltpu.VMEM((n, 2, rows, half), BF16),
                pltpu.SemaphoreType.DMA((self.bits, 2, chunks)),
                pltpu.SemaphoreType.DMA((self.bits, 2, chunks)),
                pltpu.SemaphoreType.DMA((2, n, chunks)),
                pltpu.SemaphoreType.DMA((2, n, chunks)),
            ]
        return shapes

    def bind(self, refs):
        if self.gather:
            (self.out, self.into, self.acc, self.ss, self.rs,
             self.full, self.gs, self.gr, self.fs, self.fr) = refs
        else:
            self.out, self.into, self.acc, self.ss, self.rs = refs
        self.tok, self.me = lax.axis_index("tok"), lax.axis_index("ch")

    def neighbours(self):
        return [self.peer(b) for b in range(self.bits)]

    def peer(self, b):
        return (self.tok, self.me ^ (1 << b))

    def bit_of(self, part, mask):
        return low_bit(mask) if part == 0 else high_bit(mask)

    def incoming(self, part, mask):
        if mask == 0:
            return list(range(self.bits)) if part == 0 else list(reversed(range(self.bits)))
        if part == 0:
            return list(range(low_bit(mask)))
        return list(reversed(range(high_bit(mask) + 1, self.bits)))

    def stage_of(self, part, mask):
        return low_bit(mask) if part == 0 else self.bits - 1 - high_bit(mask)

    def span(self, c):
        return pl.ds(pl.multiple_of(c * self.size, self.size), self.size)

    def reduce_copy(self, part, mask, c):
        return pltpu.make_async_remote_copy(
            self.out.at[part, mask, self.span(c)],
            self.into.at[part, mask, self.span(c)],
            self.ss.at[part, mask, c],
            self.rs.at[part, mask, c],
            self.peer(self.bit_of(part, mask)),
            MESH,
        )

    def produce(self, c, block):
        span = self.span(c)
        for mask in sorted(range(self.n), key=lambda m: -m.bit_count()):
            value = block(mask)
            for part in range(2):
                piece = value[:, part * self.half : (part + 1) * self.half]
                if (part, mask) in self.keeps:
                    self.acc[self.keeps.index((part, mask)), span, :] = piece
                else:
                    self.out[part, mask, span, :] = piece.astype(BF16)
                    self.reduce_copy(part, mask, c).start()

    def summed(self, part, mask, c):
        span = self.span(c)
        value = self.acc[self.keeps.index((part, mask)), span, :]
        for b in self.incoming(part, mask):
            came = mask | (1 << b)
            self.reduce_copy(part, came, c).wait_recv()
            value = value + self.into[part, came, span, :].astype(F32)
        return value

    def pass_on(self, stage, c):
        for part in range(2):
            for mask in range(1, self.n):
                if self.stage_of(part, mask) == stage:
                    value = self.summed(part, mask, c)
                    self.out[part, mask, self.span(c), :] = value.astype(BF16)
                    self.reduce_copy(part, mask, c).start()

    def close_reduce(self, c):
        for part in range(2):
            for mask in range(1, self.n):
                self.reduce_copy(part, mask, c).wait_send()

    def gather_copy(self, part, mask, b, c):
        block = self.full.at[self.me ^ mask, part, self.span(c)]
        if mask == 0:
            return pltpu.make_async_remote_copy(
                block, block, self.gs.at[b, part, c], self.gr.at[b, part, c], self.peer(b), MESH
            )
        got = mask | (1 << b)
        return pltpu.make_async_remote_copy(
            block, block, self.fs.at[part, got, c], self.fr.at[part, got, c], self.peer(b), MESH
        )

    def arrived(self, part, mask, c):
        block = self.full.at[self.me ^ mask, part, self.span(c)]
        if mask.bit_count() == 1:
            b = low_bit(mask)
            sems = (self.gs.at[b, part, c], self.gr.at[b, part, c])
        else:
            sems = (self.fs.at[part, mask, c], self.fr.at[part, mask, c])
        pltpu.make_async_remote_copy(block, block, *sems, self.peer(0), MESH).wait_recv()

    def gather_start(self, c, halves):
        for part in range(2):
            self.full[self.me, part, self.span(c), :] = halves[part].astype(BF16)
            for b in range(self.bits):
                self.gather_copy(part, 0, b, c).start()

    def nexts(self, part, mask):
        return range(high_bit(mask) + 1, self.bits) if part == 0 else range(low_bit(mask))

    def gather_pass(self, stage, c):
        for mask in [m for m in range(1, self.n) if m.bit_count() == stage]:
            for part in range(2):
                self.arrived(part, mask, c)
                for b in self.nexts(part, mask):
                    self.gather_copy(part, mask, b, c).start()

    def gather_close(self, c):
        for part in range(2):
            self.arrived(part, self.n - 1, c)
        for part in range(2):
            for b in range(self.bits):
                self.gather_copy(part, 0, b, c).wait_send()
            for mask in range(1, self.n):
                for b in self.nexts(part, mask):
                    self.gather_copy(part, mask, b, c).wait_send()

    def piece(self, owner, c):
        span = self.span(c)
        return jnp.concatenate([self.full[owner, 0, span, :], self.full[owner, 1, span, :]], axis=1)

    def own_sum(self, c):
        return [self.summed(part, 0, c) for part in range(2)]

    def run(self, stages):
        depth = len(stages)

        def turn(t, _):
            for s in reversed(range(depth)):
                c = t - s

                @pl.when(jnp.logical_and(c >= 0, c < self.chunks))
                def _():
                    stages[s](c)

            return 0

        lax.fori_loop(0, self.chunks + depth - 1, turn, 0)


def mid_kernel(ex, branch, w_out, x_own, gain, normed, full_o, own_o, scale_o, *refs):
    ex.bind(refs)
    n, width = ex.n, ex.width
    greet(ex.neighbours())

    def first(c):
        rows = branch[ex.span(c), :]

        def block(mask):
            at = pl.multiple_of((ex.me ^ mask) * width, 128)
            return jnp.dot(rows, w_out[:, pl.ds(at, width)], preferred_element_type=F32)

        ex.produce(c, block)

    def own(c):
        span = ex.span(c)
        value = jnp.concatenate(ex.own_sum(c), axis=1) + x_own[span, :].astype(F32)
        own_o[span, :] = value
        ex.gather_start(c, [value[:, : ex.half], value[:, ex.half :]])
        ex.close_reduce(c)

    def final(c):
        ex.gather_close(c)
        span = ex.span(c)
        total = jnp.zeros((ex.size, 1), F32)
        for d in range(n):
            value = ex.piece(d, c).astype(F32)
            total = total + jnp.sum(value * value, axis=1, keepdims=True)
        scale = lax.rsqrt(total * (1.0 / (n * width)) + 1e-06)
        scale_o[span, :] = scale
        for d in range(n):
            columns = slice(d * width, (d + 1) * width)
            value = ex.piece(d, c)
            full_o[span, columns] = value
            normed[span, columns] = (value.astype(F32) * scale * gain[:, columns]).astype(BF16)

    stages = [first]
    stages += [functools.partial(ex.pass_on, s) for s in range(1, ex.bits)]
    stages += [own]
    stages += [functools.partial(ex.gather_pass, s) for s in range(1, ex.bits)]
    stages += [final]
    ex.run(stages)


def mid_exchange(branch, w_out, x_own, gain, ident, chunks=8):
    n = lax.axis_size("ch")
    rows, width = x_own.shape
    ex = Exchange(n, rows, width, chunks, True)
    full = jax.ShapeDtypeStruct((rows, n * width), BF16)
    return pl.pallas_call(
        functools.partial(mid_kernel, ex),
        out_shape=[
            full, full,
            jax.ShapeDtypeStruct((rows, width), F32),
            jax.ShapeDtypeStruct((rows, 1), F32),
        ],
        in_specs=whole_vmem(4),
        out_specs=whole_vmem(4),
        scratch_shapes=ex.scratch(),
        compiler_params=pltpu.CompilerParams(
            collective_id=ident, has_side_effects=True, vmem_limit_bytes=60 << 20
        ),
    )(branch, w_out, x_own, gain)


def back_kernel(
    ex, grad_gate, grad_up, w_gate, w_up, full, mid_own, cot, cot_own, scale, gain_own,
    block_o, own_o, gain_o, *refs,
):
    ex.bind(refs)
    n, width = ex.n, ex.width
    greet(ex.neighbours())
    gain_o[...] = jnp.zeros_like(gain_o)

    def first(c):
        span = ex.span(c)
        left, right = grad_gate[span, :], grad_up[span, :]

        def block(mask):
            at = pl.ds(pl.multiple_of((ex.me ^ mask) * width, 128), width)
            return nt_dot(left, w_gate[at, :]) + nt_dot(right, w_up[at, :])

        ex.produce(c, block)

    def own(c):
        span = ex.span(c)
        s = scale[span, :]
        grad = jnp.concatenate(ex.own_sum(c), axis=1)
        value = cot_own[span, :].astype(F32) + grad * gain_own[...] * s
        own_o[span, :] = value
        ex.gather_start(c, [value[:, : ex.half], value[:, ex.half :]])
        ex.close_reduce(c)
        product = grad * mid_own[span, :] * s
        gain_o[...] += jnp.sum(product.reshape(-1, 8, width), axis=0)

    def final(c):
        ex.gather_close(c)
        span = ex.span(c)
        s = scale[span, :]
        total = jnp.zeros((ex.size, 1), F32)
        for d in range(n):
            columns = slice(d * width, (d + 1) * width)
            delta = ex.piece(d, c).astype(F32) - cot[span, columns].astype(F32)
            total = total + jnp.sum(delta * full[span, columns].astype(F32), axis=1, keepdims=True)
        factor = s * s * total * (1.0 / (n * width))
        own_o[span, :] = own_o[span, :] - factor * mid_own[span, :]
        for d in range(n):
            columns = slice(d * width, (d + 1) * width)
            value = ex.piece(d, c).astype(F32) - factor * full[span, columns].astype(F32)
            block_o[span, columns] = value.astype(BF16)

    stages = [first]
    stages += [functools.partial(ex.pass_on, s) for s in range(1, ex.bits)]
    stages += [own]
    stages += [functools.partial(ex.gather_pass, s) for s in range(1, ex.bits)]
    stages += [final]
    ex.run(stages)


def back_exchange(
    grad_gate, grad_up, w_gate, w_up, full, mid_own, cot, cot_own, scale, gain_own, ident, chunks=8
):
    n = lax.axis_size("ch")
    rows, width = mid_own.shape
    ex = Exchange(n, rows, width, chunks, True)
    return pl.pallas_call(
        functools.partial(back_kernel, ex),
        out_shape=[
            jax.ShapeDtypeStruct((rows, n * width), BF16),
            jax.ShapeDtypeStruct((rows, width), F32),
            jax.ShapeDtypeStruct((8, width), F32),
        ],
        in_specs=whole_vmem(10),
        out_specs=whole_vmem(3),
        scratch_shapes=ex.scratch(),
        compiler_params=pltpu.CompilerParams(
            collective_id=ident, has_side_effects=True, vmem_limit_bytes=63 << 20
        ),
    )(grad_gate, grad_up, w_gate, w_up, full, mid_own, cot, cot_own, scale, gain_own)


def end_kernel(
    ex, g_rec, g_pre, w_branch, w_gelu, stat, small,
    own_o, stat_o, small_o, stats, smalls, st_s, st_r, sm_s, sm_r, *refs,
):
    ex.bind(refs)
    n, width = ex.n, ex.width
    count = lax.axis_size("tok")
    across = [(ex.tok, ex.me ^ m) for m in range(1, n)]
    greet(across + tok_targets())
    stats[ex.me] = stat[...]
    copies = []
    for m in range(1, n):
        copy = pltpu.make_async_remote_copy(
            stats.at[ex.me], stats.at[ex.me], st_s.at[m - 1], st_r.at[m - 1], across[m - 1], MESH
        )
        copy.start()
        copies.append(copy)
    smalls[ex.tok] = small[...]
    for o, target in enumerate(tok_targets()):
        copy = pltpu.make_async_remote_copy(
            smalls.at[ex.tok], smalls.at[ex.tok], sm_s.at[o], sm_r.at[o], target, MESH
        )
        copy.start()
        copies.append(copy)

    def first(c):
        span = ex.span(c)
        left, right = g_rec[span, :], g_pre[span, :]

        def block(mask):
            at = pl.ds(pl.multiple_of((ex.me ^ mask) * width, 128), width)
            return nt_dot(left, w_branch[at, :]) + nt_dot(right, w_gelu[at, :])

        ex.produce(c, block)

    def own(c):
        own_o[ex.span(c), :] = jnp.concatenate(ex.own_sum(c), axis=1)
        ex.close_reduce(c)

    stages = [first]
    stages += [functools.partial(ex.pass_on, s) for s in range(1, ex.bits)]
    stages += [own]
    ex.run(stages)
    for m in range(1, n):
        block = stats.at[ex.me ^ m]
        pltpu.make_async_remote_copy(
            block, block, st_s.at[m - 1], st_r.at[m - 1], across[m - 1], MESH
        ).wait_recv()
    for o in range(count - 1):
        source = lax.rem(ex.tok + count - 1 - o, count)
        block = smalls.at[source]
        pltpu.make_async_remote_copy(
            block, block, sm_s.at[o], sm_r.at[o], tok_targets()[o], MESH
        ).wait_recv()
    stat_o[...] = jnp.sum(stats[...], axis=0)
    small_o[...] = jnp.sum(smalls[...], axis=0)
    for copy in copies:
        copy.wait_send()


def end_exchange(g_rec, g_pre, w_branch, w_gelu, stat, small, width, ident, chunks=8):
    n, count = lax.axis_size("ch"), lax.axis_size("tok")
    rows = g_rec.shape[0]
    ex = Exchange(n, rows, width, chunks, False)
    return pl.pallas_call(
        functools.partial(end_kernel, ex),
        out_shape=[
            jax.ShapeDtypeStruct((rows, width), F32),
            jax.ShapeDtypeStruct(stat.shape, F32),
            jax.ShapeDtypeStruct(small.shape, F32),
        ],
        in_specs=whole_vmem(6),
        out_specs=whole_vmem(3),
        scratch_shapes=[
            pltpu.VMEM((n, *stat.shape), F32),
            pltpu.VMEM((count, *small.shape), F32),
            pltpu.SemaphoreType.DMA((n - 1,)),
            pltpu.SemaphoreType.DMA((n - 1,)),
            pltpu.SemaphoreType.DMA((count - 1,)),
            pltpu.SemaphoreType.DMA((count - 1,)),
        ]
        + ex.scratch(),
        compiler_params=pltpu.CompilerParams(
            collective_id=ident, has_side_effects=True, vmem_limit_bytes=60 << 20
        ),
    )(g_rec, g_pre, w_branch, w_gelu, stat, small)


def dense_blocks(blocks):
    count, size = blocks.shape[0], blocks.shape[1]
    rows = [
        jnp.pad(blocks[i], ((0, 0), (i * size, (count - 1 - i) * size))) for i in range(count)
    ]
    return jnp.concatenate(rows, axis=0)


def diagonal_blocks(full, count, size):
    return jnp.stack(
        [full[i * size : (i + 1) * size, i * size : (i + 1) * size] for i in range(count)]
    )


def tok_scatter(full, dim):
    summed = lax.psum_scatter(full.astype(BF16), "tok", scatter_dimension=dim, tiled=True)
    return summed.astype(F32)


def local(
    layer_in,
    positions,
    norm_gain,
    w_branch,
    w_gelu,
    conv_w,
    conv_b,
    w_rgate,
    b_rgate,
    w_igate,
    b_igate,
    decay_param,
    w_out,
    mlp_gain,
    w_gate,
    w_up,
    w_down,
    cotangent,
):
    rows, width = layer_in.shape
    ch_index = lax.axis_index("ch")
    column = ch_index * width
    chans = decay_param.shape[0]
    gates, gate_width = w_rgate.shape[0], w_rgate.shape[1]
    pos = positions[:, None]
    pos_tall = jnp.pad(positions, (0, 8))[:, None]
    sp = jax.nn.softplus(-decay_param)[None]
    sg = jax.nn.sigmoid(-decay_param)[None]
    dense_r, dense_i = dense_blocks(w_rgate), dense_blocks(w_igate)

    full_in = gather_columns(layer_in, 0)
    total = full_in.shape[1]
    tied_cot, full_in = lax.optimization_barrier((cotangent, full_in))
    cot = lax.all_gather(tied_cot, "ch", axis=1, tiled=True)
    full_f = full_in.astype(F32)
    scale_in = lax.rsqrt(jnp.mean(full_f * full_f, axis=1, keepdims=True) + 1e-06)
    normed = (full_f * scale_in * norm_gain).astype(BF16)
    rec_in = jnp.dot(normed, w_branch, preferred_element_type=F32)
    gate_pre = jnp.dot(normed, w_gelu, preferred_element_type=F32)
    ext, conv, rate, igate, lru, branch = recur_fwd(
        rec_in, gate_pre, pos, conv_w, conv_b[None], dense_r, b_rgate[None], dense_i,
        b_igate[None], sp, 1,
    )
    normed_mid, mid_full, mid_own, scale_mid = mid_exchange(
        branch, w_out, layer_in, mlp_gain[None], 2
    )
    gate_val = jnp.dot(normed_mid, w_gate, preferred_element_type=F32)
    up_val = jnp.dot(normed_mid, w_up, preferred_element_type=F32)
    act, slope = gelu_parts(gate_val)
    hidden = (act * up_val).astype(BF16)
    down = jnp.dot(hidden, w_down, preferred_element_type=F32).astype(BF16)
    mlp_out = lax.psum_scatter(down, "ch", scatter_dimension=1, tiled=True)
    layer_out = (mid_own + mlp_out.astype(F32)).astype(BF16)
    grad_hidden = nt_dot(cot, w_down)
    grad_gate = (grad_hidden * up_val * slope).astype(BF16)
    grad_up = (grad_hidden * act).astype(BF16)
    grad_wdown = tok_scatter(tn_dot(hidden, cot), 1)
    gain_mid_own = lax.dynamic_slice_in_dim(mlp_gain, column, width, 0)[None]
    grad_block, grad_mid_own, gain_sum = back_exchange(
        grad_gate, grad_up, w_gate, w_up, mid_full, mid_own, cot, cotangent, scale_mid,
        gain_mid_own, 3,
    )
    grad_wgate = tok_scatter(tn_dot(normed_mid, grad_gate), 0)
    grad_wup = tok_scatter(tn_dot(normed_mid, grad_up), 0)
    grad_branch = nt_dot(grad_block, w_out)
    grad_wout = tok_scatter(tn_dot(branch, grad_block), 1)
    grad_rec, grad_gate_pre, grad_rate, grad_input, sums, row_term = recur_bwd(
        grad_branch, gate_pre, ext, conv, rate, igate, lru, pos_tall, conv_w, dense_r, dense_i,
        sp, sg, 4,
    )
    conv_low = conv.astype(BF16)
    grad_wr = diagonal_blocks(tn_dot(conv_low, grad_rate), gates, gate_width)
    grad_wi = diagonal_blocks(tn_dot(conv_low, grad_input), gates, gate_width)
    stat = row_term.reshape(8, rows // 8)
    small_width = max(chans, width)
    small = jnp.concatenate(
        [
            jnp.pad(sums, ((0, 0), (0, small_width - chans))),
            jnp.pad(
                jnp.sum(gain_sum, axis=0, keepdims=True), ((0, 7), (0, small_width - width))
            ),
        ],
        axis=0,
    )
    own_normed, stat_sum, small_sum = end_exchange(
        grad_rec, grad_gate_pre, w_branch, w_gelu, stat, small, width, 5
    )
    grad_wbranch = tok_scatter(tn_dot(normed, grad_rec), 0)
    grad_wgelu = tok_scatter(tn_dot(normed, grad_gate_pre), 0)
    grad_wr = tok_scatter(grad_wr, 1)
    grad_wi = tok_scatter(grad_wi, 1)
    own_in = layer_in.astype(F32)
    own_gain = lax.dynamic_slice_in_dim(norm_gain, column, width, 0)
    row_stat = stat_sum.reshape(rows, 1)
    input_grad = (
        grad_mid_own
        + scale_in * own_gain * own_normed
        - scale_in * scale_in * own_in * (row_stat / total)
    )
    own_norm_gain = lax.psum(jnp.sum(own_normed * own_in * scale_in, axis=0), "tok")
    return (
        layer_out,
        input_grad,
        own_norm_gain,
        grad_wbranch,
        grad_wgelu,
        small_sum[4:8, :chans],
        small_sum[3, :chans],
        grad_wr,
        small_sum[1, :chans],
        grad_wi,
        small_sum[2, :chans],
        small_sum[0, :chans],
        grad_wout,
        small_sum[8, :width],
        grad_wgate,
        grad_wup,
        grad_wdown,
    )


def solution(mesh):
    placed = (
        P("tok", "ch"),
        P("tok"),
        P(),
        P(None, "ch"),
        P(None, "ch"),
        P(None, "ch"),
        P("ch"),
        P("ch", None, None),
        P("ch"),
        P("ch", None, None),
        P("ch"),
        P("ch"),
        P("ch", None),
        P(),
        P(None, "ch"),
        P(None, "ch"),
        P("ch", None),
        P("tok", "ch"),
    )
    return jax.shard_map(
        local,
        mesh=mesh,
        in_specs=placed,
        out_specs=(
            P("tok", "ch"),
            P("tok", "ch"),
            P("ch"),
            P("tok", "ch"),
            P("tok", "ch"),
            P(None, "ch"),
            P("ch"),
            P("ch", "tok", None),
            P("ch"),
            P("ch", "tok", None),
            P("ch"),
            P("ch"),
            P("ch", "tok"),
            P("ch"),
            P("tok", "ch"),
            P("tok", "ch"),
            P("ch", "tok"),
        ),
        check_vma=False,
    )
```

time: 1970 us -> 858 us (0.44)
  waiting for transfers between devices: 1010 us -> 283 us
  local copies, waits for them, and re-layouts: 470 us -> 19.2 us
  Pallas kernels: 0 us -> 352 us
  other arithmetic: 147 us -> 33.5 us
  blocking collectives: 105 us -> 14.2 us
  matrix products: 200 us -> 130 us
    reduce_scatter x8 -> x7, waiting for transfers between devices: 638 us -> 283 us  [the longest x6 231 us: tok_scatter(): lax.psum_scatter(full.astype(BF16), 'tok', scatter_dimension=dim, tiled=T...]
    pallas_call x0 -> x6, Pallas kernels: none -> 352 us  [the longest x1 91.1 us: back_exchange(): pl.pallas_call(functools.partial(back_kernel, ex), out_shape=[jax.ShapeDt...]
    psum x2 -> x0, waiting for transfers between devices: 287 us -> none  [the longest x1 172 us: local(): lax.psum(jnp.dot(branch, w_out, preferred_element_type=jnp.float32), 'ch')]
    slice x144 -> x3, local copies, waits for them, and re-layouts: 239 us -> 4.13 us  [the longest x1 1.51 us: local(): small_sum[0, :chans]]
    pad x72 -> x1, local copies, waits for them, and re-layouts: 139 us -> 0.01 us  [local(): pos_tall = jnp.pad(positions, (0, 8))[:, None]]
    all_gather x2 -> x1, waiting for transfers between devices: 79 us -> 0.01 us  [local(): cot = lax.all_gather(tied_cot, 'ch', axis=1, tiled=True)]
    dot_general x24 -> x15, matrix products: 200 us -> 130 us  [the longest x8 59 us: tn_dot(): lax.dot_general(a, b, (((0,), (0,)), ((), ())), preferred_element_type=F32)]
    all_gather x4 -> x0, blocking collectives: 57.7 us -> none  [carried_in(): gathered = jax.tree.map(lambda a: lax.all_gather(a, axis), part)]
  transfers between devices with their start and end apart: 15 -> 9, of which waited for: 14 -> 5; matrix products, arithmetic and copies ran while one was open for 11% -> 17% of each run, Pallas kernels for 0% -> 20%
where the time goes in v1:
time: 858 us; the launch traced here: 849 us
  Pallas kernels  352 us (41%)
  waiting for transfers between devices  283 us (33%)
  matrix products  130 us (15%)
  other arithmetic  33.5 us (4%)
  local copies, waits for them, and re-layouts  19.2 us (2%)
  between operations  15.3 us (2%)
  blocking collectives  14.2 us (2%)
    reduce_scatter x6, waiting for transfers between devices, tok_scatter(): lax.psum_scatter(full.astype(BF16), 'tok', scatter_dimension=dim, tiled=T...  231 us
    pallas_call x1, Pallas kernels, back_exchange(): pl.pallas_call(functools.partial(back_kernel, ex), out_shape=[jax.ShapeDt...  91.1 us
    pallas_call x1, Pallas kernels, mid_exchange(): pl.pallas_call(functools.partial(mid_kernel, ex), out_shape=[full, full,...  83.4 us
    dot_general x8, matrix products, tn_dot(): lax.dot_general(a, b, (((0,), (0,)), ((), ())), preferred_element_type=F32)  59 us
    reduce_scatter x1, waiting for transfers between devices, local(): mlp_out = lax.psum_scatter(down, 'ch', scatter_dimension=1, tiled=True)  52.8 us
    pallas_call x1, Pallas kernels, recur_bwd(): pl.pallas_call(recur_bwd_kernel, out_shape=[half, half, half, half, jax.S...  50.4 us
    pallas_call x1, Pallas kernels, end_exchange(): pl.pallas_call(functools.partial(end_kernel, ex), out_shape=[jax.ShapeDty...  48.3 us
    pallas_call x1, Pallas kernels, gather_columns(): pl.pallas_call(functools.partial(gather_kernel, n, chunks), out_shape=jax...  39.7 us
  transfers between devices with their start and end apart: 9, of which 5 were waited for; matrix products, arithmetic and copies ran while one was open for 17% of the time, Pallas kernels for 20%

profile of v1, /device:TPU:0, one launch (start us, length us, event | category | flops | bytes accessed | tf_op | source)
XLA Modules:
  0.0 848.9 jit_solution(3790807641618804071)
XLA Ops:
  7.2 39.7 %shard_map.305 = bf16[1024,2048]{1,0:T(8,128)(2,1)} custom-call(bf16[1024,512]{1,0:T(8,128)(2,1)} %x_own.1), custom_call_target="tpu_custom_call" | custom-call | tf_op jit(solution)/shard_map/pallas_call | solution.py:169
  47.2 3.2 fusion
  50.4 0.6 fusion.32
  51.0 0.6 broadcast_in_dim.37.sp
  51.6 1.0 copy.41.pos
  52.6 0.6 broadcast_in_dim.34.cb
  53.2 0.6 broadcast_in_dim.35.br
  53.8 0.6 broadcast_in_dim.36.bi
  54.4 0.6 broadcast_in_dim.41.sg
  55.0 1.0 broadcast_in_dim.43.pos
  56.0 1.3 dynamic_slice.6
  57.3 5.3 fusion.26
  62.6 7.3 fusion.35.gpre
  69.9 5.0 fusion.37.rec
  74.9 39.5 %shard_map.306 = (f32[1032,640]{1,0:T(8,128)}, f32[1024,640]{1,0:T(8,128)}, f32[1024,640]{1,0:T(8,128)}, f32[1024,640]{1,0:T(8,128)}, f32[1032,640]{1,0:T(8,128)}, /*index=5*/bf16[1024,640]{1,0:T(8,128)(2,1)}) custom-call(f32[1024,640]{1,0:T(8,128)} %fusion.37.rec, f32[1024,640]{1,0:T(8,128)} %fusion.35.gpre, s32[1024,1]{1,0:T(8,128)} %copy.41.pos, ...), custom_call_target="tpu_custom_call" | custom-call | tf_op jit(solution)/shard_map/pallas_call | solution.py:330
  114.5 83.4 %shard_map.307 = (bf16[1024,2048]{1,0:T(8,128)(2,1)}, bf16[1024,2048]{1,0:T(8,128)(2,1)}, f32[1024,512]{1,0:T(8,128)}, f32[1024,1]{1,0:T(8,128)}) custom-call(bf16[1024,640]{1,0:T(8,128)(2,1)} %get-tuple-element.42.branch, bf16[640,2048]{1,0:T(8,128)(2,1)} %w_out.1, bf16[1024,512]{1,0:T(8,128)(2,1)} %x_own.1, f32[1,2048]{1,0:T(1,128)} %bitcast.69), custom_call_target="tpu_custom_call" | custom-call | tf_op jit(solution)/shard_map/pallas_call | solution.py:759
  197.9 12.1 %fusion.39 = f32[1024,1536]{1,0:T(8,128)} fusion(bf16[1024,2048]{1,0:T(8,128)(2,1)} %get-tuple-element.44, bf16[2048,1536]{1,0:T(8,128)(2,1)} %w_gate.1), kind=kOutput, calls=%fused_computation.90 | convolution fusion | flops 6442450944 | bytes 16777216 | tf_op jit(solution)/shard_map/dot_general | solution.py:1005
  210.0 8.6 %fusion.40 = f32[1024,1536]{1,0:T(8,128)} fusion(bf16[1024,2048]{1,0:T(8,128)(2,1)S(1)} %copy-done.22, bf16[2048,1536]{1,0:T(8,128)(2,1)S(1)} %bitcast.66), kind=kOutput, calls=%fused_computation.91 | convolution fusion | flops 6442450944 | bytes 16777216 | tf_op jit(solution)/shard_map/dot_general | solution.py:1006
  218.6 18.8 %multiply_convert_fusion = (bf16[1024,1536]{1,0:T(8,128)(2,1)}, bf16[1024,1536]{1,0:T(8,128)(2,1)}, bf16[1024,1536]{1,0:T(8,128)(2,1)}) fusion(f32[1024,1536]{1,0:T(8,128)} %fusion.39, f32[1024,1536]{1,0:T(8,128)} %fusion.40, bf16[1024,2048]{1,0:T(8,128)(2,1)} %all-gather.2.cloned.1.call-done.cot, bf16[1536,2048]{1,0:T(8,128)(2,1)} %param.34), kind=kOutput, calls=%fused_computation.17 | convolution fusion | flops 6481772544 | bytes 32505856 | tf_op jit(solution)/shard_map/dot_general | solution.py:47
  237.4 91.1 %shard_map.308 = (bf16[1024,2048]{1,0:T(8,128)(2,1)}, f32[1024,512]{1,0:T(8,128)}, f32[8,512]{1,0:T(8,128)}) custom-call(bf16[1024,1536]{1,0:T(8,128)(2,1)} %get-tuple-element.106.grad_gate, bf16[1024,1536]{1,0:T(8,128)(2,1)} %get-tuple-element.105.grad_up, bf16[2048,1536]{1,0:T(8,128)(2,1)} %w_gate.1, bf16[2048,1536]{1,0:T(8,128)(2,1)} %w_up.1, ...), custom_call_target="tpu_custom_call" | custom-call | tf_op jit(solution)/shard_map/pallas_call | solution.py:835
  328.5 8.1 fusion.41.gb
  336.5 50.4 %shard_map.309 = (bf16[1024,640]{1,0:T(8,128)(2,1)}, bf16[1024,640]{1,0:T(8,128)(2,1)}, bf16[1024,640]{1,0:T(8,128)(2,1)}, bf16[1024,640]{1,0:T(8,128)(2,1)}, f32[8,640]{1,0:T(8,128)}, /*index=5*/f32[1024,1]{1,0:T(8,128)}) custom-call(f32[1024,640]{1,0:T(8,128)} %fusion.41.gb, f32[1024,640]{1,0:T(8,128)} %fusion.35.gpre, f32[1032,640]{1,0:T(8,128)} %get-tuple-element.50.ext, ...), custom_call_target="tpu_custom_call" | custom-call | tf_op jit(solution)/shard_map/pallas_call | solution.py:511
  386.9 2.6 convolution_convert_fusion.7
  389.8 1.0 copy.44
  390.8 1.2 convolution_convert_fusion.8
  392.3 1.0 copy.43
  393.3 0.2 reduce-scatter.14.cloned.1.call-start
  393.5 7.1 convolution_convert_fusion.4
  400.8 7.6 convolution_convert_fusion.5
  408.4 7.5 convolution_convert_fusion.6
  415.9 0.3 reduce-scatter.8.cloned.1.call-start
  416.2 11.1 %convolution_convert_fusion.3 = bf16[1024,2048]{1,0:T(8,128)(2,1)} fusion(bf16[1024,1536]{1,0:T(8,128)(2,1)} %get-tuple-element.107, bf16[1536,2048]{1,0:T(8,128)(2,1)} %param.34), kind=kOutput, calls=%fused_computation.20 | convolution fusion | flops 6444548096 | bytes 13631488 | tf_op jit(solution)/shard_map/dot_general | solution.py:1009
  427.4 1.8 copy-done.4
  429.2 11.0 %convolution_convert_fusion.2 = bf16[2048,1536]{1,0:T(8,128)(2,1)} fusion(bf16[1024,2048]{1,0:T(8,128)(2,1)} %get-tuple-element.44, bf16[1024,1536]{1,0:T(8,128)(2,1)S(1)} %copy-done.4), kind=kOutput, calls=%fused_computation.9 | convolution fusion | flops 6445596672 | bytes 13631488 | tf_op jit(solution)/shard_map/dot_general | solution.py:51
  440.3 1.8 copy-done.3
  442.1 11.0 %convolution_convert_fusion.1 = bf16[2048,1536]{1,0:T(8,128)(2,1)} fusion(bf16[1024,2048]{1,0:T(8,128)(2,1)} %get-tuple-element.44, bf16[1024,1536]{1,0:T(8,128)(2,1)S(1)} %copy-done.3), kind=kOutput, calls=%fused_computation.8 | convolution fusion | flops 6445596672 | bytes 13631488 | tf_op jit(solution)/shard_map/dot_general | solution.py:51
  453.2 0.3 reduce-scatter.20.cloned.1.call-start
  453.5 1.6 copy-done.25
  455.1 10.8 %convolution_convert_fusion = bf16[1536,2048]{1,0:T(8,128)(2,1)} fusion(bf16[1024,1536]{1,0:T(8,128)(2,1)S(1)} %copy-done.25, bf16[1024,2048]{1,0:T(8,128)(2,1)} %all-gather.2.cloned.1.call-done.cot), kind=kOutput, calls=%fused_computation.7 | convolution fusion | flops 6445596672 | bytes 13631488 | tf_op jit(solution)/shard_map/dot_general | solution.py:51
  466.0 0.5 copy-done.24
  466.6 0.6 dynamic-slice
  467.9 0.8 reduce
  468.7 0.6 select_maximum_fusion.small
  469.3 48.3 %shard_map.310 = (f32[1024,512]{1,0:T(8,128)}, f32[8,128]{1,0:T(8,128)}, f32[16,640]{1,0:T(8,128)}) custom-call(bf16[1024,640]{1,0:T(8,128)(2,1)} %get-tuple-element.55.g_rec, bf16[1024,640]{1,0:T(8,128)(2,1)} %get-tuple-element.56.g_pre, bf16[2048,640]{1,0:T(8,128)(2,1)} %w_branch.1, bf16[2048,640]{1,0:T(8,128)(2,1)} %w_gelu.1, f32[8,128]{1,0:T(8,128)} %bitcast.67, ...), custom_call_target="tpu_custom_call" | custom-call | tf_op jit(solution)/shard_map/pallas_call | solution.py:915
  517.6 1.3 slice.82
  518.9 1.3 slice.95
  520.2 0.7 multiply_bitcast_fusion
  520.9 3.8 fusion.13
  524.7 14.2 %psum.7 = f32[512]{0:T(512)} all-reduce(f32[512]{0:T(512)S(1)} %get-tuple-element.108), channel_id=1, replica_groups=mesh['tok'=8,'ch'=4] {'tok'}, use_global_device_ids=true, to_apply=%region_4.5 | all-reduce | flops 512 | bytes 4096 | tf_op jit(solution)/shard_map/psum | solution.py:1058
  538.9 1.5 slice_reduce_fusion
  540.4 1.4 dynamic-slice_convert_fusion
  541.8 1.4 dynamic-slice_convert_fusion.1
  543.2 1.9 convert_element_type.105
  545.1 1.9 convert_element_type.100
  546.9 24.5 %reduce-scatter.10.cloned.1.call-done = bf16[256,640]{1,0:T(8,128)(2,1)} async-done(((bf16[2048,640]{1,0:T(8,128)(2,1)}), bf16[256,640]{1,0:T(8,128)(2,1)}) %reduce-scatter.10.cloned.1.call-update) | async-done | bytes 327696 | tf_op jit(solution)/shard_map/reduce_scatter | solution.py:954
  571.4 1.9 convert_element_type.98
  573.3 52.8 %reduce-scatter.8.cloned.1.call-done = bf16[1024,512]{1,0:T(8,128)(2,1)} async-done(((bf16[1024,2048]{1,0:T(8,128)(2,1)}), bf16[1024,512]{1,0:T(8,128)(2,1)}) %reduce-scatter.8.cloned.1.call-update) | async-done | bytes 1048592 | tf_op jit(solution)/shard_map/reduce_scatter | solution.py:1010
  626.0 2.5 add_convert_fusion
  628.6 69.7 %reduce-scatter.16.cloned.1.call-done = bf16[256,1536]{1,0:T(8,128)(2,1)} async-done(((bf16[2048,1536]{1,0:T(8,128)(2,1)}), bf16[256,1536]{1,0:T(8,128)(2,1)}) %reduce-scatter.16.cloned.1.call-update) | async-done | bytes 786448 | tf_op jit(solution)/shard_map/reduce_scatter | solution.py:954
  698.3 2.5 convert_element_type.107
  700.7 68.2 %reduce-scatter.18.cloned.1.call-done = bf16[256,1536]{1,0:T(8,128)(2,1)} async-done(((bf16[2048,1536]{1,0:T(8,128)(2,1)}), bf16[256,1536]{1,0:T(8,128)(2,1)}) %reduce-scatter.18.cloned.1.call-update) | async-done | bytes 786448 | tf_op jit(solution)/shard_map/reduce_scatter | solution.py:954
  768.9 2.5 convert_element_type.109
  771.4 68.2 %reduce-scatter.20.cloned.1.call-done = bf16[1536,256]{1,0:T(8,128)(2,1)} async-done(((bf16[1536,2048]{1,0:T(8,128)(2,1)}), bf16[1536,256]{1,0:T(8,128)(2,1)}) %reduce-scatter.20.cloned.1.call-update) | async-done | bytes 786448 | tf_op jit(solution)/shard_map/reduce_scatter | solution.py:954
  839.5 2.4 convert_element_type.111
  (82 shorter events, 1.1 us)
Async XLA Ops:
  7.2 39.9 %copy-start.11 = (bf16[4,160,160]{2,1,0:T(8,128)(2,1)S(1)}, bf16[4,160,160]{2,1,0:T(8,128)(2,1)}, u32[]{:S(2)}) copy-start(bf16[4,160,160]{2,1,0:T(8,128)(2,1)} %param.27) | copy-start | bytes 614404
  7.2 211.4 %all-gather.2.cloned.1.call-start = ((), (), s32[]{:S(2)}) async-start(), calls=%async_computation.8 | async-start | bytes 5242880 | tf_op jit(solution)/shard_map/all_gather | solution.py:992
  47.0 4.0 copy-start.17
  47.0 4.6 copy-start.15
  47.0 5.7 copy-start.18
  47.0 6.2 copy-start.19
  47.0 6.8 copy-start.20
  47.0 10.3 %copy-start.12 = (bf16[4,160,160]{2,1,0:T(8,128)(2,1)S(1)}, bf16[4,160,160]{2,1,0:T(8,128)(2,1)}, u32[]{:S(2)}) copy-start(bf16[4,160,160]{2,1,0:T(8,128)(2,1)} %param.25) | copy-start | bytes 614404
  47.1 493.3 %all-reduce.15.cloned.1.call-start = ((), (), s32[]{:S(2)}) async-start(), calls=%async_computation.15 | async-start | bytes 1310720
  47.1 15.5 %copy-start.6 = (bf16[2048,640]{1,0:T(8,128)(2,1)S(1)}, bf16[2048,640]{1,0:T(8,128)(2,1)}, u32[]{:S(2)}) copy-start(bf16[2048,640]{1,0:T(8,128)(2,1)} %w_gelu.1) | copy-start | bytes 7864324
  47.2 15.5 %copy-start.21 = (f32[2048]{0:T(1024)S(1)}, f32[2048]{0:T(1024)}, u32[]{:S(2)}) copy-start(f32[2048]{0:T(1024)} %param.20) | copy-start | bytes 24580
  62.6 7.3 copy-start
  62.6 7.3 copy-start.5
  114.5 95.5 %slice-start = ((s8[6291456]{0:T(1024)(128)(4,1)}), s8[2097152]{0:T(1024)(128)(4,1)S(1)}, s32[]{:S(2)}) async-start(s8[6291456]{0:T(1024)(128)(4,1)} %bitcast.65), calls=%async_computation.16 | async-start | bytes 4194304
  197.9 12.1 %slice-start.1 = ((s8[6291456]{0:T(1024)(128)(4,1)}), s8[4194304]{0:T(1024)(128)(4,1)S(1)}, s32[]{:S(2)}) async-start(s8[6291456]{0:T(1024)(128)(4,1)} %bitcast.65), calls=%async_computation.17 | async-start | bytes 8388608
  197.9 12.1 %copy-start.22 = (bf16[1024,2048]{1,0:T(8,128)(2,1)S(1)}, bf16[1024,2048]{1,0:T(8,128)(2,1)}, u32[]{:S(2)}) copy-start(bf16[1024,2048]{1,0:T(8,128)(2,1)} %get-tuple-element.44) | copy-start | bytes 12582916
  336.5 50.4 %copy-start.7 = (f32[1024,640]{1,0:T(8,128)S(1)}, f32[1024,640]{1,0:T(8,128)}, u32[]{:S(2)}) copy-start(f32[1024,640]{1,0:T(8,128)} %get-tuple-element.51.conv) | copy-start | bytes 7864324
  386.9 3.9 copy-start.23
  393.3 7.4 copy-start.9
  393.3 149.9 %reduce-scatter.14.cloned.1.call-start = ((), (), s32[]{:S(2)}) async-start(), calls=%async_computation.11 | async-start | bytes 2949120 | tf_op jit(solution)/shard_map/reduce_scatter | solution.py:954
  400.7 144.4 %reduce-scatter.12.cloned.1.call-start = ((), (), s32[]{:S(2)}) async-start(), calls=%async_computation.10 | async-start | bytes 2949120 | tf_op jit(solution)/shard_map/reduce_scatter | solution.py:954
  400.7 7.7 copy-start.8
  408.4 163.1 %reduce-scatter.10.cloned.1.call-start = ((), (), s32[]{:S(2)}) async-start(), calls=%async_computation.9 | async-start | bytes 2949120 | tf_op jit(solution)/shard_map/reduce_scatter | solution.py:954
  415.9 210.1 %reduce-scatter.8.cloned.1.call-start = ((), (), s32[]{:S(2)}) async-start(), calls=%async_computation.7 | async-start | bytes 5242880 | tf_op jit(solution)/shard_map/reduce_scatter | solution.py:1010
  427.3 1.9 copy-start.4
  427.4 270.9 %reduce-scatter.16.cloned.1.call-start = ((), (), s32[]{:S(2)}) async-start(), calls=%async_computation.12 | async-start | bytes 7077888 | tf_op jit(solution)/shard_map/reduce_scatter | solution.py:954
  440.2 1.9 copy-start.3
  440.3 328.6 %reduce-scatter.18.cloned.1.call-start = ((), (), s32[]{:S(2)}) async-start(), calls=%async_computation.13 | async-start | bytes 7077888 | tf_op jit(solution)/shard_map/reduce_scatter | solution.py:954
  453.2 1.9 copy-start.25
  453.2 386.3 %reduce-scatter.20.cloned.1.call-start = ((), (), s32[]{:S(2)}) async-start(), calls=%async_computation.14 | async-start | bytes 7077888 | tf_op jit(solution)/shard_map/reduce_scatter | solution.py:954
  465.9 0.7 copy-start.24
  465.9 1.9 copy-start.16
  465.9 1.9 copy-start.10
  465.9 2.8 copy-start.13
  467.8 53.1 %copy-start.1 = (bf16[1024,512]{1,0:T(8,128)(2,1)S(1)}, bf16[1024,512]{1,0:T(8,128)(2,1)}, u32[]{:S(2)}) copy-start(bf16[1024,512]{1,0:T(8,128)(2,1)} %x_own.1) | copy-start | bytes 3145732
  467.8 53.0 %copy-start.14 = (f32[1024]{0:T(1024)S(1)}, f32[1024]{0:T(1024)}, u32[]{:S(2)}) copy-start(f32[1024]{0:T(1024)} %get-tuple-element.126) | copy-start | bytes 12292
  520.9 105.2 %copy-start.2 = (f32[1024,512]{1,0:T(8,128)S(1)}, f32[1024,512]{1,0:T(8,128)}, u32[]{:S(2)}) copy-start(f32[1024,512]{1,0:T(8,128)} %get-tuple-element.43.mid_own) | copy-start | bytes 6291460
Sparse Core Ops, SparseCore 0:
  47.2 52.8 all-gather.1
  393.4 56.7 all-reduce.14
  452.6 40.8 reduce-scatter.13
  495.6 37.2 reduce-scatter.11
  535.0 36.3 reduce-scatter.9
  574.3 51.7 reduce-scatter.7
  628.5 69.7 reduce-scatter.15
  700.7 68.1 reduce-scatter.17
  771.3 68.1 reduce-scatter.19

commit v2 on v1

v2 whole, which is shorter than its diff:
```python
import functools

import jax
import jax.numpy as jnp
from jax import lax
from jax.experimental import pallas as pl
from jax.experimental.pallas import tpu as pltpu
from jax.sharding import PartitionSpec as P

MESH = pl.DeviceIdType.MESH
F32 = jnp.float32
BF16 = jnp.bfloat16
SEGS = 8
GELU_A = 0.7978845608028654
GELU_B = 0.044715


def low_bit(mask):
    return (mask & -mask).bit_length() - 1


def high_bit(mask):
    return mask.bit_length() - 1


def gelu_parts(x):
    inner = jnp.tanh(GELU_A * (x + GELU_B * x * x * x))
    act = 0.5 * x * (1.0 + inner)
    slope = 0.5 * (1.0 + inner) + 0.5 * x * (1.0 - inner * inner) * GELU_A * (
        1.0 + 3.0 * GELU_B * x * x
    )
    return act, slope


def gelu_value(x):
    return 0.5 * x * (1.0 + jnp.tanh(GELU_A * (x + GELU_B * x * x * x)))


def minus_expm1(y, exp_y):
    series = 1.0 + y * (1.0 / 7.0)
    for k in (6, 5, 4, 3, 2):
        series = 1.0 + y * (1.0 / k) * series
    return jnp.where(y > -0.35, -y * series, 1.0 - exp_y)


def nt_dot(a, b):
    return lax.dot_general(a, b, (((1,), (1,)), ((), ())), preferred_element_type=F32)


def tn_dot(a, b):
    return lax.dot_general(a, b, (((0,), (0,)), ((), ())), preferred_element_type=F32)


def whole_vmem(count):
    return [pl.BlockSpec(memory_space=pltpu.VMEM)] * count


def greet(targets):
    barrier = pltpu.get_barrier_semaphore()
    for target in targets:
        pl.semaphore_signal(barrier, inc=1, device_id=target, device_id_type=MESH)
    pl.semaphore_wait(barrier, len(targets))


class Routes:
    def __init__(self, n, rows, width):
        self.n, self.rows, self.width = n, rows, width
        self.bits = n.bit_length() - 1
        self.half = width // 2
        self.keeps = [(part, m) for part in range(2) for m in range(n) if self.incoming(part, m)]

    def peer(self, b):
        return (self.tok, self.me ^ (1 << b))

    def neighbours(self):
        return [self.peer(b) for b in range(self.bits)]

    def bit_of(self, part, mask):
        return low_bit(mask) if part == 0 else high_bit(mask)

    def incoming(self, part, mask):
        if mask == 0:
            return list(range(self.bits)) if part == 0 else list(reversed(range(self.bits)))
        if part == 0:
            return list(range(low_bit(mask)))
        return list(reversed(range(high_bit(mask) + 1, self.bits)))

    def stage_of(self, part, mask):
        return low_bit(mask) if part == 0 else self.bits - 1 - high_bit(mask)


class Spread(Routes):
    def scratch(self):
        shape = (2, self.n, self.rows, self.half)
        keeps = (len(self.keeps), self.rows, self.half)
        return [
            pltpu.VMEM(shape, BF16),
            pltpu.VMEM(keeps, BF16),
            pltpu.SemaphoreType.DMA((2, self.n)),
            pltpu.SemaphoreType.DMA((2, self.n)),
            pltpu.SemaphoreType.DMA((len(self.keeps),)),
        ]

    def bind(self, refs, source):
        self.into, self.own, self.ss, self.rs, self.ls = refs
        self.source = source
        self.tok, self.me = lax.axis_index("tok"), lax.axis_index("ch")

    def view(self, part, mask):
        at = (self.me ^ mask) * self.width + part * self.half
        return self.source.at[:, pl.ds(pl.multiple_of(at, 128), self.half)]

    def copy(self, part, mask):
        held = (part, mask) in self.keeps
        block = self.own.at[self.keeps.index((part, mask))] if held else self.view(part, mask)
        return pltpu.make_async_remote_copy(
            block,
            self.into.at[part, mask],
            self.ss.at[part, mask],
            self.rs.at[part, mask],
            self.peer(self.bit_of(part, mask)),
            MESH,
        )

    def fetch(self, at):
        return pltpu.make_async_copy(self.view(*self.keeps[at]), self.own.at[at], self.ls.at[at])

    def launch(self):
        for part in range(2):
            for mask in range(1, self.n):
                if (part, mask) not in self.keeps:
                    self.copy(part, mask).start()
        for at in range(len(self.keeps)):
            self.fetch(at).start()

    def gather_in(self, part, mask, write):
        at = self.keeps.index((part, mask))
        self.fetch(at).wait()
        came = [mask | (1 << b) for b in self.incoming(part, mask)]
        for m in came:
            self.copy(part, m).wait_recv()

        def add(i, _):
            span = pl.ds(i * 32, 32)
            value = self.own[at, span, :].astype(F32)
            for m in came:
                value = value + self.into[part, m, span, :].astype(F32)
            write(at, span, value)
            return 0

        lax.fori_loop(0, self.rows // 32, add, 0, unroll=2)

    def relay(self, stage):
        def write(at, span, value):
            self.own[at, span, :] = value.astype(BF16)

        for part in range(2):
            for mask in range(1, self.n):
                if self.stage_of(part, mask) == stage:
                    self.gather_in(part, mask, write)
                    self.copy(part, mask).start()

    def settle(self, result):
        for part in range(2):

            def write(at, span, value, part=part):
                result[span, part * self.half : (part + 1) * self.half] = value

            self.gather_in(part, 0, write)
        for part in range(2):
            for mask in range(1, self.n):
                self.copy(part, mask).wait_send()


def tok_targets():
    count = lax.axis_size("tok")
    tok, ch = lax.axis_index("tok"), lax.axis_index("ch")
    return [(lax.rem(tok + o, count), ch) for o in range(1, count)]


def share_rows(buffer, send, recv):
    tok = lax.axis_index("tok")
    copies = []
    for o, target in enumerate(tok_targets()):
        copy = pltpu.make_async_remote_copy(
            buffer.at[tok], buffer.at[tok], send.at[o], recv.at[o], target, MESH
        )
        copy.start()
        copies.append(copy)
    count = lax.axis_size("tok")
    for o in range(count - 1):
        source = lax.rem(tok + count - 1 - o, count)
        pltpu.make_async_remote_copy(
            buffer.at[source], buffer.at[source], send.at[o], recv.at[o], tok_targets()[o], MESH
        ).wait_recv()
    return copies


class Gather(Routes):
    def __init__(self, n, rows, width, chunks):
        super().__init__(n, rows, width)
        self.chunks, self.size = chunks, rows // chunks

    def scratch(self):
        sem = pltpu.SemaphoreType.DMA
        near, far = (self.bits, self.chunks), (2, self.n, self.chunks)
        return [sem(near), sem(near), sem(far), sem(far), sem]

    def bind(self, refs, x, full):
        self.gs, self.gr, self.fs, self.fr, self.here = refs
        self.x, self.full = x, full
        self.tok, self.me = lax.axis_index("tok"), lax.axis_index("ch")

    def place(self, owner, part, c):
        span = pl.ds(c * self.size, self.size)
        if part is None:
            return self.full.at[span, pl.ds(pl.multiple_of(owner * self.width, 128), self.width)]
        at = owner * self.width + part * self.half
        return self.full.at[span, pl.ds(pl.multiple_of(at, 128), self.half)]

    def near_copy(self, b, c, owner):
        return pltpu.make_async_remote_copy(
            self.x.at[pl.ds(c * self.size, self.size)],
            self.place(owner, None, c),
            self.gs.at[b, c],
            self.gr.at[b, c],
            self.peer(b),
            MESH,
        )

    def far_copy(self, part, mask, b, c):
        block, got = self.place(self.me ^ mask, part, c), mask | (1 << b)
        return pltpu.make_async_remote_copy(
            block, block, self.fs.at[part, got, c], self.fr.at[part, got, c], self.peer(b), MESH
        )

    def own_copy(self):
        at = pl.ds(pl.multiple_of(self.me * self.width, 128), self.width)
        return pltpu.make_async_copy(self.x, self.full.at[:, at], self.here)

    def launch(self, order):
        for c in order:
            for b in range(self.bits):
                self.near_copy(b, c, self.me).start()
        self.own_copy().start()

    def nexts(self, part, mask):
        return range(high_bit(mask) + 1, self.bits) if part == 0 else range(low_bit(mask))

    def far_arrived(self, part, mask, c):
        block = self.place(self.me ^ mask, part, c)
        pltpu.make_async_remote_copy(
            block, block, self.fs.at[part, mask, c], self.fr.at[part, mask, c], self.peer(0), MESH
        ).wait_recv()

    def forward(self, c):
        for count in range(1, self.bits):
            for mask in [m for m in range(1, self.n) if m.bit_count() == count]:
                if count == 1:
                    self.near_copy(low_bit(mask), c, self.me ^ mask).wait_recv()
                for part in range(2):
                    if count > 1:
                        self.far_arrived(part, mask, c)
                    for b in self.nexts(part, mask):
                        self.far_copy(part, mask, b, c).start()

    def finish(self, c):
        for part in range(2):
            self.far_arrived(part, self.n - 1, c)

    def close(self):
        for c in range(self.chunks):
            for b in range(self.bits):
                self.near_copy(b, c, self.me).wait_send()
            for mask in range(1, self.n):
                for part in range(2):
                    for b in self.nexts(part, mask):
                        self.far_copy(part, mask, b, c).wait_send()


def over_rows(start, rows, step, body, unroll=1):
    def one(i, _):
        body(pl.multiple_of(start + i * step, 8))
        return 0

    lax.fori_loop(0, rows // step, one, 0, unroll=unroll)


def eight(value):
    return value.reshape(-1, SEGS, value.shape[-1])


def with_segments(value, seg):
    return (eight(value) * seg[None]).reshape(value.shape)


def front_kernel(
    ga, late, x, gain, pos, wb_h, wg_h, cw, cb, wr_h, br, wi_h, bi, sp, cot,
    normed_h, scale, gpre_h, ext_h, conv_h, rate_h, igate_h, lru, branch, cot_full,
    full, normed, wb, wg, wr, wi, gpre, ext, conv, rate, igate, low, a_s, h_s, carry, halo, ends,
    wsem, osem, halo_send, halo_recv, send, recv, *refs,
):
    held = len(ga.scratch())
    ga.bind(refs[:held], x, full)
    late.bind(refs[held:], cot, cot_full)
    rows, chans = gpre.shape
    taps = cw.shape[0]
    pad = 8 * (taps - 1)
    tok, ch = lax.axis_index("tok"), lax.axis_index("ch")
    count = lax.axis_size("tok")
    total_width = full.shape[1]
    greet(tok_targets() + ga.neighbours())
    order = [ga.chunks - 1] + list(range(ga.chunks - 1))
    ga.launch(order)
    loads = [
        pltpu.make_async_copy(a, b, wsem.at[i])
        for i, (a, b) in enumerate(((wb_h, wb), (wg_h, wg), (wr_h, wr), (wi_h, wi)))
    ]
    for load in loads:
        load.start()
    step = 16
    size = ga.size
    stores = []

    def store(source, target):
        copy = pltpu.make_async_copy(source, target, osem.at[len(stores)])
        copy.start()
        stores.append(copy)

    halo_copy = pltpu.make_async_remote_copy(
        ext.at[pl.ds(rows, pad)], halo, halo_send, halo_recv,
        (lax.rem(tok + 1, count), ch), MESH,
    )

    def norm_rows(at):
        span = pl.ds(at, step)
        value = full[span, :].astype(F32)
        s = lax.rsqrt(
            jnp.sum(value * value, axis=1, keepdims=True) * (1.0 / total_width) + 1e-06
        )
        scale[span, :] = s
        normed[span, :] = (value * s * gain[...]).astype(BF16)

    def enter(c):
        over_rows(c * size, size, step, norm_rows)
        span = pl.ds(c * size, size)
        ext[pl.ds(pad + c * size, size), :] = jnp.dot(
            normed[span, :], wb[...], preferred_element_type=F32
        )
        gpre[span, :] = jnp.dot(normed[span, :], wg[...], preferred_element_type=F32)

    def conv_rows(at):
        span = pl.ds(at, step)
        window = ext[pl.ds(at, step + pad), :]
        where = pos[span, :]
        value = cb[...] + cw[0:1, :] * window[pad : pad + step]
        for k in range(1, taps):
            shifted = window[pad - 8 * k : pad - 8 * k + step]
            value = value + jnp.where(where >= k, cw[k : k + 1, :] * shifted, 0.0)
        conv[span, :] = value
        low[span, :] = value.astype(BF16)

    def gate_rows(at):
        span = pl.ds(at, step)
        where = pos[span, :]
        r = jax.nn.sigmoid(rate[span, :])
        g = jax.nn.sigmoid(igate[span, :])
        rate[span, :] = r
        igate[span, :] = g
        log_decay = -8.0 * r * sp[...]
        decay = jnp.exp(log_decay)
        mult = jnp.sqrt(minus_expm1(2.0 * log_decay, decay * decay))
        mult = jnp.where(where > 0, mult, 1.0)
        a_s[span, :] = jnp.where(where > 0, decay, 0.0)
        h_s[span, :] = g * conv[span, :] * mult

    def scan_rows(c):
        def one(t, state):
            h, p = state
            span = pl.ds(pl.multiple_of(c * size + t * SEGS, SEGS), SEGS)
            a = a_s[span, :]
            h = a * h + h_s[span, :]
            p = a * p
            h_s[span, :] = h
            a_s[span, :] = p
            return h, p

        h, p = lax.fori_loop(0, size // SEGS, one, (carry[0], carry[1]), unroll=4)
        carry[0] = h
        carry[1] = p

    def recur(c):
        over_rows(c * size, size, step, conv_rows, 2)
        span = pl.ds(c * size, size)
        rate[span, :] = jnp.dot(low[span, :], wr[...], preferred_element_type=F32) + br[...]
        igate[span, :] = jnp.dot(low[span, :], wi[...], preferred_element_type=F32) + bi[...]
        over_rows(c * size, size, step, gate_rows, 2)
        scan_rows(c)

    carry[0] = jnp.zeros((SEGS, chans), F32)
    carry[1] = jnp.ones((SEGS, chans), F32)
    for i, c in enumerate(order):
        if i == 0:
            ga.forward(c)
        if i + 1 < len(order):
            ga.forward(order[i + 1])
        if i + 2 == len(order):
            late.launch(range(late.chunks))
        ga.finish(c)
        if i == 0:
            ga.own_copy().wait()
            for load in loads:
                load.wait()
        enter(c)
        if i == 0:
            halo_copy.start()
        if i == 1:
            halo_copy.wait()
            last_row = lax.broadcasted_iota(jnp.int32, (SEGS, chans), 0) == SEGS - 1
            for j in range(taps - 1):
                here = ext[pl.ds(rows + 8 * j, 8), :]
                joined = jnp.where(last_row, halo[8 * j : 8 * j + 8, :], here)
                ext[8 * j : 8 * j + 8, :] = pltpu.roll(joined, 1, 0)
        if i + 1 == len(order):
            late.forward(0)
        if i >= 1:
            recur(c)
    late.forward(1)
    store(normed, normed_h)
    store(gpre, gpre_h)
    store(ext, ext_h)
    recur(ga.chunks - 1)
    late.forward(2)
    store(conv, conv_h)
    store(rate, rate_h)
    store(igate, igate_h)
    h_end, p_end = carry[0], carry[1]
    total_h, total_p = jnp.zeros((1, chans), F32), jnp.ones((1, chans), F32)
    for s in range(SEGS):
        total_h = p_end[s : s + 1] * total_h + h_end[s : s + 1]
        total_p = p_end[s : s + 1] * total_p
    ends[tok, 0:1, :] = total_h
    ends[tok, 1:2, :] = total_p
    sends = share_rows(ends, send, recv)
    state = jnp.zeros((1, chans), F32)
    for source in range(count - 1):
        after = ends[source, 1:2, :] * state + ends[source, 0:1, :]
        state = jnp.where(source < tok, after, state)
    for s in range(SEGS):
        lru[s : s + 1, :] = state
        state = p_end[s : s + 1] * state + h_end[s : s + 1]
    seg = lru[0:8, :]
    late.forward(3)

    def finish_rows(at):
        span = pl.ds(at, step)
        value = h_s[span, :] + with_segments(a_s[span, :], seg)
        lru[pl.ds(8 + at, step), :] = value
        branch[span, :] = (value * gelu_value(gpre[span, :])).astype(BF16)

    over_rows(0, rows, step, finish_rows, 2)
    for copy in sends:
        copy.wait_send()
    ga.close()
    for c in range(late.chunks):
        late.finish(c)
    late.close()
    late.own_copy().wait()
    for copy in stores:
        copy.wait()


def front(x, gain, pos, w_branch, w_gelu, cw, cb, wr, br, wi, bi, sp, cot, ident, chunks=4):
    n, count = lax.axis_size("ch"), lax.axis_size("tok")
    rows, width = x.shape
    total, chans = w_branch.shape
    taps = cw.shape[0]
    pad = 8 * (taps - 1)
    ga, late = Gather(n, rows, width, chunks), Gather(n, rows, width, 4)
    sem = pltpu.SemaphoreType.DMA
    grid = (rows, chans)
    anywhere = pl.BlockSpec(memory_space=pl.ANY)
    vmem = pl.BlockSpec(memory_space=pltpu.VMEM)
    return pl.pallas_call(
        functools.partial(front_kernel, ga, late),
        out_shape=[
            jax.ShapeDtypeStruct((rows, total), BF16),
            jax.ShapeDtypeStruct((rows, 1), F32),
            jax.ShapeDtypeStruct(grid, F32),
            jax.ShapeDtypeStruct((rows + pad, chans), F32),
            jax.ShapeDtypeStruct(grid, F32),
            jax.ShapeDtypeStruct(grid, F32),
            jax.ShapeDtypeStruct(grid, F32),
            jax.ShapeDtypeStruct((rows + 8, chans), F32),
            jax.ShapeDtypeStruct(grid, BF16),
            jax.ShapeDtypeStruct((rows, total), BF16),
        ],
        in_specs=[
            anywhere, vmem, vmem, anywhere, anywhere, vmem, vmem, anywhere, vmem, anywhere, vmem,
            vmem, anywhere,
        ],
        out_specs=[
            anywhere, vmem, anywhere, anywhere, anywhere, anywhere, anywhere, vmem, vmem,
            anywhere,
        ],
        scratch_shapes=[
            pltpu.VMEM((rows, total), BF16),
            pltpu.VMEM((rows, total), BF16),
            pltpu.VMEM(w_branch.shape, BF16),
            pltpu.VMEM(w_gelu.shape, BF16),
            pltpu.VMEM(wr.shape, BF16),
            pltpu.VMEM(wi.shape, BF16),
            pltpu.VMEM(grid, F32),
            pltpu.VMEM((rows + pad, chans), F32),
            pltpu.VMEM(grid, F32),
            pltpu.VMEM(grid, F32),
            pltpu.VMEM(grid, F32),
            pltpu.VMEM(grid, BF16),
            pltpu.VMEM(grid, F32),
            pltpu.VMEM(grid, F32),
            pltpu.VMEM((2, SEGS, chans), F32),
            pltpu.VMEM((pad, chans), F32),
            pltpu.VMEM((count, 8, chans), F32),
            sem((4,)), sem((6,)), sem, sem, sem((count - 1,)), sem((count - 1,)),
        ]
        + ga.scratch()
        + late.scratch(),
        compiler_params=pltpu.CompilerParams(
            collective_id=ident, has_side_effects=True, vmem_limit_bytes=60 << 20
        ),
    )(x, gain, pos, w_branch, w_gelu, cw, cb, wr, br, wi, bi, sp, cot)


def recur_bwd_kernel(
    ex, g_block_h, w_out_h, gpre_h, ext_h, conv_h, rate_h, igate_h, lru_h, pos, cw, wr_h, wi_h, sp,
    sg, down,
    grec, ggp, grate, ginput, sums, row_term, down_sum,
    g_block, w_out, gpre, ext, conv, rate, igate, lru, wr, wi,
    g_s, a_s, gc, ends, edge, landed, acc, lsem, edge_send, edge_recv, send, recv, *refs,
):
    ex.bind(refs, down)
    rows, chans = conv.shape
    taps = cw.shape[0]
    pad = 8 * (taps - 1)
    tok, ch = lax.axis_index("tok"), lax.axis_index("ch")
    count = lax.axis_size("tok")
    pairs = (
        (g_block_h, g_block), (w_out_h, w_out), (gpre_h, gpre), (lru_h, lru), (rate_h, rate),
        (igate_h, igate), (conv_h, conv), (wr_h, wr), (wi_h, wi), (ext_h, ext),
    )
    loads = [pltpu.make_async_copy(a, b, lsem.at[i]) for i, (a, b) in enumerate(pairs)]
    for load in loads:
        load.start()
    greet(tok_targets() + ex.neighbours())
    ex.launch()
    step = 16
    big = min(256, rows)
    for load in loads[:5]:
        load.wait()

    def begin_rows(at):
        span = pl.ds(at, step)
        act, slope = gelu_parts(gpre[span, :])
        grad = g_s[span, :]
        g_s[span, :] = grad * act
        ggp[span, :] = (grad * lru[pl.ds(8 + at, step), :] * slope).astype(BF16)
        a_s[span, :] = jnp.where(pos[span, :] > 0, jnp.exp(-8.0 * rate[span, :] * sp[...]), 0.0)

    def begin(i, state):
        at = pl.multiple_of(rows - (i + 1) * big, 8)
        g_s[pl.ds(at, big), :] = nt_dot(g_block[pl.ds(at, big), :], w_out[...])
        over_rows(at, big, step, begin_rows, 2)

        def one(t, state):
            v, q = state
            span = pl.ds(pl.multiple_of(at + big - (t + 1) * SEGS, SEGS), SEGS)
            a = a_s[span, :]
            c = g_s[span, :] + v
            g_s[span, :] = c
            a_s[span, :] = q
            return a * c, a * q

        return lax.fori_loop(0, big // SEGS, one, state, unroll=4)

    v_end, q_end = lax.fori_loop(
        0, rows // big, begin, (jnp.zeros((SEGS, chans), F32), jnp.ones((SEGS, chans), F32))
    )
    total_v, total_q = jnp.zeros((1, chans), F32), jnp.ones((1, chans), F32)
    for s in reversed(range(SEGS)):
        total_v = q_end[s : s + 1] * total_v + v_end[s : s + 1]
        total_q = q_end[s : s + 1] * total_q
    ends[tok, 0:1, :] = total_v
    ends[tok, 1:2, :] = total_q
    sends = share_rows(ends, send, recv)
    state = jnp.zeros((1, chans), F32)
    for source in reversed(range(1, count)):
        after = ends[source, 1:2, :] * state + ends[source, 0:1, :]
        state = jnp.where(source > tok, after, state)
    entering = [None] * SEGS
    for s in reversed(range(SEGS)):
        entering[s] = state
        state = q_end[s : s + 1] * state + v_end[s : s + 1]
    for s in range(SEGS):
        edge[s : s + 1, :] = entering[s]
    seg = edge[0:8, :]
    acc[...] = jnp.zeros_like(acc)
    for load in loads[5:]:
        load.wait()

    def folded(x):
        return jnp.sum(eight(x), axis=0)

    def middle_rows(at):
        span = pl.ds(at, step)
        carried = g_s[span, :] + with_segments(a_s[span, :], seg)
        before = lru[span, :]
        keep = pos[span, :] > 0
        r, g, out = rate[span, :], igate[span, :], conv[span, :]
        log_decay = -8.0 * r * sp[...]
        decay = jnp.exp(log_decay)
        square = decay * decay
        mult = jnp.where(keep, jnp.sqrt(minus_expm1(2.0 * log_decay, square)), 1.0)
        scaled = carried * g
        grad_log = jnp.where(keep, decay * carried * before - scaled * out * square / mult, 0.0)
        slope = 8.0 * r * grad_log
        grad_rate = (-slope * sp[...] * (1.0 - r)).astype(BF16)
        grad_input = (scaled * out * mult * (1.0 - g)).astype(BF16)
        grate[span, :] = grad_rate
        ginput[span, :] = grad_input
        gc[span, :] = scaled * mult
        acc[0] += folded(slope * sg[...])
        acc[1] += folded(grad_rate.astype(F32))
        acc[2] += folded(grad_input.astype(F32))

    def middle(i, _):
        at = pl.multiple_of(i * big, 8)
        over_rows(at, big, step, middle_rows)
        span = pl.ds(at, big)
        gc[span, :] += nt_dot(grate[span, :], wr[...]) + nt_dot(ginput[span, :], wi[...])
        return 0

    lax.fori_loop(0, rows // big, middle, 0)
    gc[pl.ds(rows, pad), :] = jnp.zeros((pad, chans), F32)
    for j in range(1, taps):
        value = jnp.zeros((8, chans), F32)
        for k in range(j, taps):
            e = 8 * (k - j)
            masked = jnp.where(pos[e : e + 8, :] >= k, gc[e : e + 8, :], 0.0)
            value = value + cw[k : k + 1, :] * masked
        edge[pad - 8 * j : pad - 8 * j + 8, :] = value
    edge_copy = pltpu.make_async_remote_copy(
        edge, landed, edge_send, edge_recv, (lax.rem(tok + count - 1, count), ch), MESH
    )
    edge_copy.start()
    for stage in range(1, ex.bits):
        ex.relay(stage)

    def last_rows(at):
        span = pl.ds(at, step)
        window = gc[pl.ds(at, step + pad), :]
        where = pos[pl.ds(at, step + pad), :]
        source = ext[pl.ds(at, step + pad), :]
        here = window[:step]
        total = cw[0:1, :] * here
        acc[3] += folded(here)
        acc[4] += folded(here * source[pad : pad + step])
        for k in range(1, taps):
            masked = jnp.where(where >= k, window, 0.0)
            total = total + cw[k : k + 1, :] * masked[8 * k : 8 * k + step]
            acc[4 + k] += folded(masked[:step] * source[pad - 8 * k : pad - 8 * k + step])
        gc[span, :] = total
        grec[span, :] = total.astype(BF16)
        both = total.astype(BF16).astype(F32) * source[pad : pad + step]
        both = both + ggp[span, :].astype(F32) * gpre[span, :]
        row_term[span, :] = jnp.sum(both, axis=1, keepdims=True)

    over_rows(0, rows, step, last_rows)
    edge_copy.wait()
    first_row = lax.broadcasted_iota(jnp.int32, (SEGS, chans), 0) == 0
    for j in range(0, pad, 8):
        joined = jnp.where(first_row, landed[j : j + 8, :], edge[j : j + 8, :])
        at = pl.ds(rows - pad + j, 8)
        gc[at, :] = gc[at, :] + pltpu.roll(joined, SEGS - 1, 0)
    tail = -(-pad // 16) * 16
    span = pl.ds(rows - tail, tail)
    total = gc[span, :].astype(BF16)
    grec[span, :] = total
    both = total.astype(F32) * ext[pl.ds(pad + rows - tail, tail), :]
    both = both + ggp[span, :].astype(F32) * gpre[span, :]
    row_term[span, :] = jnp.sum(both, axis=1, keepdims=True)
    for k in range(8):
        sums[k : k + 1, :] = jnp.sum(acc[k], axis=0, keepdims=True)
    ex.settle(down_sum)
    for copy in sends:
        copy.wait_send()


def recur_bwd(
    g_block, w_out, gpre, ext, conv, rate, igate, lru, pos, cw, wr, wi, sp, sg, down, ident
):
    rows, chans = conv.shape
    n, count = lax.axis_size("ch"), lax.axis_size("tok")
    width = down.shape[1] // n
    pad = 8 * (cw.shape[0] - 1)
    ex = Spread(n, rows, width)
    half = jax.ShapeDtypeStruct((rows, chans), BF16)
    sem = pltpu.SemaphoreType.DMA
    anywhere = pl.BlockSpec(memory_space=pl.ANY)
    vmem = pl.BlockSpec(memory_space=pltpu.VMEM)
    loaded = (g_block, w_out, gpre, ext, conv, rate, igate, lru, wr, wi)
    return pl.pallas_call(
        functools.partial(recur_bwd_kernel, ex),
        out_shape=[
            half, half, half, half,
            jax.ShapeDtypeStruct((8, chans), F32),
            jax.ShapeDtypeStruct((rows, 1), F32),
            jax.ShapeDtypeStruct((rows, width), F32),
        ],
        in_specs=[anywhere] * 8 + [vmem] * 2 + [anywhere] * 2 + [vmem] * 2 + [anywhere],
        out_specs=[vmem] * 7,
        scratch_shapes=[pltpu.VMEM(array.shape, array.dtype) for array in loaded]
        + [
            pltpu.VMEM((rows, chans), F32),
            pltpu.VMEM((rows, chans), F32),
            pltpu.VMEM((rows + pad, chans), F32),
            pltpu.VMEM((count, 8, chans), F32),
            pltpu.VMEM((pad, chans), F32),
            pltpu.VMEM((pad, chans), F32),
            pltpu.VMEM((8, 8, chans), F32),
            sem((len(loaded),)), sem, sem, sem((count - 1,)), sem((count - 1,)),
        ]
        + ex.scratch(),
        compiler_params=pltpu.CompilerParams(
            collective_id=ident, has_side_effects=True, vmem_limit_bytes=62 << 20
        ),
    )(g_block, w_out, gpre, ext, conv, rate, igate, lru, pos, cw, wr, wi, sp, sg, down)


class Exchange(Routes):
    def __init__(self, n, rows, width, chunks, gather):
        super().__init__(n, rows, width)
        self.chunks, self.gather = chunks, gather
        self.size = rows // chunks

    def scratch(self):
        n, rows, half, chunks = self.n, self.rows, self.half, self.chunks
        shapes = [
            pltpu.VMEM((2, n - 1, rows, half), BF16),
            pltpu.VMEM((2, n - 1, rows, half), BF16),
            pltpu.VMEM((len(self.keeps), rows, half), F32),
            pltpu.SemaphoreType.DMA((2, n, chunks)),
            pltpu.SemaphoreType.DMA((2, n, chunks)),
        ]
        if self.gather:
            shapes += [
                pltpu.VMEM((n, 2, rows, half), BF16),
                pltpu.SemaphoreType.DMA((self.bits, 2, chunks)),
                pltpu.SemaphoreType.DMA((self.bits, 2, chunks)),
                pltpu.SemaphoreType.DMA((2, n, chunks)),
                pltpu.SemaphoreType.DMA((2, n, chunks)),
            ]
        return shapes

    def bind(self, refs):
        if self.gather:
            (self.out, self.into, self.acc, self.ss, self.rs,
             self.full, self.gs, self.gr, self.fs, self.fr) = refs
        else:
            self.out, self.into, self.acc, self.ss, self.rs = refs
        self.tok, self.me = lax.axis_index("tok"), lax.axis_index("ch")

    def span(self, c):
        return pl.ds(pl.multiple_of(c * self.size, self.size), self.size)

    def reduce_copy(self, part, mask, c):
        return pltpu.make_async_remote_copy(
            self.out.at[part, mask - 1, self.span(c)],
            self.into.at[part, mask - 1, self.span(c)],
            self.ss.at[part, mask, c],
            self.rs.at[part, mask, c],
            self.peer(self.bit_of(part, mask)),
            MESH,
        )

    def produce(self, c, block):
        span = self.span(c)
        for mask in sorted(range(self.n), key=lambda m: -m.bit_count()):
            value = block(mask)
            for part in range(2):
                piece = value[:, part * self.half : (part + 1) * self.half]
                if (part, mask) in self.keeps:
                    self.acc[self.keeps.index((part, mask)), span, :] = piece
                else:
                    self.out[part, mask - 1, span, :] = piece.astype(BF16)
                    self.reduce_copy(part, mask, c).start()

    def summed(self, part, mask, c):
        span = self.span(c)
        value = self.acc[self.keeps.index((part, mask)), span, :]
        for b in self.incoming(part, mask):
            came = mask | (1 << b)
            self.reduce_copy(part, came, c).wait_recv()
            value = value + self.into[part, came - 1, span, :].astype(F32)
        return value

    def pass_on(self, stage, c):
        for part in range(2):
            for mask in range(1, self.n):
                if self.stage_of(part, mask) == stage:
                    value = self.summed(part, mask, c)
                    self.out[part, mask - 1, self.span(c), :] = value.astype(BF16)
                    self.reduce_copy(part, mask, c).start()

    def close_reduce(self, c):
        for part in range(2):
            for mask in range(1, self.n):
                self.reduce_copy(part, mask, c).wait_send()

    def gather_copy(self, part, mask, b, c):
        block = self.full.at[self.me ^ mask, part, self.span(c)]
        if mask == 0:
            return pltpu.make_async_remote_copy(
                block, block, self.gs.at[b, part, c], self.gr.at[b, part, c], self.peer(b), MESH
            )
        got = mask | (1 << b)
        return pltpu.make_async_remote_copy(
            block, block, self.fs.at[part, got, c], self.fr.at[part, got, c], self.peer(b), MESH
        )

    def arrived(self, part, mask, c):
        block = self.full.at[self.me ^ mask, part, self.span(c)]
        if mask.bit_count() == 1:
            b = low_bit(mask)
            sems = (self.gs.at[b, part, c], self.gr.at[b, part, c])
        else:
            sems = (self.fs.at[part, mask, c], self.fr.at[part, mask, c])
        pltpu.make_async_remote_copy(block, block, *sems, self.peer(0), MESH).wait_recv()

    def gather_start(self, c, halves):
        for part in range(2):
            self.full[self.me, part, self.span(c), :] = halves[part].astype(BF16)
            for b in range(self.bits):
                self.gather_copy(part, 0, b, c).start()

    def nexts(self, part, mask):
        return range(high_bit(mask) + 1, self.bits) if part == 0 else range(low_bit(mask))

    def gather_pass(self, stage, c):
        for mask in [m for m in range(1, self.n) if m.bit_count() == stage]:
            for part in range(2):
                self.arrived(part, mask, c)
                for b in self.nexts(part, mask):
                    self.gather_copy(part, mask, b, c).start()

    def gather_close(self, c):
        for part in range(2):
            self.arrived(part, self.n - 1, c)
        for part in range(2):
            for b in range(self.bits):
                self.gather_copy(part, 0, b, c).wait_send()
            for mask in range(1, self.n):
                for b in self.nexts(part, mask):
                    self.gather_copy(part, mask, b, c).wait_send()

    def piece(self, owner, c):
        span = self.span(c)
        return jnp.concatenate([self.full[owner, 0, span, :], self.full[owner, 1, span, :]], axis=1)

    def own_sum(self, c):
        return [self.summed(part, 0, c) for part in range(2)]

    def run(self, stages, extra=None, after=None):
        depth = len(stages)

        def turn(t, _):
            if extra is not None:
                extra(t)
            for s in reversed(range(depth)):
                c = t - s

                @pl.when(jnp.logical_and(c >= 0, c < self.chunks))
                def _():
                    stages[s](c)

            if after is not None:
                after(t)
            return 0

        lax.fori_loop(0, self.chunks + depth - 1, turn, 0)


def tile_of(size):
    return next(t for t in (512, 384, 256, 128, size) if size % t == 0)


def mid_kernel(
    ex, branch, w_out, x_own, gain, wg_h, wu_h, wd_h, cot_h,
    normed_h, full_h, own_o, scale_o, hidden_h, gg_h, gu_h, down_h,
    wg, wu, wd, cot, normed, hidden, gg, gu, down, wsem, csem, osem, fsem, *refs,
):
    ex.bind(refs)
    n, width = ex.n, ex.width
    units = wg.shape[1]
    tile = tile_of(units)
    greet(ex.neighbours())
    loads = [
        pltpu.make_async_copy(a, b, wsem.at[i])
        for i, (a, b) in enumerate(((wg_h, wg), (wu_h, wu), (wd_h, wd)))
    ]
    for load in loads:
        load.start()

    def cot_load(c):
        return pltpu.make_async_copy(cot_h.at[ex.span(c)], cot, csem)

    outs = ((normed, normed_h), (hidden, hidden_h), (gg, gg_h), (gu, gu_h), (down, down_h))

    def store(i, c):
        source, target = outs[i]
        return pltpu.make_async_copy(source, target.at[ex.span(c)], osem.at[i])

    def full_store(c):
        span = ex.span(c)
        return pltpu.make_async_copy(
            ex.full.at[:, :, span], full_h.at[:, :, span], fsem.at[c]
        )

    cot_load(0).start()

    def first(c):
        rows = branch[ex.span(c), :]

        def block(mask):
            at = pl.multiple_of((ex.me ^ mask) * width, 128)
            return jnp.dot(rows, w_out[:, pl.ds(at, width)], preferred_element_type=F32)

        ex.produce(c, block)

    def own(c):
        span = ex.span(c)
        value = jnp.concatenate(ex.own_sum(c), axis=1) + x_own[span, :].astype(F32)
        own_o[span, :] = value
        ex.gather_start(c, [value[:, : ex.half], value[:, ex.half :]])
        ex.close_reduce(c)

    def final(c):
        ex.gather_close(c)
        full_store(c).start()

        @pl.when(c > 0)
        def _():
            store(0, c - 1).wait()

        def norm_rows(at):
            span = pl.ds(pl.multiple_of(c * ex.size + at, 16), 16)
            pieces = [
                ex.full[d, part, span, :].astype(F32) for d in range(n) for part in range(2)
            ]
            total = sum(jnp.sum(p * p, axis=1, keepdims=True) for p in pieces)
            scale = lax.rsqrt(total * (1.0 / (n * width)) + 1e-06)
            scale_o[span, :] = scale
            for i, p in enumerate(pieces):
                columns = slice(i * ex.half, (i + 1) * ex.half)
                normed[pl.ds(at, 16), columns] = (p * scale * gain[:, columns]).astype(BF16)

        over_rows(0, ex.size, 16, norm_rows)
        store(0, c).start()

    def feed(c):
        @pl.when(c == 0)
        def _():
            for load in loads:
                load.wait()

        cot_load(c).wait()

        @pl.when(c > 0)
        def _():
            for i in range(1, 5):
                store(i, c - 1).wait()

        for j in range(units // tile):
            columns = slice(j * tile, (j + 1) * tile)
            act, slope = gelu_parts(
                jnp.dot(normed[...], wg[:, columns], preferred_element_type=F32)
            )
            up = jnp.dot(normed[...], wu[:, columns], preferred_element_type=F32)
            grad = nt_dot(cot[...], wd[columns, :])
            hidden[:, columns] = (act * up).astype(BF16)
            gg[:, columns] = (grad * up * slope).astype(BF16)
            gu[:, columns] = (grad * act).astype(BF16)

        @pl.when(c + 1 < ex.chunks)
        def _():
            cot_load(c + 1).start()

        for i in range(1, 4):
            store(i, c).start()
        down[...] = jnp.dot(hidden[...], wd[...], preferred_element_type=F32).astype(BF16)
        store(4, c).start()

    stages = [first]
    stages += [functools.partial(ex.pass_on, s) for s in range(1, ex.bits)]
    stages += [own]
    stages += [functools.partial(ex.gather_pass, s) for s in range(1, ex.bits)]
    stages += [final]
    depth = len(stages)

    def after(t):
        c = t - (depth - 1)

        @pl.when(c >= 0)
        def _():
            feed(c)

    ex.run(stages, after=after)
    for i in range(5):
        store(i, ex.chunks - 1).wait()
    for c in range(ex.chunks):
        full_store(c).wait()


def mid_exchange(branch, w_out, x_own, gain, w_gate, w_up, w_down, cot, ident, chunks=4):
    n = lax.axis_size("ch")
    rows, width = x_own.shape
    units = w_gate.shape[1]
    ex = Exchange(n, rows, width, chunks, True)
    whole = jax.ShapeDtypeStruct((rows, n * width), BF16)
    inner = jax.ShapeDtypeStruct((rows, units), BF16)
    wide, narrow = pltpu.VMEM((ex.size, n * width), BF16), pltpu.VMEM((ex.size, units), BF16)
    sem = pltpu.SemaphoreType.DMA
    anywhere = pl.BlockSpec(memory_space=pl.ANY)
    vmem = pl.BlockSpec(memory_space=pltpu.VMEM)
    return pl.pallas_call(
        functools.partial(mid_kernel, ex),
        out_shape=[
            whole,
            jax.ShapeDtypeStruct((n, 2, rows, ex.half), BF16),
            jax.ShapeDtypeStruct((rows, width), F32),
            jax.ShapeDtypeStruct((rows, 1), F32),
            inner, inner, inner, whole,
        ],
        in_specs=[vmem] * 4 + [anywhere] * 4,
        out_specs=[anywhere, anywhere, vmem, vmem] + [anywhere] * 4,
        scratch_shapes=[
            pltpu.VMEM(w_gate.shape, BF16),
            pltpu.VMEM(w_up.shape, BF16),
            pltpu.VMEM(w_down.shape, BF16),
            wide, wide, narrow, narrow, narrow, wide,
            sem((3,)), sem, sem((5,)), sem((chunks,)),
        ]
        + ex.scratch(),
        compiler_params=pltpu.CompilerParams(
            collective_id=ident, has_side_effects=True, vmem_limit_bytes=62 << 20
        ),
    )(branch, w_out, x_own, gain, w_gate, w_up, w_down, cot)


def back_kernel(
    ex, grad_gate, grad_up, w_gate, w_up, full, mid_own, cot, cot_own, scale, gain_own,
    block_o, own_o, gain_o, *refs,
):
    ex.bind(refs)
    n, width = ex.n, ex.width
    greet(ex.neighbours())
    gain_o[...] = jnp.zeros_like(gain_o)

    def whole(d, c):
        span = ex.span(c)
        return jnp.concatenate([full[d, 0, span, :], full[d, 1, span, :]], axis=1).astype(F32)

    def first(c):
        span = ex.span(c)
        left, right = grad_gate[span, :], grad_up[span, :]

        def block(mask):
            at = pl.ds(pl.multiple_of((ex.me ^ mask) * width, 128), width)
            return nt_dot(left, w_gate[at, :]) + nt_dot(right, w_up[at, :])

        ex.produce(c, block)

    def own(c):
        span = ex.span(c)
        s = scale[span, :]
        grad = jnp.concatenate(ex.own_sum(c), axis=1)
        value = cot_own[span, :].astype(F32) + grad * gain_own[...] * s
        own_o[span, :] = value
        ex.gather_start(c, [value[:, : ex.half], value[:, ex.half :]])
        ex.close_reduce(c)
        product = grad * mid_own[span, :] * s
        gain_o[...] += jnp.sum(product.reshape(-1, 8, width), axis=0)

    def final(c):
        ex.gather_close(c)
        span = ex.span(c)
        s = scale[span, :]
        total = jnp.zeros((ex.size, 1), F32)
        for d in range(n):
            columns = slice(d * width, (d + 1) * width)
            delta = ex.piece(d, c).astype(F32) - cot[span, columns].astype(F32)
            total = total + jnp.sum(delta * whole(d, c), axis=1, keepdims=True)
        factor = s * s * total * (1.0 / (n * width))
        own_o[span, :] = own_o[span, :] - factor * mid_own[span, :]
        for d in range(n):
            columns = slice(d * width, (d + 1) * width)
            value = ex.piece(d, c).astype(F32) - factor * whole(d, c)
            block_o[span, columns] = value.astype(BF16)

    stages = [first]
    stages += [functools.partial(ex.pass_on, s) for s in range(1, ex.bits)]
    stages += [own]
    stages += [functools.partial(ex.gather_pass, s) for s in range(1, ex.bits)]
    stages += [final]
    ex.run(stages)


def back_exchange(
    grad_gate, grad_up, w_gate, w_up, full, mid_own, cot, cot_own, scale, gain_own, ident, chunks=4
):
    n = lax.axis_size("ch")
    rows, width = mid_own.shape
    ex = Exchange(n, rows, width, chunks, True)
    return pl.pallas_call(
        functools.partial(back_kernel, ex),
        out_shape=[
            jax.ShapeDtypeStruct((rows, n * width), BF16),
            jax.ShapeDtypeStruct((rows, width), F32),
            jax.ShapeDtypeStruct((8, width), F32),
        ],
        in_specs=whole_vmem(10),
        out_specs=whole_vmem(3),
        scratch_shapes=ex.scratch(),
        compiler_params=pltpu.CompilerParams(
            collective_id=ident, has_side_effects=True, vmem_limit_bytes=63 << 20
        ),
    )(grad_gate, grad_up, w_gate, w_up, full, mid_own, cot, cot_own, scale, gain_own)


class Line:
    def __init__(self, count, shape):
        self.count, self.shape, self.chips = count, shape, count // 2

    def scratch(self):
        blocks = (self.chips, *self.shape)
        hops = (max(self.chips - 1, 1), *self.shape)
        sems = [pltpu.SemaphoreType.DMA((self.chips,))] * 6
        return [pltpu.VMEM(blocks, BF16)] * 3 + [pltpu.VMEM(hops, BF16)] * 4 + sems

    def bind(self, refs):
        (self.pair_out, self.pair_in, self.home, self.up_out, self.up_in, self.dn_out, self.dn_in,
         self.ps, self.pr, self.us, self.ur, self.ds, self.dr) = refs
        self.tok, self.ch = lax.axis_index("tok"), lax.axis_index("ch")
        self.place, self.core = self.tok // 2, self.tok % 2

    def pair_copy(self, z):
        return pltpu.make_async_remote_copy(
            self.pair_out.at[z], self.pair_in.at[z], self.ps.at[z], self.pr.at[z],
            (self.tok + 1 - 2 * self.core, self.ch), MESH,
        )

    def away(self, z):
        return 2 * z + 1 - self.core

    def kept(self, z):
        return 2 * z + self.core

    def put_away(self, z, value):
        self.pair_out[z] = value.astype(BF16)
        self.pair_copy(z).start()

    def put_home(self, z, value):
        self.home[z] = value.astype(BF16)

    def over_rows(self, body):
        size = 32

        def one(i, _):
            body(pl.ds(i * size, size))
            return 0

        lax.fori_loop(0, self.shape[0] // size, one, 0, unroll=2)

    def join(self):
        for z in range(self.chips):
            self.pair_copy(z).wait_recv()

            def add(span, z=z):
                total = self.home[z, span, :].astype(F32) + self.pair_in[z, span, :].astype(F32)
                self.home[z, span, :] = total.astype(BF16)

            self.over_rows(add)

    def ways(self):
        last = self.chips - 1
        rising = (self.up_out, self.up_in, self.us, self.ur, self.place, 1)
        falling = (self.dn_out, self.dn_in, self.ds, self.dr, last - self.place, -1)
        return rising, falling

    def hop(self, way, far):
        out, into, ss, rs, _, sign = way
        count = self.count
        return pltpu.make_async_remote_copy(
            out.at[far - 1], into.at[far - 1], ss.at[far - 1], rs.at[far - 1],
            ((self.tok + 2 * sign + count) % count, self.ch), MESH,
        )

    def step(self, far):
        for way in self.ways():
            out, into, _, _, rank, sign = way

            @pl.when(rank + far <= self.chips - 1)
            def _():
                if far < self.chips - 1:

                    @pl.when(rank >= 1)
                    def _():
                        self.hop(way, far + 1).wait_recv()

                def add(span):
                    value = self.home[self.place + sign * far, span, :].astype(F32)
                    if far < self.chips - 1:
                        came = into[far, span, :].astype(F32)
                        value = value + jnp.where(rank >= 1, came, 0.0)
                    out[far - 1, span, :] = value.astype(BF16)

                self.over_rows(add)
                self.hop(way, far).start()

    def settle(self, result):
        if self.chips > 1:
            for way in self.ways():

                @pl.when(way[4] >= 1)
                def _():
                    self.hop(way, 1).wait_recv()

        def add(span):
            value = self.home[self.place, span, :].astype(F32)
            for way in self.ways() if self.chips > 1 else ():
                value = value + jnp.where(way[4] >= 1, way[1][0, span, :].astype(F32), 0.0)
            result[span, :] = value

        self.over_rows(add)

    def close(self):
        for z in range(self.chips):
            self.pair_copy(z).wait_send()
        for far in range(1, self.chips):
            for way in self.ways():

                @pl.when(way[4] + far <= self.chips - 1)
                def _():
                    self.hop(way, far).wait_send()


def end_kernel(
    ex, lines,
    g_rec, g_pre, w_branch, w_gelu, stat, small, normed, branch, g_block, gate_blocks, x_own,
    scale, gain_own, mid_own,
    input_o, small_o, gain_o, wb_o, wg_o, wo_o, gate_o,
    stats, stat_sum, smalls, gains, gain_acc, st_s, st_r, sm_s, sm_r, gn_s, gn_r, *refs,
):
    held = len(lines[0].scratch())
    for i, line in enumerate(lines):
        line.bind(refs[i * held : (i + 1) * held])
    ex.bind(refs[len(lines) * held :])
    n, width = ex.n, ex.width
    count = lax.axis_size("tok")
    across = [(ex.tok, ex.me ^ m) for m in range(1, n)]
    greet(across + tok_targets())
    stats[ex.me] = stat[...]
    copies = []
    for m in range(1, n):
        copy = pltpu.make_async_remote_copy(
            stats.at[ex.me], stats.at[ex.me], st_s.at[m - 1], st_r.at[m - 1], across[m - 1], MESH
        )
        copy.start()
        copies.append(copy)

    def spread(buffer, send, recv):
        for o, target in enumerate(tok_targets()):
            copy = pltpu.make_async_remote_copy(
                buffer.at[ex.tok], buffer.at[ex.tok], send.at[o], recv.at[o], target, MESH
            )
            copy.start()
            copies.append(copy)

    def collect(buffer, send, recv):
        for o in range(count - 1):
            block = buffer.at[lax.rem(ex.tok + count - 1 - o, count)]
            pltpu.make_async_remote_copy(
                block, block, send.at[o], recv.at[o], tok_targets()[o], MESH
            ).wait_recv()

    smalls[ex.tok] = small[...]
    spread(smalls, sm_s, sm_r)
    wo_line, wb_line, wg_line, gate_line = lines

    def columns(source, block, line):
        size = source.shape[1] // count
        return source[:, pl.ds(pl.multiple_of(block * size, 128), size)]

    def fill(line, product):
        def far_side(z, _):
            line.put_away(z, product(line.away(z)))
            return 0

        def near_side(z, _):
            line.put_home(z, product(line.kept(z)))
            return 0

        lax.fori_loop(0, line.chips, far_side, 0)
        lax.fori_loop(0, line.chips, near_side, 0)

    def start(line):
        line.join()
        if line.chips > 1:
            line.step(line.chips - 1)

    fill(gate_line, lambda d: gate_blocks[d].astype(F32))
    fill(wo_line, lambda d: tn_dot(branch[...], columns(g_block, d, wo_line)))
    start(wo_line)
    fill(wb_line, lambda d: tn_dot(columns(normed, d, wb_line), g_rec[...]))
    start(gate_line)
    start(wb_line)
    fill(wg_line, lambda d: tn_dot(columns(normed, d, wg_line), g_pre[...]))
    start(wg_line)
    for m in range(1, n):
        block = stats.at[ex.me ^ m]
        pltpu.make_async_remote_copy(
            block, block, st_s.at[m - 1], st_r.at[m - 1], across[m - 1], MESH
        ).wait_recv()
    stat_sum[...] = jnp.sum(stats[...], axis=0)
    gain_acc[...] = jnp.zeros_like(gain_acc)

    def first(c):
        span = ex.span(c)
        left, right = g_rec[span, :], g_pre[span, :]

        def block(mask):
            at = pl.ds(pl.multiple_of((ex.me ^ mask) * width, 128), width)
            return nt_dot(left, w_branch[at, :]) + nt_dot(right, w_gelu[at, :])

        ex.produce(c, block)

    def own(c):
        span = ex.span(c)
        grad = jnp.concatenate(ex.own_sum(c), axis=1)
        along = stat_sum[pl.ds(c, 1), :]
        square = (ex.size, ex.size)
        same = lax.broadcasted_iota(jnp.int32, square, 0) == lax.broadcasted_iota(
            jnp.int32, square, 1
        )
        term = jnp.sum(jnp.where(same, along, 0.0), axis=1, keepdims=True)
        s = scale[span, :]
        mine = x_own[span, :].astype(F32)
        input_o[span, :] = (
            mid_own[span, :]
            + s * gain_own[...] * grad
            - s * s * mine * (term * (1.0 / (n * width)))
        )
        gain_acc[...] += jnp.sum((grad * mine * s).reshape(-1, 8, width), axis=0)
        ex.close_reduce(c)

    stages = [first]
    stages += [functools.partial(ex.pass_on, s) for s in range(1, ex.bits)]
    stages += [own]
    turns = ex.chunks + len(stages) - 1
    acts = [
        functools.partial(line.step, far)
        for far in range(wo_line.chips - 2, 0, -1)
        for line in (wo_line, gate_line, wb_line, wg_line)
    ]

    def extra(t):
        for i, act in enumerate(acts):
            when = 2 + i * (turns - 2) // max(len(acts), 1)

            @pl.when(t == when)
            def _():
                act()

    ex.run(stages, extra)
    gains[ex.tok] = jnp.broadcast_to(jnp.sum(gain_acc[...], axis=0, keepdims=True), (8, width))
    spread(gains, gn_s, gn_r)
    collect(smalls, sm_s, sm_r)
    small_o[...] = jnp.sum(smalls[...], axis=0)
    wo_line.settle(wo_o)
    gate_line.settle(gate_o)
    wb_line.settle(wb_o)
    wg_line.settle(wg_o)
    collect(gains, gn_s, gn_r)
    gain_o[...] = jnp.sum(gains[...], axis=0)
    for copy in copies:
        copy.wait_send()
    for line in lines:
        line.close()


def end_exchange(
    g_rec, g_pre, w_branch, w_gelu, stat, small, normed, branch, g_block, gate_blocks, x_own,
    scale, gain_own, mid_own, ident,
):
    n, count = lax.axis_size("ch"), lax.axis_size("tok")
    rows, width = x_own.shape
    chans, total = g_rec.shape[1], normed.shape[1]
    chunks = stat.shape[0]
    ex = Exchange(n, rows, width, chunks, False)
    lines = [
        Line(count, (chans, total // count)),
        Line(count, (total // count, chans)),
        Line(count, (total // count, chans)),
        Line(count, gate_blocks.shape[1:]),
    ]
    sem = pltpu.SemaphoreType.DMA
    return pl.pallas_call(
        functools.partial(end_kernel, ex, lines),
        out_shape=[
            jax.ShapeDtypeStruct((rows, width), F32),
            jax.ShapeDtypeStruct(small.shape, F32),
            jax.ShapeDtypeStruct((8, width), F32),
            jax.ShapeDtypeStruct(lines[1].shape, F32),
            jax.ShapeDtypeStruct(lines[2].shape, F32),
            jax.ShapeDtypeStruct(lines[0].shape, F32),
            jax.ShapeDtypeStruct(lines[3].shape, F32),
        ],
        in_specs=whole_vmem(14),
        out_specs=whole_vmem(7),
        scratch_shapes=[
            pltpu.VMEM((n, *stat.shape), F32),
            pltpu.VMEM(stat.shape, F32),
            pltpu.VMEM((count, *small.shape), F32),
            pltpu.VMEM((count, 8, width), F32),
            pltpu.VMEM((8, width), F32),
            sem((n - 1,)), sem((n - 1,)),
            sem((count - 1,)), sem((count - 1,)),
            sem((count - 1,)), sem((count - 1,)),
        ]
        + [shape for line in lines for shape in line.scratch()]
        + ex.scratch(),
        compiler_params=pltpu.CompilerParams(
            collective_id=ident, has_side_effects=True, vmem_limit_bytes=63 << 20
        ),
    )(g_rec, g_pre, w_branch, w_gelu, stat, small, normed, branch, g_block, gate_blocks, x_own,
      scale, gain_own, mid_own)


def dense_blocks(blocks):
    count, size = blocks.shape[0], blocks.shape[1]
    whole = count * size
    column = lax.broadcasted_iota(jnp.int32, (size, whole), 1)
    copies = (column % size == lax.broadcasted_iota(jnp.int32, (size, whole), 0)).astype(BF16)
    tiled = jnp.dot(blocks.reshape(whole, size), copies, preferred_element_type=F32)
    shape = (whole, whole)
    row = lax.broadcasted_iota(jnp.int32, shape, 0) // size
    same = row == lax.broadcasted_iota(jnp.int32, shape, 1) // size
    return jnp.where(same, tiled, 0.0).astype(BF16)


def diagonal_blocks(full, count, size):
    return jnp.stack(
        [full[i * size : (i + 1) * size, i * size : (i + 1) * size] for i in range(count)]
    )


def to_major(rows):
    count, width = rows.shape
    return rows.reshape(SEGS, count // SEGS, width).swapaxes(0, 1).reshape(count, width)


def from_major(rows):
    count, width = rows.shape
    return rows.reshape(count // SEGS, SEGS, width).swapaxes(0, 1).reshape(count, width)


def tok_scatter(full, dim):
    summed = lax.psum_scatter(full.astype(BF16), "tok", scatter_dimension=dim, tiled=True)
    return summed.astype(F32)


def local(
    layer_in,
    positions,
    norm_gain,
    w_branch,
    w_gelu,
    conv_w,
    conv_b,
    w_rgate,
    b_rgate,
    w_igate,
    b_igate,
    decay_param,
    w_out,
    mlp_gain,
    w_gate,
    w_up,
    w_down,
    cotangent,
):
    rows, width = layer_in.shape
    ch_index = lax.axis_index("ch")
    column = ch_index * width
    chans = decay_param.shape[0]
    gates, gate_width = w_rgate.shape[0], w_rgate.shape[1]
    layer_in, cotangent = to_major(layer_in), to_major(cotangent)
    pos = to_major(positions[:, None])
    pos_tall = jnp.pad(pos, ((0, 8 * (conv_w.shape[0] - 1)), (0, 0)))
    sp = jax.nn.softplus(-decay_param)[None]
    sg = jax.nn.sigmoid(-decay_param)[None]
    dense_r, dense_i = dense_blocks(w_rgate), dense_blocks(w_igate)

    normed, scale_in, gate_pre, ext, conv, rate, igate, lru, branch, cot = front(
        layer_in, norm_gain[None], pos, w_branch, w_gelu, conv_w, conv_b[None], dense_r,
        b_rgate[None], dense_i, b_igate[None], sp, cotangent, 0,
    )
    normed_mid, mid_full, mid_own, scale_mid, hidden, grad_gate, grad_up, down = mid_exchange(
        branch, w_out, layer_in, mlp_gain[None], w_gate, w_up, w_down, cot, 2
    )
    grad_wdown = tok_scatter(tn_dot(hidden, cot), 1)
    grad_wgate = tok_scatter(tn_dot(normed_mid, grad_gate), 0)
    grad_wup = tok_scatter(tn_dot(normed_mid, grad_up), 0)
    gain_mid_own = lax.dynamic_slice_in_dim(mlp_gain, column, width, 0)[None]
    grad_block, grad_mid_own, gain_sum = back_exchange(
        grad_gate, grad_up, w_gate, w_up, mid_full, mid_own, cot, cotangent, scale_mid,
        gain_mid_own, 3,
    )
    count = lax.axis_size("tok")
    grad_rec, grad_gate_pre, grad_rate, grad_input, sums, row_term, mlp_out = recur_bwd(
        grad_block, w_out, gate_pre, ext, conv, rate, igate, lru, pos_tall, conv_w, dense_r,
        dense_i, sp, sg, down, 4,
    )
    layer_out = from_major((mid_own + mlp_out).astype(BF16))
    def gate_blocks(full):
        parts = diagonal_blocks(full, gates, gate_width).reshape(gates, count, -1, gate_width)
        return jnp.swapaxes(parts, 0, 1).reshape(count, -1, gate_width)

    conv_low = conv.astype(BF16)
    gate_parts = jnp.concatenate(
        [gate_blocks(tn_dot(conv_low, grad_rate)), gate_blocks(tn_dot(conv_low, grad_input))],
        axis=1,
    ).astype(BF16)
    stat = row_term.reshape(8, rows // 8)
    small_width = max(chans, width)
    small = jnp.concatenate(
        [
            jnp.pad(sums, ((0, 0), (0, small_width - chans))),
            jnp.pad(
                jnp.sum(gain_sum, axis=0, keepdims=True), ((0, 7), (0, small_width - width))
            ),
        ],
        axis=0,
    )
    own_gain = lax.dynamic_slice_in_dim(norm_gain, column, width, 0)[None]
    input_grad, small_sum, norm_gain_sum, grad_wbranch, grad_wgelu, grad_wout, gate_sum = (
        end_exchange(
            grad_rec, grad_gate_pre, w_branch, w_gelu, stat, small, normed, branch, grad_block,
            gate_parts, layer_in, scale_in, own_gain, grad_mid_own, 5,
        )
    )
    input_grad = from_major(input_grad)
    gate_grads = gate_sum.reshape(2, gates, -1, gate_width)
    own_norm_gain = norm_gain_sum[0]
    return (
        layer_out,
        input_grad,
        own_norm_gain,
        grad_wbranch,
        grad_wgelu,
        small_sum[4:8, :chans],
        small_sum[3, :chans],
        gate_grads[0],
        small_sum[1, :chans],
        gate_grads[1],
        small_sum[2, :chans],
        small_sum[0, :chans],
        grad_wout,
        small_sum[8, :width],
        grad_wgate,
        grad_wup,
        grad_wdown,
    )


def solution(mesh):
    placed = (
        P("tok", "ch"),
        P("tok"),
        P(),
        P(None, "ch"),
        P(None, "ch"),
        P(None, "ch"),
        P("ch"),
        P("ch", None, None),
        P("ch"),
        P("ch", None, None),
        P("ch"),
        P("ch"),
        P("ch", None),
        P(),
        P(None, "ch"),
        P(None, "ch"),
        P("ch", None),
        P("tok", "ch"),
    )
    return jax.shard_map(
        local,
        mesh=mesh,
        in_specs=placed,
        out_specs=(
            P("tok", "ch"),
            P("tok", "ch"),
            P("ch"),
            P("tok", "ch"),
            P("tok", "ch"),
            P(None, "ch"),
            P("ch"),
            P("ch", "tok", None),
            P("ch"),
            P("ch", "tok", None),
            P("ch"),
            P("ch"),
            P("ch", "tok"),
            P("ch"),
            P("tok", "ch"),
            P("tok", "ch"),
            P("ch", "tok"),
        ),
        check_vma=False,
    )
```

time: 858 us -> 536 us (0.62)
  waiting for transfers between devices: 283 us -> 0.05 us
  matrix products: 130 us -> 52 us
  Pallas kernels: 352 us -> 416 us
  other arithmetic: 33.5 us -> 13.5 us
  blocking collectives: 14.2 us -> 0 us
  local copies, waits for them, and re-layouts: 19.2 us -> 31.3 us
    reduce_scatter x6 -> x3, waiting for transfers between devices: 231 us -> 0.01 us  [tok_scatter(): lax.psum_scatter(full.astype(BF16), 'tok', scatter_dimension=dim, tiled=T...]
    pallas_call x5 -> x4, Pallas kernels: 261 us -> 330 us  [the longest x1 107 us: end_exchange(): pl.pallas_call(functools.partial(end_kernel, ex, lines), out_shape=[jax.S...]
    dot_general x7 -> x2, matrix products: 70.9 us -> 2.64 us  [dense_blocks(): jnp.dot(blocks.reshape(whole, size), copies, preferred_element_type=F32)]
    reduce_scatter x1 -> x0, waiting for transfers between devices: 52.8 us -> none  [local(): mlp_out = lax.psum_scatter(down, 'ch', scatter_dimension=1, tiled=True)]
    psum x1 -> x0, blocking collectives: 14.2 us -> none  [local(): lax.psum(jnp.sum(own_normed * own_in * scale_in, axis=0), 'tok')]
    dot_general x8 -> x5, matrix products: 59 us -> 49.3 us  [tn_dot(): lax.dot_general(a, b, (((0,), (0,)), ((), ())), preferred_element_type=F32)]
  transfers between devices with their start and end apart: 9 -> 3, of which waited for: 5 -> 0; matrix products, arithmetic and copies ran while one was open for 17% -> 12% of each run, Pallas kernels for 20% -> 45%
where the time goes in v2:
time: 536 us; the launch traced here: 527 us
  Pallas kernels  416 us (78%)
  matrix products  52 us (10%)
  local copies, waits for them, and re-layouts  31.3 us (6%)
  between operations  14.5 us (3%)
  other arithmetic  13.5 us (3%)
    pallas_call x1, Pallas kernels, end_exchange(): pl.pallas_call(functools.partial(end_kernel, ex, lines), out_shape=[jax.S...  107 us
    pallas_call x1, Pallas kernels, mid_exchange(): pl.pallas_call(functools.partial(mid_kernel, ex), out_shape=[whole, jax.S...  91.9 us
    pallas_call x1, Pallas kernels, front(): pl.pallas_call(functools.partial(front_kernel, ga, late), out_shape=[jax....  86.7 us
    pallas_call x1, Pallas kernels, back_exchange(): pl.pallas_call(functools.partial(back_kernel, ex), out_shape=[jax.ShapeDt...  85.5 us
    dot_general x5, matrix products, tn_dot(): lax.dot_general(a, b, (((0,), (0,)), ((), ())), preferred_element_type=F32)  49.3 us
    pallas_call x1, Pallas kernels, recur_bwd(): pl.pallas_call(functools.partial(recur_bwd_kernel, ex), out_shape=[half,...  44.8 us
  transfers between devices with their start and end apart: 3, of which 0 were waited for; matrix products, arithmetic and copies ran while one was open for 12% of the time, Pallas kernels for 45%

profile of v2, /device:TPU:0, one launch (start us, length us, event | category | flops | bytes accessed | tf_op | source)
XLA Modules:
  0.0 527.0 jit_solution(5290214845300254437)
XLA Ops:
  7.2 0.0 copy-start
  7.2 0.0 reduce-scatter.8.cloned.1.call-start
  7.3 1.3 broadcast_in_dim.36.cb
  8.6 1.3 broadcast_in_dim.38.br
  9.9 1.3 broadcast_in_dim.39.bi
  11.2 0.7 add_divide_fusion
  11.9 0.6 broadcast_in_dim.40.sp
  12.4 0.8 copy.52
  13.2 1.0 reshape.123.pos
  14.2 1.3 fusion.wi_h
  15.5 1.3 fusion.1.wr_h
  16.9 0.5 copy-done.8
  17.4 2.5 copy_bitcast_fusion
  19.9 86.7 %shard_map.305 = (bf16[1024,2048]{1,0:T(8,128)(2,1)}, f32[1024,1]{1,0:T(8,128)}, f32[1024,640]{1,0:T(8,128)}, f32[1048,640]{1,0:T(8,128)}, f32[1024,640]{1,0:T(8...) custom-call(bf16[1024,512]{1,0:T(8,128)(2,1)} %get-tuple-element.144, ...), custom_call_target="tpu_custom_call" | custom-call | tf_op jit(solution)/shard_map/pallas_call | solution.py:484
  106.5 91.9 %shard_map.306 = (bf16[1024,2048]{1,0:T(8,128)(2,1)}, bf16[4,2,1024,256]{3,2,1,0:T(8,128)(2,1)}, f32[1024,512]{1,0:T(8,128)}, f32[1024,1]{1,0:T(8,128)}, bf16[10...) custom-call(bf16[1024,640]{1,0:T(8,128)(2,1)} %get-tuple-element.52.b, ...), custom_call_target="tpu_custom_call" | custom-call | tf_op jit(solution)/shard_map/pallas_call | solution.py:1034
  198.5 11.3 %convolution_convert_fusion = bf16[1536,2048]{1,0:T(8,128)(2,1)} fusion(bf16[1024,1536]{1,0:T(8,128)(2,1)} %get-tuple-element.86, bf16[1024,2048]{1,0:T(8,128)(2,1)} %get-tuple-element.53.cot_h.cot), kind=kOutput, calls=%fused_computation | convolution fusion | flops 6445596672 | bytes 13631488 | tf_op jit(solution)/shard_map/dot_general | solution.py:51
  209.8 0.0 reduce-scatter.8.cloned.1.call-update
  209.8 0.0 reduce-scatter.6.cloned.1.call-start
  209.9 1.8 copy-done.4
  211.7 20.7 %convolution_convert_fusion.1 = bf16[2048,1536]{1,0:T(8,128)(2,1)} fusion(bf16[1024,2048]{1,0:T(8,128)(2,1)} %get-tuple-element.85, bf16[1024,1536]{1,0:T(8,128)(2,1)S(1)} %copy-done.4), kind=kOutput, calls=%fused_computation.1 | convolution fusion | flops 6445596672 | bytes 13631488 | tf_op jit(solution)/shard_map/dot_general | solution.py:51
  232.4 0.0 reduce-scatter.6.cloned.1.call-update
  232.4 0.0 reduce-scatter.4.cloned.1.call-start
  232.5 1.8 copy-done.3
  234.3 11.2 %convolution_convert_fusion.2 = bf16[2048,1536]{1,0:T(8,128)(2,1)} fusion(bf16[1024,2048]{1,0:T(8,128)(2,1)} %get-tuple-element.85, bf16[1024,1536]{1,0:T(8,128)(2,1)S(1)} %copy-done.3), kind=kOutput, calls=%fused_computation.2 | convolution fusion | flops 6445596672 | bytes 13631488 | tf_op jit(solution)/shard_map/dot_general | solution.py:51
  245.6 0.0 reduce-scatter.4.cloned.1.call-update
  245.6 1.4 dynamic_slice.7
  247.0 1.3 dynamic_slice.6
  248.3 0.8 pad.8.pos
  249.2 0.6 broadcast_in_dim.43.sg
  249.7 85.5 %shard_map.307 = (bf16[1024,2048]{1,0:T(8,128)(2,1)}, f32[1024,512]{1,0:T(8,128)}, f32[8,512]{1,0:T(8,128)}) custom-call(bf16[1024,1536]{1,0:T(8,128)(2,1)} %get-tuple-element.55.grad_gate, bf16[1024,1536]{1,0:T(8,128)(2,1)} %get-tuple-element.56.grad_up, bf16[2048,1536]{1,0:T(8,128)(2,1)} %w_gate.1, bf16[2048,1536]{1,0:T(8,128)(2,1)} %w_up.1, ...), custom_call_target="tpu_custom_call" | custom-call | tf_op jit(solution)/shard_map/pallas_call | solution.py:1123
  335.2 44.8 %shard_map.308 = (bf16[1024,640]{1,0:T(8,128)(2,1)}, bf16[1024,640]{1,0:T(8,128)(2,1)}, bf16[1024,640]{1,0:T(8,128)(2,1)}, bf16[1024,640]{1,0:T(8,128)(2,1)}, f3...) custom-call(bf16[1024,2048]{1,0:T(8,128)(2,1)} %get-tuple-element.59.g_block_h.g_block, ...), custom_call_target="tpu_custom_call" | custom-call | tf_op jit(solution)/shard_map/pallas_call | solution.py:711
  380.1 3.5 convolution_convert_fusion.3
  383.6 0.1 fusion.18
  383.8 2.5 convolution_convert_fusion.4
  386.4 0.1 fusion.17
  386.6 0.0 copy-start.15
  386.6 0.0 copy-start.12
  386.6 0.1 maximum_bitcast_fusion.1
  386.8 0.1 copy.60
  386.8 0.1 copy.62
  387.0 0.1 maximum_bitcast_fusion
  387.1 0.1 copy.59
  387.2 0.1 copy.61
  387.2 0.0 copy-done.15
  387.3 0.3 copy-done.12
  387.6 0.8 reduce
  388.4 0.6 select_maximum_fusion.small
  389.1 0.9 pad_maximum_fusion.gate_blocks
  390.0 106.6 %shard_map.309 = (f32[1024,512]{1,0:T(8,128)}, f32[16,640]{1,0:T(8,128)}, f32[8,512]{1,0:T(8,128)}, f32[256,640]{1,0:T(8,128)}, f32[256,640]{1,0:T(8,128)}, /*index=5*/f32[640,256]{1,0:T(8,128)}, f32[160,160]{1,0:T(8,128)}) custom-call(bf16[1024,640]{1,0:T(8,128)(2,1)} %get-tuple-element.68.g_rec, bf16[1024,640]{1,0:T(8,128)(2,1)} %get-tuple-element.69.g_pre, ...), custom_call_target="tpu_custom_call" | custom-call | tf_op jit(solution)/shard_map/pallas_call | solution.py:1416
  496.6 1.3 slice.77
  497.9 1.3 slice.70
  499.3 2.7 fusion.2
  502.0 1.3 copy.58
  503.3 2.5 copy.63
  505.8 1.3 slice.69
  507.1 0.7 copy.65
  507.8 0.7 copy.64
  508.5 1.5 slice_reduce_fusion
  510.0 2.4 convert_element_type.44
  512.4 2.6 convert_element_type.42
  515.0 2.5 convert_element_type.40
  517.5 0.8 copy.73
  518.4 0.8 copy.74
  519.2 0.8 copy.75
  (44 shorter events, 0.4 us)
Async XLA Ops:
  7.2 7.0 %copy-start = (bf16[4,160,160]{2,1,0:T(8,128)(2,1)S(1)}, bf16[4,160,160]{2,1,0:T(8,128)(2,1)}, u32[]{:S(2)}) copy-start(bf16[4,160,160]{2,1,0:T(8,128)(2,1)} %param.27) | copy-start | bytes 614404
  7.2 8.3 %copy-start.16 = (bf16[4,160,160]{2,1,0:T(8,128)(2,1)S(1)}, bf16[4,160,160]{2,1,0:T(8,128)(2,1)}, u32[]{:S(2)}) copy-start(bf16[4,160,160]{2,1,0:T(8,128)(2,1)} %param.25) | copy-start | bytes 614404
  7.2 502.8 %reduce-scatter.8.cloned.1.call-start = ((), (), s32[]{:S(2)}) async-start(), calls=%async_computation.5 | async-start | bytes 7077888 | tf_op jit(solution)/shard_map/reduce_scatter | solution.py:1477
  15.5 1.3 copy-start.7
  15.5 1.8 copy-start.8
  209.8 1.9 copy-start.4
  209.8 302.6 %reduce-scatter.6.cloned.1.call-start = ((), (), s32[]{:S(2)}) async-start(), calls=%async_computation.4 | async-start | bytes 7077888 | tf_op jit(solution)/shard_map/reduce_scatter | solution.py:1477
  232.4 1.9 copy-start.3
  232.4 282.5 %reduce-scatter.4.cloned.1.call-start = ((), (), s32[]{:S(2)}) async-start(), calls=%async_computation.3 | async-start | bytes 7077888 | tf_op jit(solution)/shard_map/reduce_scatter | solution.py:1477
  245.6 2.8 copy-start.2
  380.1 3.7 copy-start.5
  386.6 0.7 copy-start.15
  386.6 1.1 copy-start.12
  386.6 1.8 copy-start.14
  499.3 4.0 copy-start.6
  503.3 3.8 copy-start.13
  512.4 5.1 copy-start.11
  512.4 6.0 %copy-start.10 = (f32[256,640]{1,0:T(8,128)S(1)}, f32[256,640]{1,0:T(8,128)}, u32[]{:S(2)}) copy-start(f32[256,640]{1,0:T(8,128)} %get-tuple-element.166) | copy-start | bytes 1966084
  512.4 7.6 %copy-start.1 = (bf16[4,160,160]{2,1,0:T(8,128)(2,1)S(1)}, bf16[4,160,160]{2,1,0:T(8,128)(2,1)}, u32[]{:S(2)}) copy-start(bf16[4,160,160]{2,1,0:T(8,128)(2,1)} %param.27) | copy-start | bytes 614404
  515.0 4.2 copy-start.9
Sparse Core Ops, SparseCore 0:
  209.9 67.0 reduce-scatter.7
  279.3 68.1 reduce-scatter.5
  349.8 82.8 reduce-scatter.3

commit v3 on v2

--- a/solution.py
+++ b/solution.py
@@ -49,6 +49,23 @@
 
 def tn_dot(a, b):
     return lax.dot_general(a, b, (((0,), (0,)), ((), ())), preferred_element_type=F32)
+
+
+def block_of(shape, axis, size):
+    index = lax.broadcasted_iota(jnp.int32, shape, axis).astype(F32)
+    return jnp.floor((index + 0.5) * (1.0 / size))
+
+
+def tiled_ones(size, count):
+    shape = (size, count * size)
+    row = lax.broadcasted_iota(jnp.int32, shape, 0).astype(F32)
+    column = lax.broadcasted_iota(jnp.int32, shape, 1).astype(F32)
+    return (column - block_of(shape, 1, size) * size == row).astype(BF16)
+
+
+def same_block(count, size):
+    shape = (count * size, count * size)
+    return block_of(shape, 0, size) == block_of(shape, 1, size)
 
 
 def whole_vmem(count):
@@ -295,14 +312,21 @@
 
 
 def front_kernel(
-    ga, late, x, gain, pos, wb_h, wg_h, cw, cb, wr_h, br, wi_h, bi, sp, cot,
-    normed_h, scale, gpre_h, ext_h, conv_h, rate_h, igate_h, lru, branch, cot_full,
-    full, normed, wb, wg, wr, wi, gpre, ext, conv, rate, igate, low, a_s, h_s, carry, halo, ends,
+    ga, late, x, gain, pos_in, wb_h, wg_h, cw, cb_in, br_in, bi_in, dp_in, gate_r, gate_i, cot,
+    normed_h, scale, gpre_h, ext_h, conv_h, rate_h, igate_h, lru, branch, cot_full, vectors, wr, wi,
+    pos,
+    full, normed, wb, wg, gpre, ext, conv, rate, igate, low, a_s, h_s, carry, halo, ends,
     wsem, osem, halo_send, halo_recv, send, recv, *refs,
 ):
     held = len(ga.scratch())
     ga.bind(refs[:held], x, full)
     late.bind(refs[held:], cot, cot_full)
+    cb, br, bi, sp = (vectors.at[i : i + 1] for i in range(4))
+    for i, vector in enumerate((cb_in, br_in, bi_in)):
+        vectors[i : i + 1, :] = vector[...].reshape(1, -1)
+    minus = -dp_in[...].reshape(1, -1)
+    vectors[3:4, :] = jnp.maximum(minus, 0.0) + jnp.log1p(jnp.exp(-jnp.abs(minus)))
+    vectors[4:5, :] = jax.nn.sigmoid(minus)
     rows, chans = gpre.shape
     taps = cw.shape[0]
     pad = 8 * (taps - 1)
@@ -314,10 +338,17 @@
     ga.launch(order)
     loads = [
         pltpu.make_async_copy(a, b, wsem.at[i])
-        for i, (a, b) in enumerate(((wb_h, wb), (wg_h, wg), (wr_h, wr), (wi_h, wi)))
+        for i, (a, b) in enumerate(((wb_h, wb), (wg_h, wg)))
     ]
     for load in loads:
         load.start()
+    blocks, block = gate_r.shape[0] // gate_r.shape[1], gate_r.shape[1]
+    for source, target in ((gate_r, wr), (gate_i, wi)):
+        copies = jnp.dot(source[...], tiled_ones(block, blocks), preferred_element_type=F32)
+        target[...] = jnp.where(same_block(blocks, block), copies, 0.0).astype(BF16)
+    for t in range(rows // SEGS):
+        pos[t * SEGS : (t + 1) * SEGS, :] = pos_in[:, t : t + 1]
+    pos[rows:, :] = jnp.zeros((pos.shape[0] - rows, 1), jnp.int32)
     step = 16
     size = ga.size
     stores = []
@@ -470,7 +501,7 @@
         copy.wait()
 
 
-def front(x, gain, pos, w_branch, w_gelu, cw, cb, wr, br, wi, bi, sp, cot, ident, chunks=4):
+def front(x, gain, pos, w_branch, w_gelu, cw, cb, br, bi, dp, gate_r, gate_i, cot, ident, chunks=4):
     n, count = lax.axis_size("ch"), lax.axis_size("tok")
     rows, width = x.shape
     total, chans = w_branch.shape
@@ -494,22 +525,21 @@
             jax.ShapeDtypeStruct((rows + 8, chans), F32),
             jax.ShapeDtypeStruct(grid, BF16),
             jax.ShapeDtypeStruct((rows, total), BF16),
+            jax.ShapeDtypeStruct((8, chans), F32),
+            jax.ShapeDtypeStruct((chans, chans), BF16),
+            jax.ShapeDtypeStruct((chans, chans), BF16),
+            jax.ShapeDtypeStruct((rows + pad, 1), jnp.int32),
         ],
-        in_specs=[
-            anywhere, vmem, vmem, anywhere, anywhere, vmem, vmem, anywhere, vmem, anywhere, vmem,
-            vmem, anywhere,
-        ],
+        in_specs=[anywhere, vmem, vmem, anywhere, anywhere] + [vmem] * 7 + [anywhere],
         out_specs=[
             anywhere, vmem, anywhere, anywhere, anywhere, anywhere, anywhere, vmem, vmem,
-            anywhere,
+            anywhere, vmem, vmem, vmem, vmem,
         ],
         scratch_shapes=[
             pltpu.VMEM((rows, total), BF16),
             pltpu.VMEM((rows, total), BF16),
             pltpu.VMEM(w_branch.shape, BF16),
             pltpu.VMEM(w_gelu.shape, BF16),
-            pltpu.VMEM(wr.shape, BF16),
-            pltpu.VMEM(wi.shape, BF16),
             pltpu.VMEM(grid, F32),
             pltpu.VMEM((rows + pad, chans), F32),
             pltpu.VMEM(grid, F32),
@@ -521,24 +551,26 @@
             pltpu.VMEM((2, SEGS, chans), F32),
             pltpu.VMEM((pad, chans), F32),
             pltpu.VMEM((count, 8, chans), F32),
-            sem((4,)), sem((6,)), sem, sem, sem((count - 1,)), sem((count - 1,)),
+            sem((2,)), sem((6,)), sem, sem, sem((count - 1,)), sem((count - 1,)),
         ]
         + ga.scratch()
         + late.scratch(),
         compiler_params=pltpu.CompilerParams(
             collective_id=ident, has_side_effects=True, vmem_limit_bytes=60 << 20
         ),
-    )(x, gain, pos, w_branch, w_gelu, cw, cb, wr, br, wi, bi, sp, cot)
+    )(x, gain, pos, w_branch, w_gelu, cw, cb, br, bi, dp, gate_r, gate_i, cot)
 
 
 def recur_bwd_kernel(
-    ex, g_block_h, w_out_h, gpre_h, ext_h, conv_h, rate_h, igate_h, lru_h, pos, cw, wr_h, wi_h, sp,
-    sg, down,
-    grec, ggp, grate, ginput, sums, row_term, down_sum,
+    ex, g_block_h, w_out_h, gpre_h, ext_h, conv_h, rate_h, igate_h, lru_h, pos, cw, wr_h, wi_h, vectors,
+    down,
+    grec, ggp_h, gate_o, sums, row_term, down_sum,
     g_block, w_out, gpre, ext, conv, rate, igate, lru, wr, wi,
-    g_s, a_s, gc, ends, edge, landed, acc, lsem, edge_send, edge_recv, send, recv, *refs,
+    ggp, grate, ginput, low,
+    g_s, a_s, gc, ends, edge, landed, acc, lsem, osem, edge_send, edge_recv, send, recv, *refs,
 ):
     ex.bind(refs, down)
+    sp, sg = vectors.at[3:4], vectors.at[4:5]
     rows, chans = conv.shape
     taps = cw.shape[0]
     pad = 8 * (taps - 1)
@@ -591,6 +623,8 @@
         total_q = q_end[s : s + 1] * total_q
     ends[tok, 0:1, :] = total_v
     ends[tok, 1:2, :] = total_q
+    ggp_store = pltpu.make_async_copy(ggp, ggp_h, osem)
+    ggp_store.start()
     sends = share_rows(ends, send, recv)
     state = jnp.zeros((1, chans), F32)
     for source in reversed(range(1, count)):
@@ -627,6 +661,7 @@
         grad_input = (scaled * out * mult * (1.0 - g)).astype(BF16)
         grate[span, :] = grad_rate
         ginput[span, :] = grad_input
+        low[span, :] = out.astype(BF16)
         gc[span, :] = scaled * mult
         acc[0] += folded(slope * sg[...])
         acc[1] += folded(grad_rate.astype(F32))
@@ -655,7 +690,28 @@
     for stage in range(1, ex.bits):
         ex.relay(stage)
 
+    block = gate_o.shape[2]
+    blocks = chans // block
+    each = block // count
+    shape = (chans, chans)
+    row = lax.broadcasted_iota(jnp.int32, shape, 0).astype(F32)
+    part = block_of(shape, 0, blocks * each)
+    which = block_of(shape, 0, each) - part * blocks
+    within = row - block_of(shape, 0, each) * each
+    wanted = which * block + part * each + within
+    column = lax.broadcasted_iota(jnp.int32, shape, 1).astype(F32)
+    order = (column == wanted).astype(BF16)
+    same = same_block(blocks, block)
+    for i, grads in enumerate((grate, ginput)):
+        kept = jnp.where(same, tn_dot(low[...], grads[...]), 0.0).astype(BF16)
+        folded_in = nt_dot(kept, tiled_ones(block, blocks)).astype(BF16)
+        value = jnp.dot(order, folded_in, preferred_element_type=F32)
+        height = blocks * each
+        for d in range(count):
+            gate_o[d, i * height : (i + 1) * height, :] = value[d * height : (d + 1) * height]
+
     def last_rows(at):
+        step = 32
         span = pl.ds(at, step)
         window = gc[pl.ds(at, step + pad), :]
         where = pos[pl.ds(at, step + pad), :]
@@ -674,7 +730,7 @@
         both = both + ggp[span, :].astype(F32) * gpre[span, :]
         row_term[span, :] = jnp.sum(both, axis=1, keepdims=True)
 
-    over_rows(0, rows, step, last_rows)
+    over_rows(0, rows, 32, last_rows)
     edge_copy.wait()
     first_row = lax.broadcasted_iota(jnp.int32, (SEGS, chans), 0) == 0
     for j in range(0, pad, 8):
@@ -691,12 +747,13 @@
     for k in range(8):
         sums[k : k + 1, :] = jnp.sum(acc[k], axis=0, keepdims=True)
     ex.settle(down_sum)
+    ggp_store.wait()
     for copy in sends:
         copy.wait_send()
 
 
 def recur_bwd(
-    g_block, w_out, gpre, ext, conv, rate, igate, lru, pos, cw, wr, wi, sp, sg, down, ident
+    g_block, w_out, gpre, ext, conv, rate, igate, lru, pos, cw, wr, wi, vectors, down, block, ident
 ):
     rows, chans = conv.shape
     n, count = lax.axis_size("ch"), lax.axis_size("tok")
@@ -711,14 +768,16 @@
     return pl.pallas_call(
         functools.partial(recur_bwd_kernel, ex),
         out_shape=[
-            half, half, half, half,
+            half, half,
+            jax.ShapeDtypeStruct((count, 2 * chans // count, block), F32),
             jax.ShapeDtypeStruct((8, chans), F32),
             jax.ShapeDtypeStruct((rows, 1), F32),
             jax.ShapeDtypeStruct((rows, width), F32),
         ],
-        in_specs=[anywhere] * 8 + [vmem] * 2 + [anywhere] * 2 + [vmem] * 2 + [anywhere],
-        out_specs=[vmem] * 7,
+        in_specs=[anywhere] * 8 + [vmem] * 2 + [anywhere] * 2 + [vmem, anywhere],
+        out_specs=[vmem, anywhere] + [vmem] * 4,
         scratch_shapes=[pltpu.VMEM(array.shape, array.dtype) for array in loaded]
+        + [pltpu.VMEM((rows, chans), BF16)] * 4
         + [
             pltpu.VMEM((rows, chans), F32),
             pltpu.VMEM((rows, chans), F32),
@@ -727,13 +786,13 @@
             pltpu.VMEM((pad, chans), F32),
             pltpu.VMEM((pad, chans), F32),
             pltpu.VMEM((8, 8, chans), F32),
-            sem((len(loaded),)), sem, sem, sem((count - 1,)), sem((count - 1,)),
+            sem((len(loaded),)), sem, sem, sem, sem((count - 1,)), sem((count - 1,)),
         ]
         + ex.scratch(),
         compiler_params=pltpu.CompilerParams(
             collective_id=ident, has_side_effects=True, vmem_limit_bytes=62 << 20
         ),
-    )(g_block, w_out, gpre, ext, conv, rate, igate, lru, pos, cw, wr, wi, sp, sg, down)
+    )(g_block, w_out, gpre, ext, conv, rate, igate, lru, pos, cw, wr, wi, vectors, down)
 
 
 class Exchange(Routes):
@@ -741,13 +800,14 @@
         super().__init__(n, rows, width)
         self.chunks, self.gather = chunks, gather
         self.size = rows // chunks
+        self.ring = min(chunks, self.bits + 2)
 
     def scratch(self):
         n, rows, half, chunks = self.n, self.rows, self.half, self.chunks
         shapes = [
             pltpu.VMEM((2, n - 1, rows, half), BF16),
             pltpu.VMEM((2, n - 1, rows, half), BF16),
-            pltpu.VMEM((len(self.keeps), rows, half), F32),
+            pltpu.VMEM((len(self.keeps), self.ring * self.size, half), F32),
             pltpu.SemaphoreType.DMA((2, n, chunks)),
             pltpu.SemaphoreType.DMA((2, n, chunks)),
         ]
@@ -772,6 +832,10 @@
     def span(self, c):
         return pl.ds(pl.multiple_of(c * self.size, self.size), self.size)
 
+    def acc_span(self, c):
+        at = lax.rem(c, self.ring) * self.size
+        return pl.ds(pl.multiple_of(at, self.size), self.size)
+
     def reduce_copy(self, part, mask, c):
         return pltpu.make_async_remote_copy(
             self.out.at[part, mask - 1, self.span(c)],
@@ -789,14 +853,14 @@
             for part in range(2):
                 piece = value[:, part * self.half : (part + 1) * self.half]
                 if (part, mask) in self.keeps:
-                    self.acc[self.keeps.index((part, mask)), span, :] = piece
+                    self.acc[self.keeps.index((part, mask)), self.acc_span(c), :] = piece
                 else:
                     self.out[part, mask - 1, span, :] = piece.astype(BF16)
                     self.reduce_copy(part, mask, c).start()
 
     def summed(self, part, mask, c):
         span = self.span(c)
-        value = self.acc[self.keeps.index((part, mask)), span, :]
+        value = self.acc[self.keeps.index((part, mask)), self.acc_span(c), :]
         for b in self.incoming(part, mask):
             came = mask | (1 << b)
             self.reduce_copy(part, came, c).wait_recv()
@@ -889,14 +953,18 @@
         lax.fori_loop(0, self.chunks + depth - 1, turn, 0)
 
 
+def own_part(gain, ex):
+    return gain[:, pl.ds(pl.multiple_of(ex.me * ex.width, 128), ex.width)]
+
+
 def tile_of(size):
     return next(t for t in (512, 384, 256, 128, size) if size % t == 0)
 
 
 def mid_kernel(
     ex, branch, w_out, x_own, gain, wg_h, wu_h, wd_h, cot_h,
-    normed_h, full_h, own_o, scale_o, hidden_h, gg_h, gu_h, down_h,
-    wg, wu, wd, cot, normed, hidden, gg, gu, down, wsem, csem, osem, fsem, *refs,
+    normed_h, full_h, own_o, scale_o, hidden_h, gg_h, gu_h,
+    wg, wu, wd, cot, normed, hidden, gg, gu, wsem, csem, osem, fsem, *refs,
 ):
     ex.bind(refs)
     n, width = ex.n, ex.width
@@ -913,7 +981,7 @@
     def cot_load(c):
         return pltpu.make_async_copy(cot_h.at[ex.span(c)], cot, csem)
 
-    outs = ((normed, normed_h), (hidden, hidden_h), (gg, gg_h), (gu, gu_h), (down, down_h))
+    outs = ((normed, normed_h), (hidden, hidden_h), (gg, gg_h), (gu, gu_h))
 
     def store(i, c):
         source, target = outs[i]
@@ -976,7 +1044,7 @@
 
         @pl.when(c > 0)
         def _():
-            for i in range(1, 5):
+            for i in range(1, 4):
                 store(i, c - 1).wait()
 
         for j in range(units // tile):
@@ -996,8 +1064,6 @@
 
         for i in range(1, 4):
             store(i, c).start()
-        down[...] = jnp.dot(hidden[...], wd[...], preferred_element_type=F32).astype(BF16)
-        store(4, c).start()
 
     stages = [first]
     stages += [functools.partial(ex.pass_on, s) for s in range(1, ex.bits)]
@@ -1014,7 +1080,7 @@
             feed(c)
 
     ex.run(stages, after=after)
-    for i in range(5):
+    for i in range(4):
         store(i, ex.chunks - 1).wait()
     for c in range(ex.chunks):
         full_store(c).wait()
@@ -1038,16 +1104,16 @@
             jax.ShapeDtypeStruct((n, 2, rows, ex.half), BF16),
             jax.ShapeDtypeStruct((rows, width), F32),
             jax.ShapeDtypeStruct((rows, 1), F32),
-            inner, inner, inner, whole,
+            inner, inner, inner,
         ],
         in_specs=[vmem] * 4 + [anywhere] * 4,
-        out_specs=[anywhere, anywhere, vmem, vmem] + [anywhere] * 4,
+        out_specs=[anywhere, anywhere, vmem, vmem] + [anywhere] * 3,
         scratch_shapes=[
             pltpu.VMEM(w_gate.shape, BF16),
             pltpu.VMEM(w_up.shape, BF16),
             pltpu.VMEM(w_down.shape, BF16),
-            wide, wide, narrow, narrow, narrow, wide,
-            sem((3,)), sem, sem((5,)), sem((chunks,)),
+            wide, wide, narrow, narrow, narrow,
+            sem((3,)), sem, sem((4,)), sem((chunks,)),
         ]
         + ex.scratch(),
         compiler_params=pltpu.CompilerParams(
@@ -1056,24 +1122,174 @@
     )(branch, w_out, x_own, gain, w_gate, w_up, w_down, cot)
 
 
+class Halving:
+    def __init__(self, count, rows, columns):
+        self.count, self.chips = count, count // 2
+        self.bits = self.chips.bit_length() - 1
+        self.rows, self.columns = rows // count, columns
+
+    def scratch(self):
+        block = (self.rows, self.columns)
+        sem = pltpu.SemaphoreType.DMA
+        steps = max(self.bits, 1)
+        return [
+            pltpu.VMEM((self.chips, *block), BF16),
+            pltpu.VMEM((self.chips, *block), BF16),
+            pltpu.VMEM((max(self.chips - 1, 1), *block), BF16),
+            sem((self.chips,)), sem((self.chips,)), sem((self.chips,)),
+            sem((max(self.chips - 1, 1),)), sem((max(self.chips - 1, 1),)),
+        ]
+
+    def bind(self, refs, source):
+        (self.home, self.pair, self.into, self.ls, self.ps, self.pr, self.ss, self.rs) = refs
+        self.source = source
+        self.tok, self.ch = lax.axis_index("tok"), lax.axis_index("ch")
+        self.place, self.core = self.tok // 2, self.tok % 2
+
+    def targets(self):
+        found = [(self.tok + 1 - 2 * self.core, self.ch)]
+        for step in range(self.bits):
+            bit = (self.place // (1 << step)) % 2
+            found.append((self.tok + (2 << step) * (1 - 2 * bit), self.ch))
+        return found
+
+    def rows_of(self, block):
+        return self.source.at[pl.ds(pl.multiple_of(block * self.rows, self.rows), self.rows)]
+
+    def chip_at(self, i):
+        return self.place + sum(
+            (1 << b) * (1 - 2 * ((self.place // (1 << b)) % 2)) for b in range(self.bits) if i >> b & 1
+        )
+
+    def load(self, i):
+        return pltpu.make_async_copy(
+            self.rows_of(2 * self.chip_at(i) + self.core), self.home.at[i], self.ls.at[i]
+        )
+
+    def pair_copy(self, i):
+        away = self.rows_of(2 * self.chip_at(i) + 1 - self.core)
+        return pltpu.make_async_remote_copy(
+            away, self.pair.at[i], self.ps.at[i], self.pr.at[i], self.targets()[0], MESH
+        )
+
+    def sent_at(self, step):
+        return [i for i in range(1, self.chips) if low_bit(i) == step]
+
+    def hop(self, i):
+        return pltpu.make_async_remote_copy(
+            self.home.at[i], self.into.at[i - 1], self.ss.at[i - 1], self.rs.at[i - 1],
+            self.targets()[1 + low_bit(i)], MESH,
+        )
+
+    def launch(self):
+        for i in reversed(range(self.chips)):
+            self.pair_copy(i).start()
+        for i in reversed(range(self.chips)):
+            self.load(i).start()
+
+    def add(self, i, came):
+        def rows(at):
+            span = pl.ds(pl.multiple_of(at, 16), 16)
+            total = self.home[i, span, :].astype(F32)
+            for ref, j in came:
+                total = total + ref[j, span, :].astype(F32)
+            self.home[i, span, :] = total.astype(BF16)
+
+        over_rows(0, self.rows, 16, rows, 2)
+
+    def join(self):
+        for i in sorted(range(self.chips), key=lambda i: i % 2 == 0):
+            self.load(i).wait()
+            self.pair_copy(i).wait_recv()
+            self.add(i, [(self.pair, i)])
+            if i in self.sent_at(0):
+                self.hop(i).start()
+
+    def step(self, step):
+        for i in self.sent_at(step):
+            came = [i | (1 << b) for b in range(step)]
+            for j in came:
+                self.hop(j).wait_recv()
+            self.add(i, [(self.into, j - 1) for j in came])
+            self.hop(i).start()
+
+    def settle(self, result):
+        came = [1 << b for b in range(self.bits)]
+        for j in came:
+            self.hop(j).wait_recv()
+
+        def rows(at):
+            span = pl.ds(pl.multiple_of(at, 16), 16)
+            total = self.home[0, span, :].astype(F32)
+            for j in came:
+                total = total + self.into[j - 1, span, :].astype(F32)
+            result[span, :] = total
+
+        over_rows(0, self.rows, 16, rows, 2)
+        for i in range(self.chips):
+            self.pair_copy(i).wait_send()
+        for i in range(1, self.chips):
+            self.hop(i).wait_send()
+
+
 def back_kernel(
-    ex, grad_gate, grad_up, w_gate, w_up, full, mid_own, cot, cot_own, scale, gain_own,
-    block_o, own_o, gain_o, *refs,
+    ex, half, gg_h, gu_h, wg_h, wu_h, full_h, mid_own, cot_h, cot_own, scale, gain, source,
+    block_o, own_o, gain_o, sum_o,
+    gg, gu, w_gate, w_up, full, cot, gsem, wsem, fsem, *refs,
 ):
-    ex.bind(refs)
+    held = len(half.scratch())
+    half.bind(refs[:held], source)
+    ex.bind(refs[held:])
     n, width = ex.n, ex.width
-    greet(ex.neighbours())
+    order = sorted(range(n), key=lambda m: -m.bit_count())
+
+    def rows_load(c):
+        span = pl.ds(c * ex.size, ex.size)
+        return [
+            pltpu.make_async_copy(gg_h.at[span], gg.at[span], gsem.at[0, c]),
+            pltpu.make_async_copy(gu_h.at[span], gu.at[span], gsem.at[1, c]),
+        ]
+
+    def weight_load(mask):
+        at = pl.ds(pl.multiple_of((ex.me ^ mask) * width, 128), width)
+        return [
+            pltpu.make_async_copy(wg_h.at[at], w_gate.at[at], wsem.at[0, mask]),
+            pltpu.make_async_copy(wu_h.at[at], w_up.at[at], wsem.at[1, mask]),
+        ]
+
+    def final_load(c):
+        span = ex.span(c)
+        return [
+            pltpu.make_async_copy(full_h.at[:, :, span], full, fsem.at[0]),
+            pltpu.make_async_copy(cot_h.at[span], cot, fsem.at[1]),
+        ]
+
+    for copy in rows_load(0):
+        copy.start()
+    for mask in order:
+        for copy in weight_load(mask):
+            copy.start()
+    for c in range(1, ex.chunks):
+        for copy in rows_load(c):
+            copy.start()
+    for copy in final_load(0):
+        copy.start()
+    greet(ex.neighbours() + half.targets())
+    half.launch()
     gain_o[...] = jnp.zeros_like(gain_o)
-
-    def whole(d, c):
-        span = ex.span(c)
-        return jnp.concatenate([full[d, 0, span, :], full[d, 1, span, :]], axis=1).astype(F32)
 
     def first(c):
         span = ex.span(c)
-        left, right = grad_gate[span, :], grad_up[span, :]
+        for copy in rows_load(c):
+            copy.wait()
+        left, right = gg[span, :], gu[span, :]
 
         def block(mask):
+            @pl.when(c == 0)
+            def _():
+                for copy in weight_load(mask):
+                    copy.wait()
+
             at = pl.ds(pl.multiple_of((ex.me ^ mask) * width, 128), width)
             return nt_dot(left, w_gate[at, :]) + nt_dot(right, w_up[at, :])
 
@@ -1083,7 +1299,7 @@
         span = ex.span(c)
         s = scale[span, :]
         grad = jnp.concatenate(ex.own_sum(c), axis=1)
-        value = cot_own[span, :].astype(F32) + grad * gain_own[...] * s
+        value = cot_own[span, :].astype(F32) + grad * own_part(gain, ex) * s
         own_o[span, :] = value
         ex.gather_start(c, [value[:, : ex.half], value[:, ex.half :]])
         ex.close_reduce(c)
@@ -1092,48 +1308,89 @@
 
     def final(c):
         ex.gather_close(c)
-        span = ex.span(c)
-        s = scale[span, :]
-        total = jnp.zeros((ex.size, 1), F32)
-        for d in range(n):
-            columns = slice(d * width, (d + 1) * width)
-            delta = ex.piece(d, c).astype(F32) - cot[span, columns].astype(F32)
-            total = total + jnp.sum(delta * whole(d, c), axis=1, keepdims=True)
-        factor = s * s * total * (1.0 / (n * width))
-        own_o[span, :] = own_o[span, :] - factor * mid_own[span, :]
-        for d in range(n):
-            columns = slice(d * width, (d + 1) * width)
-            value = ex.piece(d, c).astype(F32) - factor * whole(d, c)
-            block_o[span, columns] = value.astype(BF16)
+        for copy in final_load(c):
+            copy.wait()
+
+        def rows(at):
+            here = pl.ds(pl.multiple_of(at, 16), 16)
+            span = pl.ds(pl.multiple_of(c * ex.size + at, 16), 16)
+            s = scale[span, :]
+            pieces = [(d, part) for d in range(n) for part in range(2)]
+            values = [ex.full[d, part, span, :].astype(F32) for d, part in pieces]
+            mids = [full[d, part, here, :].astype(F32) for d, part in pieces]
+            total = jnp.zeros((16, 1), F32)
+            for i, (value, middle) in enumerate(zip(values, mids, strict=True)):
+                columns = slice(i * ex.half, (i + 1) * ex.half)
+                delta = value - cot[here, columns].astype(F32)
+                total = total + jnp.sum(delta * middle, axis=1, keepdims=True)
+            factor = s * s * total * (1.0 / (n * width))
+            own_o[span, :] = own_o[span, :] - factor * mid_own[span, :]
+            for i, (value, middle) in enumerate(zip(values, mids, strict=True)):
+                columns = slice(i * ex.half, (i + 1) * ex.half)
+                block_o[span, columns] = (value - factor * middle).astype(BF16)
+
+        over_rows(0, ex.size, 16, rows)
+
+        @pl.when(c + 1 < ex.chunks)
+        def _():
+            for copy in final_load(c + 1):
+                copy.start()
 
     stages = [first]
     stages += [functools.partial(ex.pass_on, s) for s in range(1, ex.bits)]
     stages += [own]
     stages += [functools.partial(ex.gather_pass, s) for s in range(1, ex.bits)]
     stages += [final]
-    ex.run(stages)
+    turns = ex.chunks + len(stages) - 1
+    acts = [half.join] + [functools.partial(half.step, s) for s in range(1, half.bits)]
+
+    def after(t):
+        for i, act in enumerate(acts):
+
+            @pl.when(t == min(i * turns // len(acts) + i, turns - 1))
+            def _():
+                act()
+
+    ex.run(stages, after=after)
+    half.settle(sum_o)
 
 
 def back_exchange(
-    grad_gate, grad_up, w_gate, w_up, full, mid_own, cot, cot_own, scale, gain_own, ident, chunks=4
+    grad_gate, grad_up, w_gate, w_up, full, mid_own, cot, cot_own, scale, gain_own, source, ident,
+    chunks=4,
 ):
-    n = lax.axis_size("ch")
+    n, count = lax.axis_size("ch"), lax.axis_size("tok")
     rows, width = mid_own.shape
     ex = Exchange(n, rows, width, chunks, True)
+    half = Halving(count, *source.shape)
+    sem = pltpu.SemaphoreType.DMA
+    anywhere = pl.BlockSpec(memory_space=pl.ANY)
+    vmem = pl.BlockSpec(memory_space=pltpu.VMEM)
     return pl.pallas_call(
-        functools.partial(back_kernel, ex),
+        functools.partial(back_kernel, ex, half),
         out_shape=[
             jax.ShapeDtypeStruct((rows, n * width), BF16),
             jax.ShapeDtypeStruct((rows, width), F32),
             jax.ShapeDtypeStruct((8, width), F32),
+            jax.ShapeDtypeStruct((half.rows, half.columns), F32),
         ],
-        in_specs=whole_vmem(10),
-        out_specs=whole_vmem(3),
-        scratch_shapes=ex.scratch(),
+        in_specs=[anywhere] * 5 + [vmem, anywhere, vmem, vmem, vmem, anywhere],
+        out_specs=[vmem] * 4,
+        scratch_shapes=[
+            pltpu.VMEM(grad_gate.shape, BF16),
+            pltpu.VMEM(grad_up.shape, BF16),
+            pltpu.VMEM(w_gate.shape, BF16),
+            pltpu.VMEM(w_up.shape, BF16),
+            pltpu.VMEM((n, 2, ex.size, ex.half), BF16),
+            pltpu.VMEM((ex.size, n * width), BF16),
+            sem((2, chunks)), sem((2, n)), sem((2,)),
+        ]
+        + half.scratch()
+        + ex.scratch(),
         compiler_params=pltpu.CompilerParams(
             collective_id=ident, has_side_effects=True, vmem_limit_bytes=63 << 20
         ),
-    )(grad_gate, grad_up, w_gate, w_up, full, mid_own, cot, cot_own, scale, gain_own)
+    )(grad_gate, grad_up, w_gate, w_up, full, mid_own, cot, cot_own, scale, gain_own, source)
 
 
 class Line:
@@ -1255,10 +1512,10 @@
 
 def end_kernel(
     ex, lines,
-    g_rec, g_pre, w_branch, w_gelu, stat, small, normed, branch, g_block, gate_blocks, x_own,
-    scale, gain_own, mid_own,
-    input_o, small_o, gain_o, wb_o, wg_o, wo_o, gate_o,
-    stats, stat_sum, smalls, gains, gain_acc, st_s, st_r, sm_s, sm_r, gn_s, gn_r, *refs,
+    g_rec, g_pre, wb_h, wg_h, stat, small, normed_h, branch, block_h, gate_blocks, x_own,
+    scale, gain, mid_own,
+    input_h, small_o, gain_o, mlp_o, taps_o, wb_o, wg_o, wo_o, gate_o,
+    input_v, wide, w_branch, w_gelu, isem, lsem, stats, stat_sum, smalls, gains, gain_acc, st_s, st_r, sm_s, sm_r, gn_s, gn_r, *refs,
 ):
     held = len(lines[0].scratch())
     for i, line in enumerate(lines):
@@ -1267,6 +1524,14 @@
     n, width = ex.n, ex.width
     count = lax.axis_size("tok")
     across = [(ex.tok, ex.me ^ m) for m in range(1, n)]
+    block_load = pltpu.make_async_copy(block_h, wide, lsem.at[0])
+    normed_load = pltpu.make_async_copy(normed_h, wide, lsem.at[1])
+    loads = [
+        pltpu.make_async_copy(wb_h, w_branch, lsem.at[2]),
+        pltpu.make_async_copy(wg_h, w_gelu, lsem.at[3]),
+    ]
+    for load in [block_load, *loads]:
+        load.start()
     greet(across + tok_targets())
     stats[ex.me] = stat[...]
     copies = []
@@ -1318,19 +1583,31 @@
             line.step(line.chips - 1)
 
     fill(gate_line, lambda d: gate_blocks[d].astype(F32))
-    fill(wo_line, lambda d: tn_dot(branch[...], columns(g_block, d, wo_line)))
+    block_load.wait()
+    fill(wo_line, lambda d: tn_dot(branch[...], columns(wide, d, wo_line)))
+    normed_load.start()
     start(wo_line)
-    fill(wb_line, lambda d: tn_dot(columns(normed, d, wb_line), g_rec[...]))
+    normed_load.wait()
+    fill(wb_line, lambda d: tn_dot(columns(wide, d, wb_line), g_rec[...]))
     start(gate_line)
     start(wb_line)
-    fill(wg_line, lambda d: tn_dot(columns(normed, d, wg_line), g_pre[...]))
+    fill(wg_line, lambda d: tn_dot(columns(wide, d, wg_line), g_pre[...]))
     start(wg_line)
+    for load in loads:
+        load.wait()
     for m in range(1, n):
         block = stats.at[ex.me ^ m]
         pltpu.make_async_remote_copy(
             block, block, st_s.at[m - 1], st_r.at[m - 1], across[m - 1], MESH
         ).wait_recv()
     stat_sum[...] = jnp.sum(stats[...], axis=0)
+    steps = ex.size // SEGS
+
+    def input_store(c, part):
+        source = input_v.at[pl.ds(c * steps, steps), part]
+        target = input_h.at[pl.ds(part * (ex.rows // SEGS) + c * steps, steps)]
+        return pltpu.make_async_copy(source, target, isem.at[part, c])
+
     gain_acc[...] = jnp.zeros_like(gain_acc)
 
     def first(c):
@@ -1354,11 +1631,14 @@
         term = jnp.sum(jnp.where(same, along, 0.0), axis=1, keepdims=True)
         s = scale[span, :]
         mine = x_own[span, :].astype(F32)
-        input_o[span, :] = (
+        value = (
             mid_own[span, :]
-            + s * gain_own[...] * grad
+            + s * own_part(gain, ex) * grad
             - s * s * mine * (term * (1.0 / (n * width)))
         )
+        input_v[pl.ds(c * steps, steps)] = eight(value)
+        for part in range(SEGS):
+            input_store(c, part).start()
         gain_acc[...] += jnp.sum((grad * mine * s).reshape(-1, 8, width), axis=0)
         ex.close_reduce(c)
 
@@ -1384,13 +1664,20 @@
     gains[ex.tok] = jnp.broadcast_to(jnp.sum(gain_acc[...], axis=0, keepdims=True), (8, width))
     spread(gains, gn_s, gn_r)
     collect(smalls, sm_s, sm_r)
-    small_o[...] = jnp.sum(smalls[...], axis=0)
+    all_small = jnp.sum(smalls[...], axis=0)
+    chans = g_rec.shape[1]
+    small_o[...] = all_small[:8]
+    taps_o[...] = all_small[4:8, :chans]
+    mlp_o[...] = all_small[8:9, :width]
     wo_line.settle(wo_o)
     gate_line.settle(gate_o)
     wb_line.settle(wb_o)
     wg_line.settle(wg_o)
     collect(gains, gn_s, gn_r)
-    gain_o[...] = jnp.sum(gains[...], axis=0)
+    gain_o[...] = jnp.sum(gains[...], axis=0)[0:1]
+    for c in range(ex.chunks):
+        for part in range(SEGS):
+            input_store(c, part).wait()
     for copy in copies:
         copy.wait_send()
     for line in lines:
@@ -1399,7 +1686,7 @@
 
 def end_exchange(
     g_rec, g_pre, w_branch, w_gelu, stat, small, normed, branch, g_block, gate_blocks, x_own,
-    scale, gain_own, mid_own, ident,
+    scale, gain, mid_own, ident,
 ):
     n, count = lax.axis_size("ch"), lax.axis_size("tok")
     rows, width = x_own.shape
@@ -1412,21 +1699,31 @@
         Line(count, (total // count, chans)),
         Line(count, gate_blocks.shape[1:]),
     ]
+    anywhere = pl.BlockSpec(memory_space=pl.ANY)
+    vmem = pl.BlockSpec(memory_space=pltpu.VMEM)
     sem = pltpu.SemaphoreType.DMA
     return pl.pallas_call(
         functools.partial(end_kernel, ex, lines),
         out_shape=[
             jax.ShapeDtypeStruct((rows, width), F32),
-            jax.ShapeDtypeStruct(small.shape, F32),
-            jax.ShapeDtypeStruct((8, width), F32),
+            jax.ShapeDtypeStruct((8, small.shape[1]), F32),
+            jax.ShapeDtypeStruct((1, width), F32),
+            jax.ShapeDtypeStruct((1, width), F32),
+            jax.ShapeDtypeStruct((4, chans), F32),
             jax.ShapeDtypeStruct(lines[1].shape, F32),
             jax.ShapeDtypeStruct(lines[2].shape, F32),
             jax.ShapeDtypeStruct(lines[0].shape, F32),
             jax.ShapeDtypeStruct(lines[3].shape, F32),
         ],
-        in_specs=whole_vmem(14),
-        out_specs=whole_vmem(7),
+        in_specs=[anywhere if i in (2, 3, 6, 8) else vmem for i in range(14)],
+        out_specs=[anywhere] + whole_vmem(8),
         scratch_shapes=[
+            pltpu.VMEM((rows // SEGS, SEGS, width), F32),
+            pltpu.VMEM((rows, total), BF16),
+            pltpu.VMEM(w_branch.shape, BF16),
+            pltpu.VMEM(w_gelu.shape, BF16),
+            sem((SEGS, chunks)),
+            sem((4,)),
             pltpu.VMEM((n, *stat.shape), F32),
             pltpu.VMEM(stat.shape, F32),
             pltpu.VMEM((count, *small.shape), F32),
@@ -1442,25 +1739,7 @@
             collective_id=ident, has_side_effects=True, vmem_limit_bytes=63 << 20
         ),
     )(g_rec, g_pre, w_branch, w_gelu, stat, small, normed, branch, g_block, gate_blocks, x_own,
-      scale, gain_own, mid_own)
-
-
-def dense_blocks(blocks):
-    count, size = blocks.shape[0], blocks.shape[1]
-    whole = count * size
-    column = lax.broadcasted_iota(jnp.int32, (size, whole), 1)
-    copies = (column % size == lax.broadcasted_iota(jnp.int32, (size, whole), 0)).astype(BF16)
-    tiled = jnp.dot(blocks.reshape(whole, size), copies, preferred_element_type=F32)
-    shape = (whole, whole)
-    row = lax.broadcasted_iota(jnp.int32, shape, 0) // size
-    same = row == lax.broadcasted_iota(jnp.int32, shape, 1) // size
-    return jnp.where(same, tiled, 0.0).astype(BF16)
-
-
-def diagonal_blocks(full, count, size):
-    return jnp.stack(
-        [full[i * size : (i + 1) * size, i * size : (i + 1) * size] for i in range(count)]
-    )
+      scale, gain, mid_own)
 
 
 def to_major(rows):
@@ -1473,9 +1752,116 @@
     return rows.reshape(count // SEGS, SEGS, width).swapaxes(0, 1).reshape(count, width)
 
 
+def rows_kernel(a, b, out):
+    out[...] = jnp.dot(a[...], b[...], preferred_element_type=F32).astype(BF16)
+
+
+def rows_product(a, b):
+    rows, inner = a.shape
+    right = b.shape[1]
+    size = min(256, rows)
+    return pl.pallas_call(
+        rows_kernel,
+        grid=(rows // size,),
+        out_shape=jax.ShapeDtypeStruct((rows, right), BF16),
+        in_specs=[
+            pl.BlockSpec((size, inner), lambda i: (i, 0)),
+            pl.BlockSpec((inner, right), lambda i: (0, 0)),
+        ],
+        out_specs=pl.BlockSpec((size, right), lambda i: (i, 0)),
+        compiler_params=pltpu.CompilerParams(vmem_limit_bytes=62 << 20),
+    )(a, b)
+
+
+def weight_kernel(spans, a, *refs):
+    out, at = refs[-1], 0
+    for b, (first, last) in zip(refs, spans, strict=False):
+        width = last - first
+        out[:, at : at + width] = tn_dot(a[...], b[:, first:last]).astype(BF16)
+        at += width
+
+
+def weight_product(a, *parts):
+    rows, left = a.shape
+    spans = [span for _, span in parts]
+    right = sum(last - first for first, last in spans)
+    size = next(t for t in (256, 128, left) if left % t == 0)
+    return pl.pallas_call(
+        functools.partial(weight_kernel, spans),
+        grid=(left // size,),
+        out_shape=jax.ShapeDtypeStruct((left, right), BF16),
+        in_specs=[pl.BlockSpec((rows, size), lambda i: (0, i))]
+        + [pl.BlockSpec(b.shape, lambda i: (0, 0)) for b, _ in parts],
+        out_specs=pl.BlockSpec((size, right), lambda i: (i, 0)),
+        compiler_params=pltpu.CompilerParams(vmem_limit_bytes=62 << 20),
+    )(a, *[b for b, _ in parts])
+
+
 def tok_scatter(full, dim):
-    summed = lax.psum_scatter(full.astype(BF16), "tok", scatter_dimension=dim, tiled=True)
-    return summed.astype(F32)
+    return lax.psum_scatter(full, "tok", scatter_dimension=dim, tiled=True)
+
+
+def close_kernel(
+    input_in, wb_in, wg_in, wo_in, small, mlp, gain, taps, gate, wide, left, down,
+    input_o, wb_o, wg_o, wo_o, gain_o, mlp_o, taps_o, convb_o, br_o, bi_o, decay_o, wr_o, wi_o,
+    wgate_o, wup_o, wdown_o, sem,
+):
+    pairs = ((input_in, input_o), (wb_in, wb_o), (wg_in, wg_o), (wo_in, wo_o))
+    copies = [pltpu.make_async_copy(a, b, sem.at[i]) for i, (a, b) in enumerate(pairs)]
+    for copy in copies:
+        copy.start()
+    units = wgate_o.shape[1]
+    cut = left.shape[1]
+
+    def rows(at):
+        span = pl.ds(at, 16)
+        wgate_o[span, :] = wide[span, :units].astype(F32)
+        wup_o[span, :cut] = left[span, :]
+        wup_o[span, cut:] = wide[span, units:].astype(F32)
+
+    over_rows(0, wgate_o.shape[0], 16, rows, 2)
+
+    def tall_rows(at):
+        span = pl.ds(at, 16)
+        wdown_o[span, :] = down[span, :].astype(F32)
+
+    over_rows(0, wdown_o.shape[0], 16, tall_rows, 4)
+    for i, out in enumerate((decay_o, br_o, bi_o, convb_o)):
+        out[...] = small[i, : out.shape[0]]
+    gain_o[...] = gain[0, :]
+    mlp_o[...] = mlp[0, :]
+    taps_o[...] = taps[...]
+    each, count = wr_o.shape[0], wr_o.shape[1]
+    for half, out in enumerate((wr_o, wi_o)):
+        for i in range(count):
+            first = (half * count + i) * each
+            out[:, i, :] = gate[first : first + each, :]
+    for copy in copies:
+        copy.wait()
+
+
+def close(input_in, wb, wg, wo, small, mlp, gain, taps, gate, wide, left, down, chans, units, gates):
+    width, block = gain.shape[1], gate.shape[1]
+    each = gate.shape[0] // (2 * gates)
+    anywhere = pl.BlockSpec(memory_space=pl.ANY)
+    vmem = pl.BlockSpec(memory_space=pltpu.VMEM)
+
+    def like(*shape):
+        return jax.ShapeDtypeStruct(shape, F32)
+
+    return pl.pallas_call(
+        close_kernel,
+        out_shape=[
+            like(*input_in.shape), like(*wb.shape), like(*wg.shape), like(*wo.shape), like(width),
+            like(width), like(*taps.shape), like(chans), like(chans), like(chans), like(chans),
+            like(each, gates, block), like(each, gates, block), like(wide.shape[0], units),
+            like(wide.shape[0], units), like(*down.shape),
+        ],
+        in_specs=[vmem] * 12,
+        out_specs=[anywhere] * 4 + [vmem] * 12,
+        scratch_shapes=[pltpu.SemaphoreType.DMA((4,))],
+        compiler_params=pltpu.CompilerParams(vmem_limit_bytes=60 << 20),
+    )(input_in, wb, wg, wo, small, mlp, gain, taps, gate, wide, left, down)
 
 
 def local(
@@ -1504,42 +1890,41 @@
     chans = decay_param.shape[0]
     gates, gate_width = w_rgate.shape[0], w_rgate.shape[1]
     layer_in, cotangent = to_major(layer_in), to_major(cotangent)
-    pos = to_major(positions[:, None])
-    pos_tall = jnp.pad(pos, ((0, 8 * (conv_w.shape[0] - 1)), (0, 0)))
-    sp = jax.nn.softplus(-decay_param)[None]
-    sg = jax.nn.sigmoid(-decay_param)[None]
-    dense_r, dense_i = dense_blocks(w_rgate), dense_blocks(w_igate)
-
-    normed, scale_in, gate_pre, ext, conv, rate, igate, lru, branch, cot = front(
-        layer_in, norm_gain[None], pos, w_branch, w_gelu, conv_w, conv_b[None], dense_r,
-        b_rgate[None], dense_i, b_igate[None], sp, cotangent, 0,
+    pos = positions.reshape(SEGS, rows // SEGS)
+    (
+        normed, scale_in, gate_pre, ext, conv, rate, igate, lru, branch, cot, vectors, dense_r,
+        dense_i, pos_tall,
+    ) = front(
+        layer_in, norm_gain[None], pos, w_branch, w_gelu, conv_w, conv_b, b_rgate, b_igate,
+        decay_param, w_rgate.reshape(-1, gate_width), w_igate.reshape(-1, gate_width),
+        cotangent, 0,
     )
-    normed_mid, mid_full, mid_own, scale_mid, hidden, grad_gate, grad_up, down = mid_exchange(
+    normed_mid, mid_full, mid_own, scale_mid, hidden, grad_gate, grad_up = mid_exchange(
         branch, w_out, layer_in, mlp_gain[None], w_gate, w_up, w_down, cot, 2
     )
-    grad_wdown = tok_scatter(tn_dot(hidden, cot), 1)
-    grad_wgate = tok_scatter(tn_dot(normed_mid, grad_gate), 0)
-    grad_wup = tok_scatter(tn_dot(normed_mid, grad_up), 0)
-    gain_mid_own = lax.dynamic_slice_in_dim(mlp_gain, column, width, 0)[None]
-    grad_block, grad_mid_own, gain_sum = back_exchange(
+    count = lax.axis_size("tok")
+    total, units = cot.shape[1], hidden.shape[1]
+    cut = units // 3
+    wdown_full = weight_product(hidden, (cot, (0, total)))
+    grad_up, wdown_full = lax.optimization_barrier((grad_up, wdown_full))
+    grad_wdown = tok_scatter(wdown_full, 1)
+    wup_one = weight_product(normed_mid, (grad_up, (0, cut)))
+    grad_gate, wup_one = lax.optimization_barrier((grad_gate, wup_one))
+    wide_full = weight_product(normed_mid, (grad_gate, (0, units)), (grad_up, (cut, units)))
+    wide_sum = tok_scatter(wide_full, 0)
+    hidden, wide_full = lax.optimization_barrier((hidden, wide_full))
+    down = rows_product(hidden, w_down)
+    grad_gate, down = lax.optimization_barrier((grad_gate, down))
+    grad_block, grad_mid_own, gain_sum, wup_left = back_exchange(
         grad_gate, grad_up, w_gate, w_up, mid_full, mid_own, cot, cotangent, scale_mid,
-        gain_mid_own, 3,
+        mlp_gain[None], wup_one, 3,
     )
-    count = lax.axis_size("tok")
-    grad_rec, grad_gate_pre, grad_rate, grad_input, sums, row_term, mlp_out = recur_bwd(
+    grad_rec, grad_gate_pre, gate_parts, sums, row_term, mlp_out = recur_bwd(
         grad_block, w_out, gate_pre, ext, conv, rate, igate, lru, pos_tall, conv_w, dense_r,
-        dense_i, sp, sg, down, 4,
+        dense_i, vectors, down, gate_width, 4,
     )
     layer_out = from_major((mid_own + mlp_out).astype(BF16))
-    def gate_blocks(full):
-        parts = diagonal_blocks(full, gates, gate_width).reshape(gates, count, -1, gate_width)
-        return jnp.swapaxes(parts, 0, 1).reshape(count, -1, gate_width)
-
-    conv_low = conv.astype(BF16)
-    gate_parts = jnp.concatenate(
-        [gate_blocks(tn_dot(conv_low, grad_rate)), gate_blocks(tn_dot(conv_low, grad_input))],
-        axis=1,
-    ).astype(BF16)
+    grad_rec, layer_out = lax.optimization_barrier((grad_rec, layer_out))
     stat = row_term.reshape(8, rows // 8)
     small_width = max(chans, width)
     small = jnp.concatenate(
@@ -1551,31 +1936,36 @@
         ],
         axis=0,
     )
-    own_gain = lax.dynamic_slice_in_dim(norm_gain, column, width, 0)[None]
-    input_grad, small_sum, norm_gain_sum, grad_wbranch, grad_wgelu, grad_wout, gate_sum = (
-        end_exchange(
-            grad_rec, grad_gate_pre, w_branch, w_gelu, stat, small, normed, branch, grad_block,
-            gate_parts, layer_in, scale_in, own_gain, grad_mid_own, 5,
-        )
+    (
+        input_grad, small_sum, norm_gain_sum, mlp_gain_sum, taps_sum, grad_wbranch, grad_wgelu,
+        grad_wout, gate_sum,
+    ) = end_exchange(
+        grad_rec, grad_gate_pre, w_branch, w_gelu, stat, small, normed, branch, grad_block,
+        gate_parts, layer_in, scale_in, norm_gain[None], grad_mid_own, 5,
     )
-    input_grad = from_major(input_grad)
-    gate_grads = gate_sum.reshape(2, gates, -1, gate_width)
-    own_norm_gain = norm_gain_sum[0]
+    (
+        input_grad, grad_wbranch, grad_wgelu, grad_wout, own_norm_gain, own_mlp_gain, grad_taps,
+        grad_convb, grad_brate, grad_binput, grad_decay, grad_wrate, grad_winput, grad_wgate,
+        grad_wup, grad_wdown,
+    ) = close(
+        input_grad, grad_wbranch, grad_wgelu, grad_wout, small_sum, mlp_gain_sum, norm_gain_sum,
+        taps_sum, gate_sum, wide_sum, wup_left, grad_wdown, chans, units, gates,
+    )
     return (
         layer_out,
         input_grad,
         own_norm_gain,
         grad_wbranch,
         grad_wgelu,
-        small_sum[4:8, :chans],
-        small_sum[3, :chans],
-        gate_grads[0],
-        small_sum[1, :chans],
-        gate_grads[1],
-        small_sum[2, :chans],
-        small_sum[0, :chans],
+        grad_taps,
+        grad_convb,
+        grad_wrate.swapaxes(0, 1),
+        grad_brate,
+        grad_winput.swapaxes(0, 1),
+        grad_binput,
+        grad_decay,
         grad_wout,
-        small_sum[8, :width],
+        own_mlp_gain,
         grad_wgate,
         grad_wup,
         grad_wdown,

time: 536 us -> 495 us (0.924)
  matrix products: 52 us -> 0 us
  Pallas kernels: 416 us -> 463 us
  local copies, waits for them, and re-layouts: 31.3 us -> 5.31 us
  other arithmetic: 13.5 us -> 4.15 us
    pallas_call x1 -> x6, Pallas kernels: 85.5 us -> 147 us  [the longest x1 90.8 us: back_exchange(): pl.pallas_call(functools.partial(back_kernel, ex, half), out_shape=[jax.S...]
    dot_general x7 -> x0, matrix products: 52 us -> none  [the longest x5 49.3 us: tn_dot(): lax.dot_general(a, b, (((0,), (0,)), ((), ())), preferred_element_type=F32)]
    pallas_call x1, Pallas kernels: 107 us -> 93.9 us  [end_exchange(): pl.pallas_call(functools.partial(end_kernel, ex, lines), out_shape=[jax.S...]
    unnamed x39 -> x6, local copies, waits for them, and re-layouts: 8.46 us -> 0.01 us
    convert_element_type x3 -> x0, other arithmetic: 7.5 us -> none  [tok_scatter(): return summed.astype(F32)]
    slice x7 -> x0, local copies, waits for them, and re-layouts: 5.71 us -> none  [the longest x1 1.51 us: local(): small_sum[0, :chans]]
  transfers between devices with their start and end apart: 3 -> 2, of which waited for: 0 -> 0; matrix products, arithmetic and copies ran while one was open for 12% -> 1% of each run, Pallas kernels for 45% -> 55%
where the time goes in v3:
time: 495 us; the launch traced here: 487 us
  Pallas kernels  463 us (94%)
  between operations  14.6 us (3%)
  local copies, waits for them, and re-layouts  5.31 us (1%)
    pallas_call x1, Pallas kernels, end_exchange(): pl.pallas_call(functools.partial(end_kernel, ex, lines), out_shape=[jax.S...  93.9 us
    pallas_call x1, Pallas kernels, back_exchange(): pl.pallas_call(functools.partial(back_kernel, ex, half), out_shape=[jax.S...  90.8 us
    pallas_call x1, Pallas kernels, front(): pl.pallas_call(functools.partial(front_kernel, ga, late), out_shape=[jax....  87.4 us
    pallas_call x1, Pallas kernels, mid_exchange(): pl.pallas_call(functools.partial(mid_kernel, ex), out_shape=[whole, jax.S...  86.9 us
    pallas_call x1, Pallas kernels, recur_bwd(): pl.pallas_call(functools.partial(recur_bwd_kernel, ex), out_shape=[half,...  47.7 us
    pallas_call x3, Pallas kernels, weight_product(): pl.pallas_call(functools.partial(weight_kernel, spans), grid=(left // siz...  37.3 us
    pallas_call x1, Pallas kernels, rows_product(): pl.pallas_call(rows_kernel, grid=(rows // size,), out_shape=jax.ShapeDtyp...  11.3 us
  transfers between devices with their start and end apart: 2, of which 0 were waited for; matrix products, arithmetic and copies ran while one was open for 1% of the time, Pallas kernels for 55%

profile of v3, /device:TPU:0, one launch (start us, length us, event | category | flops | bytes accessed | tf_op | source)
XLA Modules:
  0.0 486.7 jit_solution(11381053471433370880)
XLA Ops:
  7.2 0.0 reduce-scatter.5.cloned.1.call-start
  7.2 4.0 copy_bitcast_fusion
  11.3 87.4 %shard_map.305 = (bf16[1024,2048]{1,0:T(8,128)(2,1)}, f32[1024,1]{1,0:T(8,128)}, f32[1024,640]{1,0:T(8,128)}, f32[1048,640]{1,0:T(8,128)}, f32[1024,640]{1,0:T(8...) custom-call(bf16[1024,512]{1,0:T(8,128)(2,1)} %get-tuple-element.148, ...), custom_call_target="tpu_custom_call" | custom-call | tf_op jit(solution)/shard_map/pallas_call | solution.py:515
  98.7 86.9 %shard_map.306 = (bf16[1024,2048]{1,0:T(8,128)(2,1)}, bf16[4,2,1024,256]{3,2,1,0:T(8,128)(2,1)}, f32[1024,512]{1,0:T(8,128)}, f32[1024,1]{1,0:T(8,128)}, bf16[10...) custom-call(bf16[1024,640]{1,0:T(8,128)(2,1)} %get-tuple-element.82.branch, ...), custom_call_target="tpu_custom_call" | custom-call | tf_op jit(solution)/shard_map/pallas_call | solution.py:1100
  185.6 11.4 %shard_map.307 = bf16[1536,2048]{1,0:T(8,128)(2,1)} custom-call(bf16[1024,1536]{1,0:T(8,128)(2,1)} %get-tuple-element.90.a, bf16[1024,2048]{1,0:T(8,128)(2,1)} %get-tuple-element.83.cot_h.refs_0_), custom_call_target="tpu_custom_call" | custom-call | tf_op jit(solution)/shard_map/pallas_call | solution.py:1789
  197.0 0.0 reduce-scatter.5.cloned.1.call-update
  197.0 0.0 reduce-scatter.3.cloned.1.call-start
  197.1 9.1 %shard_map.308.source = bf16[2048,512]{1,0:T(8,128)(2,1)} custom-call(bf16[1024,2048]{1,0:T(8,128)(2,1)} %get-tuple-element.85.a, bf16[1024,1536]{1,0:T(8,128)(2,1)} %get-tuple-element.88.refs_0_.refs_1_.gu_h), custom_call_target="tpu_custom_call" | custom-call | tf_op jit(solution)/shard_map/pallas_call | solution.py:1789
  206.2 16.8 %shard_map.309 = bf16[2048,2560]{1,0:T(8,128)(2,1)} custom-call(bf16[1024,2048]{1,0:T(8,128)(2,1)} %get-tuple-element.85.a, bf16[1024,1536]{1,0:T(8,128)(2,1)} %get-tuple-element.91.refs_0_.gg_h, bf16[1024,1536]{1,0:T(8,128)(2,1)} %get-tuple-element.88.refs_0_.refs_1_.gu_h), custom_call_target="tpu_custom_call" | custom-call | tf_op jit(solution)/shard_map/pallas_call | solution.py:1789
  222.9 0.0 reduce-scatter.3.cloned.1.call-update
  223.0 11.3 %shard_map.310.down = bf16[1024,2048]{1,0:T(8,128)(2,1)} custom-call(bf16[1024,1536]{1,0:T(8,128)(2,1)} %get-tuple-element.90.a, bf16[1536,2048]{1,0:T(8,128)(2,1)} %b.1), custom_call_target="tpu_custom_call" | custom-call | tf_op jit(solution)/shard_map/pallas_call | solution.py:1763
  234.3 90.8 %shard_map.311 = (bf16[1024,2048]{1,0:T(8,128)(2,1)}, f32[1024,512]{1,0:T(8,128)}, f32[8,512]{1,0:T(8,128)}, f32[256,512]{1,0:T(8,128)}) custom-call(bf16[1024,1536]{1,0:T(8,128)(2,1)} %get-tuple-element.91.refs_0_.gg_h, bf16[1024,1536]{1,0:T(8,128)(2,1)} %get-tuple-element.88.refs_0_.refs_1_.gu_h, bf16[2048,1536]{1,0:T(8,128)(2,1)} %wg_h.6, ...), custom_call_target="tpu_custom_call" | custom-call | tf_op jit(solution)/shard_map/pallas_call | solution.py:1369
  325.1 47.7 %shard_map.312 = (bf16[1024,640]{1,0:T(8,128)(2,1)}, bf16[1024,640]{1,0:T(8,128)(2,1)}, f32[8,160,160]{2,1,0:T(8,128)}, f32[8,640]{1,0:T(8,128)}, f32[1024,1]{1,0:T(8,128)}, /*index=5*/f32[1024,512]{1,0:T(8,128)}) custom-call(bf16[1024,2048]{1,0:T(8,128)(2,1)} %get-tuple-element.96.g_block_h.block_h, bf16[640,2048]{1,0:T(8,128)(2,1)} %w_out_h.1, ...), custom_call_target="tpu_custom_call" | custom-call | tf_op jit(solution)/shard_map/pallas_call | solution.py:768
  372.7 0.0 copy-start.2
  372.7 0.0 copy-start
  372.7 2.7 fusion
  375.5 0.0 copy-start.1
  375.5 1.3 copy.40
  376.7 0.0 copy-done.2
  376.8 0.0 copy-done
  376.8 0.8 reduce
  377.6 0.0 copy-done.1
  377.6 0.6 select_maximum_fusion.small
  378.2 93.9 %shard_map.313 = (f32[1024,512]{1,0:T(8,128)}, f32[8,640]{1,0:T(8,128)}, f32[1,512]{1,0:T(1,128)}, f32[1,512]{1,0:T(1,128)}, f32[4,640]{1,0:T(4,128)}, /*index=5...) custom-call(bf16[1024,640]{1,0:T(8,128)(2,1)} %get-tuple-element.111.g_rec, ...), custom_call_target="tpu_custom_call" | custom-call | tf_op jit(solution)/shard_map/pallas_call | solution.py:1705
  472.1 0.0 reduce-scatter.5.cloned.1.call-done.down
  472.1 0.0 reduce-scatter.3.cloned.1.call-done.wide
  472.2 7.3 %shard_map.314 = (f32[1024,512]{1,0:T(8,128)}, f32[256,640]{1,0:T(8,128)}, f32[256,640]{1,0:T(8,128)}, f32[640,256]{1,0:T(8,128)}, f32[512]{0:T(512)}, /*index=5...) custom-call(f32[1024,512]{1,0:T(8,128)} %get-tuple-element.120.input, ...), custom_call_target="tpu_custom_call" | custom-call | tf_op jit(solution)/shard_map/pallas_call | solution.py:1852
  (1 shorter events, 0.0 us)
Async XLA Ops:
  7.2 464.9 %reduce-scatter.5.cloned.1.call-start = ((), (), s32[]{:S(2)}) async-start(), calls=%async_computation.3 | async-start | bytes 7077888 | tf_op jit(solution)/shard_map/reduce_scatter | solution.py:1801
  197.0 275.1 %reduce-scatter.3.cloned.1.call-start = ((), (), s32[]{:S(2)}) async-start(), calls=%async_computation.2 | async-start | bytes 11796480 | tf_op jit(solution)/shard_map/reduce_scatter | solution.py:1801
  372.7 4.0 copy-start.2
  372.7 4.0 copy-start
  375.5 2.1 copy-start.1
Sparse Core Ops, SparseCore 0:
  197.2 78.3 reduce-scatter.4
  277.8 121.5 reduce-scatter.2

commit v4 on v3

--- a/solution.py
+++ b/solution.py
@@ -195,7 +195,7 @@
     return [(lax.rem(tok + o, count), ch) for o in range(1, count)]
 
 
-def share_rows(buffer, send, recv):
+def share_start(buffer, send, recv):
     tok = lax.axis_index("tok")
     copies = []
     for o, target in enumerate(tok_targets()):
@@ -204,13 +204,17 @@
         )
         copy.start()
         copies.append(copy)
+    return copies
+
+
+def share_wait(buffer, send, recv):
+    tok = lax.axis_index("tok")
     count = lax.axis_size("tok")
     for o in range(count - 1):
         source = lax.rem(tok + count - 1 - o, count)
         pltpu.make_async_remote_copy(
             buffer.at[source], buffer.at[source], send.at[o], recv.at[o], tok_targets()[o], MESH
         ).wait_recv()
-    return copies
 
 
 class Gather(Routes):
@@ -312,10 +316,11 @@
 
 
 def front_kernel(
-    ga, late, x, gain, pos_in, wb_h, wg_h, cw, cb_in, br_in, bi_in, dp_in, gate_r, gate_i, cot,
+    ga, late, x, gain, pos_in, wb_h, wg_h, cw, cb_in, br_in, bi_in, dp_in, gate_r, gate_i, cot_in,
     normed_h, scale, gpre_h, ext_h, conv_h, rate_h, igate_h, lru, branch, cot_full, vectors, wr, wi,
-    pos,
-    full, normed, wb, wg, gpre, ext, conv, rate, igate, low, a_s, h_s, carry, halo, ends,
+    pos, cot,
+    full, normed, wb, wg, gpre, ext, conv, rate, igate, low, a_s, h_s, act_s, cot_f, carry, halo,
+    ends,
     wsem, osem, halo_send, halo_recv, send, recv, *refs,
 ):
     held = len(ga.scratch())
@@ -346,6 +351,24 @@
     for source, target in ((gate_r, wr), (gate_i, wi)):
         copies = jnp.dot(source[...], tiled_ones(block, blocks), preferred_element_type=F32)
         target[...] = jnp.where(same_block(blocks, block), copies, 0.0).astype(BF16)
+    length = rows // SEGS
+    for s in range(SEGS):
+
+        def lift(at, s=s):
+            value = cot_in[pl.ds(s * length + at, 16), :].astype(F32)
+            cot_f[pl.ds(at, 16), s, :] = value
+
+        over_rows(0, length, 16, lift)
+
+    def lower(at):
+        value = cot_f[pl.ds(at, 2)].reshape(16, cot_f.shape[2])
+        cot[pl.ds(pl.multiple_of(at * SEGS, 16), 16), :] = value.astype(BF16)
+
+    def lower_two(i, _):
+        lower(2 * i)
+        return 0
+
+    lax.fori_loop(0, length // 2, lower_two, 0, unroll=2)
     for t in range(rows // SEGS):
         pos[t * SEGS : (t + 1) * SEGS, :] = pos_in[:, t : t + 1]
     pos[rows:, :] = jnp.zeros((pos.shape[0] - rows, 1), jnp.int32)
@@ -472,7 +495,14 @@
         total_p = p_end[s : s + 1] * total_p
     ends[tok, 0:1, :] = total_h
     ends[tok, 1:2, :] = total_p
-    sends = share_rows(ends, send, recv)
+    sends = share_start(ends, send, recv)
+
+    def act_rows(at):
+        span = pl.ds(at, step)
+        act_s[span, :] = gelu_value(gpre[span, :])
+
+    over_rows(0, rows, step, act_rows, 2)
+    share_wait(ends, send, recv)
     state = jnp.zeros((1, chans), F32)
     for source in range(count - 1):
         after = ends[source, 1:2, :] * state + ends[source, 0:1, :]
@@ -487,7 +517,7 @@
         span = pl.ds(at, step)
         value = h_s[span, :] + with_segments(a_s[span, :], seg)
         lru[pl.ds(8 + at, step), :] = value
-        branch[span, :] = (value * gelu_value(gpre[span, :])).astype(BF16)
+        branch[span, :] = (value * act_s[span, :]).astype(BF16)
 
     over_rows(0, rows, step, finish_rows, 2)
     for copy in sends:
@@ -529,11 +559,12 @@
             jax.ShapeDtypeStruct((chans, chans), BF16),
             jax.ShapeDtypeStruct((chans, chans), BF16),
             jax.ShapeDtypeStruct((rows + pad, 1), jnp.int32),
+            jax.ShapeDtypeStruct(x.shape, BF16),
         ],
-        in_specs=[anywhere, vmem, vmem, anywhere, anywhere] + [vmem] * 7 + [anywhere],
+        in_specs=[anywhere, vmem, vmem, anywhere, anywhere] + [vmem] * 8,
         out_specs=[
             anywhere, vmem, anywhere, anywhere, anywhere, anywhere, anywhere, vmem, vmem,
-            anywhere, vmem, vmem, vmem, vmem,
+            anywhere, vmem, vmem, vmem, vmem, vmem,
         ],
         scratch_shapes=[
             pltpu.VMEM((rows, total), BF16),
@@ -548,6 +579,8 @@
             pltpu.VMEM(grid, BF16),
             pltpu.VMEM(grid, F32),
             pltpu.VMEM(grid, F32),
+            pltpu.VMEM(grid, F32),
+            pltpu.VMEM((rows // SEGS, SEGS, width), F32),
             pltpu.VMEM((2, SEGS, chans), F32),
             pltpu.VMEM((pad, chans), F32),
             pltpu.VMEM((count, 8, chans), F32),
@@ -562,14 +595,16 @@
 
 
 def recur_bwd_kernel(
-    ex, g_block_h, w_out_h, gpre_h, ext_h, conv_h, rate_h, igate_h, lru_h, pos, cw, wr_h, wi_h, vectors,
-    down,
-    grec, ggp_h, gate_o, sums, row_term, down_sum,
-    g_block, w_out, gpre, ext, conv, rate, igate, lru, wr, wi,
+    ex, line, g_block_h, w_out_h, gpre_h, ext_h, conv_h, rate_h, igate_h, lru_h, pos, cw, wr_h, wi_h, vectors,
+    down, branch_h,
+    grec, ggp_h, gate_o, sums, row_term, down_sum, carry_o,
+    g_block, w_out, gpre, ext, conv, rate, igate, lru, wr, wi, branch,
     ggp, grate, ginput, low,
     g_s, a_s, gc, ends, edge, landed, acc, lsem, osem, edge_send, edge_recv, send, recv, *refs,
 ):
-    ex.bind(refs, down)
+    held = len(line.scratch())
+    line.bind(refs[:held])
+    ex.bind(refs[held:], down)
     sp, sg = vectors.at[3:4], vectors.at[4:5]
     rows, chans = conv.shape
     taps = cw.shape[0]
@@ -578,7 +613,7 @@
     count = lax.axis_size("tok")
     pairs = (
         (g_block_h, g_block), (w_out_h, w_out), (gpre_h, gpre), (lru_h, lru), (rate_h, rate),
-        (igate_h, igate), (conv_h, conv), (wr_h, wr), (wi_h, wi), (ext_h, ext),
+        (branch_h, branch), (igate_h, igate), (conv_h, conv), (wr_h, wr), (wi_h, wi), (ext_h, ext),
     )
     loads = [pltpu.make_async_copy(a, b, lsem.at[i]) for i, (a, b) in enumerate(pairs)]
     for load in loads:
@@ -625,7 +660,13 @@
     ends[tok, 1:2, :] = total_q
     ggp_store = pltpu.make_async_copy(ggp, ggp_h, osem)
     ggp_store.start()
-    sends = share_rows(ends, send, recv)
+    sends = share_start(ends, send, recv)
+    loads[5].wait()
+    fill(line, lambda d: tn_dot(branch[...], block_columns(g_block, d, count)))
+    share_wait(ends, send, recv)
+    line.join()
+    if line.chips > 2:
+        line.step(line.chips - 1)
     state = jnp.zeros((1, chans), F32)
     for source in reversed(range(1, count)):
         after = ends[source, 1:2, :] * state + ends[source, 0:1, :]
@@ -638,7 +679,7 @@
         edge[s : s + 1, :] = entering[s]
     seg = edge[0:8, :]
     acc[...] = jnp.zeros_like(acc)
-    for load in loads[5:]:
+    for load in loads[6:]:
         load.wait()
 
     def folded(x):
@@ -689,6 +730,8 @@
     edge_copy.start()
     for stage in range(1, ex.bits):
         ex.relay(stage)
+    for far in range(line.chips - 2, 1, -1):
+        line.step(far)
 
     block = gate_o.shape[2]
     blocks = chans // block
@@ -747,13 +790,17 @@
     for k in range(8):
         sums[k : k + 1, :] = jnp.sum(acc[k], axis=0, keepdims=True)
     ex.settle(down_sum)
+    line.step(1, carry_o)
+    carry_o[2] = line.home[line.place]
+    line.close(2)
     ggp_store.wait()
     for copy in sends:
         copy.wait_send()
 
 
 def recur_bwd(
-    g_block, w_out, gpre, ext, conv, rate, igate, lru, pos, cw, wr, wi, vectors, down, block, ident
+    g_block, w_out, gpre, ext, conv, rate, igate, lru, pos, cw, wr, wi, vectors, down, branch, block,
+    ident,
 ):
     rows, chans = conv.shape
     n, count = lax.axis_size("ch"), lax.axis_size("tok")
@@ -764,18 +811,20 @@
     sem = pltpu.SemaphoreType.DMA
     anywhere = pl.BlockSpec(memory_space=pl.ANY)
     vmem = pl.BlockSpec(memory_space=pltpu.VMEM)
-    loaded = (g_block, w_out, gpre, ext, conv, rate, igate, lru, wr, wi)
+    loaded = (g_block, w_out, gpre, ext, conv, rate, igate, lru, wr, wi, branch)
+    line = Line(count, (chans, g_block.shape[1] // count))
     return pl.pallas_call(
-        functools.partial(recur_bwd_kernel, ex),
+        functools.partial(recur_bwd_kernel, ex, line),
         out_shape=[
             half, half,
             jax.ShapeDtypeStruct((count, 2 * chans // count, block), F32),
             jax.ShapeDtypeStruct((8, chans), F32),
             jax.ShapeDtypeStruct((rows, 1), F32),
             jax.ShapeDtypeStruct((rows, width), F32),
+            jax.ShapeDtypeStruct((3, *line.shape), BF16),
         ],
-        in_specs=[anywhere] * 8 + [vmem] * 2 + [anywhere] * 2 + [vmem, anywhere],
-        out_specs=[vmem, anywhere] + [vmem] * 4,
+        in_specs=[anywhere] * 8 + [vmem] * 2 + [anywhere] * 2 + [vmem, anywhere, anywhere],
+        out_specs=[vmem, anywhere] + [vmem] * 5,
         scratch_shapes=[pltpu.VMEM(array.shape, array.dtype) for array in loaded]
         + [pltpu.VMEM((rows, chans), BF16)] * 4
         + [
@@ -788,11 +837,13 @@
             pltpu.VMEM((8, 8, chans), F32),
             sem((len(loaded),)), sem, sem, sem, sem((count - 1,)), sem((count - 1,)),
         ]
+        + line.scratch()
         + ex.scratch(),
         compiler_params=pltpu.CompilerParams(
             collective_id=ident, has_side_effects=True, vmem_limit_bytes=62 << 20
         ),
-    )(g_block, w_out, gpre, ext, conv, rate, igate, lru, pos, cw, wr, wi, vectors, down)
+    )(g_block, w_out, gpre, ext, conv, rate, igate, lru, pos, cw, wr, wi, vectors, down,
+      branch)
 
 
 class Exchange(Routes):
@@ -1461,7 +1512,7 @@
             ((self.tok + 2 * sign + count) % count, self.ch), MESH,
         )
 
-    def step(self, far):
+    def step(self, far, kept=None):
         for way in self.ways():
             out, into, _, _, rank, sign = way
 
@@ -1481,7 +1532,10 @@
                     out[far - 1, span, :] = value.astype(BF16)
 
                 self.over_rows(add)
-                self.hop(way, far).start()
+                if kept is None:
+                    self.hop(way, far).start()
+                else:
+                    kept[(1 - sign) // 2] = out[far - 1]
 
     def settle(self, result):
         if self.chips > 1:
@@ -1499,10 +1553,10 @@
 
         self.over_rows(add)
 
-    def close(self):
+    def close(self, least=1):
         for z in range(self.chips):
             self.pair_copy(z).wait_send()
-        for far in range(1, self.chips):
+        for far in range(least, self.chips):
             for way in self.ways():
 
                 @pl.when(way[4] + far <= self.chips - 1)
@@ -1510,9 +1564,79 @@
                     self.hop(way, far).wait_send()
 
 
+class LastHop:
+    def __init__(self, count, shape):
+        self.count, self.chips, self.shape = count, count // 2, shape
+
+    def scratch(self):
+        sem = pltpu.SemaphoreType.DMA((2,))
+        return [pltpu.VMEM((2, *self.shape), BF16), sem, sem]
+
+    def bind(self, refs, carry):
+        self.into, self.ss, self.rs = refs
+        self.carry = carry
+        self.tok, self.ch = lax.axis_index("tok"), lax.axis_index("ch")
+        place = self.tok // 2
+        self.ranks = (place, self.chips - 1 - place)
+
+    def hop(self, way):
+        target = (self.tok + 2 - 4 * way + self.count) % self.count
+        return pltpu.make_async_remote_copy(
+            self.carry.at[way], self.into.at[way], self.ss.at[way], self.rs.at[way],
+            (target, self.ch), MESH,
+        )
+
+    def launch(self):
+        for way in range(2):
+
+            @pl.when(self.ranks[1 - way] >= 1)
+            def _():
+                self.hop(way).start()
+
+    def settle(self, result):
+        for way in range(2):
+
+            @pl.when(self.ranks[way] >= 1)
+            def _():
+                self.hop(way).wait_recv()
+
+        def rows(at):
+            span = pl.ds(pl.multiple_of(at, 16), 16)
+            total = self.carry[2, span, :].astype(F32)
+            for way in range(2):
+                came = self.into[way, span, :].astype(F32)
+                total = total + jnp.where(self.ranks[way] >= 1, came, 0.0)
+            result[span, :] = total
+
+        over_rows(0, self.shape[0], 16, rows, 2)
+        for way in range(2):
+
+            @pl.when(self.ranks[1 - way] >= 1)
+            def _():
+                self.hop(way).wait_send()
+
+
+def block_columns(source, block, count):
+    size = source.shape[1] // count
+    return source[:, pl.ds(pl.multiple_of(block * size, 128), size)]
+
+
+def fill(line, product):
+    def far_side(z, _):
+        line.put_away(z, product(line.away(z)))
+        return 0
+
+    def near_side(z, _):
+        line.put_home(z, product(line.kept(z)))
+        return 0
+
+    lax.fori_loop(0, line.chips, far_side, 0)
+    lax.fori_loop(0, line.chips, near_side, 0)
+
+
 def end_kernel(
-    ex, lines,
-    g_rec, g_pre, wb_h, wg_h, stat, small, normed_h, branch, block_h, gate_blocks, x_own,
+    ex, last, lines,
+    g_rec, g_pre, wb_h, wg_h, stat, small, normed_h, carry, gate_blocks, x_own,
     scale, gain, mid_own,
     input_h, small_o, gain_o, mlp_o, taps_o, wb_o, wg_o, wo_o, gate_o,
     input_v, wide, w_branch, w_gelu, isem, lsem, stats, stat_sum, smalls, gains, gain_acc, st_s, st_r, sm_s, sm_r, gn_s, gn_r, *refs,
@@ -1520,19 +1644,21 @@
     held = len(lines[0].scratch())
     for i, line in enumerate(lines):
         line.bind(refs[i * held : (i + 1) * held])
-    ex.bind(refs[len(lines) * held :])
+    ahead = len(lines) * held
+    last.bind(refs[ahead : ahead + 3], carry)
+    ex.bind(refs[ahead + 3 :])
     n, width = ex.n, ex.width
     count = lax.axis_size("tok")
     across = [(ex.tok, ex.me ^ m) for m in range(1, n)]
-    block_load = pltpu.make_async_copy(block_h, wide, lsem.at[0])
-    normed_load = pltpu.make_async_copy(normed_h, wide, lsem.at[1])
+    normed_load = pltpu.make_async_copy(normed_h, wide, lsem.at[0])
     loads = [
-        pltpu.make_async_copy(wb_h, w_branch, lsem.at[2]),
-        pltpu.make_async_copy(wg_h, w_gelu, lsem.at[3]),
+        pltpu.make_async_copy(wb_h, w_branch, lsem.at[1]),
+        pltpu.make_async_copy(wg_h, w_gelu, lsem.at[2]),
     ]
-    for load in [block_load, *loads]:
+    for load in [normed_load, *loads]:
         load.start()
     greet(across + tok_targets())
+    last.launch()
     stats[ex.me] = stat[...]
     copies = []
     for m in range(1, n):
@@ -1559,23 +1685,7 @@
 
     smalls[ex.tok] = small[...]
     spread(smalls, sm_s, sm_r)
-    wo_line, wb_line, wg_line, gate_line = lines
-
-    def columns(source, block, line):
-        size = source.shape[1] // count
-        return source[:, pl.ds(pl.multiple_of(block * size, 128), size)]
-
-    def fill(line, product):
-        def far_side(z, _):
-            line.put_away(z, product(line.away(z)))
-            return 0
-
-        def near_side(z, _):
-            line.put_home(z, product(line.kept(z)))
-            return 0
-
-        lax.fori_loop(0, line.chips, far_side, 0)
-        lax.fori_loop(0, line.chips, near_side, 0)
+    wb_line, wg_line, gate_line = lines
 
     def start(line):
         line.join()
@@ -1583,15 +1693,11 @@
             line.step(line.chips - 1)
 
     fill(gate_line, lambda d: gate_blocks[d].astype(F32))
-    block_load.wait()
-    fill(wo_line, lambda d: tn_dot(branch[...], columns(wide, d, wo_line)))
-    normed_load.start()
-    start(wo_line)
     normed_load.wait()
-    fill(wb_line, lambda d: tn_dot(columns(wide, d, wb_line), g_rec[...]))
+    fill(wb_line, lambda d: tn_dot(block_columns(wide, d, count), g_rec[...]))
     start(gate_line)
     start(wb_line)
-    fill(wg_line, lambda d: tn_dot(columns(wide, d, wg_line), g_pre[...]))
+    fill(wg_line, lambda d: tn_dot(block_columns(wide, d, count), g_pre[...]))
     start(wg_line)
     for load in loads:
         load.wait()
@@ -1648,8 +1754,8 @@
     turns = ex.chunks + len(stages) - 1
     acts = [
         functools.partial(line.step, far)
-        for far in range(wo_line.chips - 2, 0, -1)
-        for line in (wo_line, gate_line, wb_line, wg_line)
+        for far in range(wb_line.chips - 2, 0, -1)
+        for line in (gate_line, wb_line, wg_line)
     ]
 
     def extra(t):
@@ -1669,7 +1775,7 @@
     small_o[...] = all_small[:8]
     taps_o[...] = all_small[4:8, :chans]
     mlp_o[...] = all_small[8:9, :width]
-    wo_line.settle(wo_o)
+    last.settle(wo_o)
     gate_line.settle(gate_o)
     wb_line.settle(wb_o)
     wg_line.settle(wg_o)
@@ -1685,8 +1791,8 @@
 
 
 def end_exchange(
-    g_rec, g_pre, w_branch, w_gelu, stat, small, normed, branch, g_block, gate_blocks, x_own,
-    scale, gain, mid_own, ident,
+    g_rec, g_pre, w_branch, w_gelu, stat, small, normed, carry, gate_blocks, x_own, scale, gain,
+    mid_own, ident,
 ):
     n, count = lax.axis_size("ch"), lax.axis_size("tok")
     rows, width = x_own.shape
@@ -1694,28 +1800,28 @@
     chunks = stat.shape[0]
     ex = Exchange(n, rows, width, chunks, False)
     lines = [
-        Line(count, (chans, total // count)),
         Line(count, (total // count, chans)),
         Line(count, (total // count, chans)),
         Line(count, gate_blocks.shape[1:]),
     ]
+    last = LastHop(count, carry.shape[1:])
     anywhere = pl.BlockSpec(memory_space=pl.ANY)
     vmem = pl.BlockSpec(memory_space=pltpu.VMEM)
     sem = pltpu.SemaphoreType.DMA
     return pl.pallas_call(
-        functools.partial(end_kernel, ex, lines),
+        functools.partial(end_kernel, ex, last, lines),
         out_shape=[
             jax.ShapeDtypeStruct((rows, width), F32),
             jax.ShapeDtypeStruct((8, small.shape[1]), F32),
             jax.ShapeDtypeStruct((1, width), F32),
             jax.ShapeDtypeStruct((1, width), F32),
             jax.ShapeDtypeStruct((4, chans), F32),
+            jax.ShapeDtypeStruct(lines[0].shape, F32),
             jax.ShapeDtypeStruct(lines[1].shape, F32),
+            jax.ShapeDtypeStruct(last.shape, F32),
             jax.ShapeDtypeStruct(lines[2].shape, F32),
-            jax.ShapeDtypeStruct(lines[0].shape, F32),
-            jax.ShapeDtypeStruct(lines[3].shape, F32),
         ],
-        in_specs=[anywhere if i in (2, 3, 6, 8) else vmem for i in range(14)],
+        in_specs=[anywhere if i in (2, 3, 6) else vmem for i in range(13)],
         out_specs=[anywhere] + whole_vmem(8),
         scratch_shapes=[
             pltpu.VMEM((rows // SEGS, SEGS, width), F32),
@@ -1723,7 +1829,7 @@
             pltpu.VMEM(w_branch.shape, BF16),
             pltpu.VMEM(w_gelu.shape, BF16),
             sem((SEGS, chunks)),
-            sem((4,)),
+            sem((3,)),
             pltpu.VMEM((n, *stat.shape), F32),
             pltpu.VMEM(stat.shape, F32),
             pltpu.VMEM((count, *small.shape), F32),
@@ -1734,12 +1840,13 @@
             sem((count - 1,)), sem((count - 1,)),
         ]
         + [shape for line in lines for shape in line.scratch()]
+        + last.scratch()
         + ex.scratch(),
         compiler_params=pltpu.CompilerParams(
             collective_id=ident, has_side_effects=True, vmem_limit_bytes=63 << 20
         ),
-    )(g_rec, g_pre, w_branch, w_gelu, stat, small, normed, branch, g_block, gate_blocks, x_own,
-      scale, gain, mid_own)
+    )(g_rec, g_pre, w_branch, w_gelu, stat, small, normed, carry, gate_blocks, x_own, scale, gain,
+      mid_own)
 
 
 def to_major(rows):
@@ -1773,28 +1880,28 @@
     )(a, b)
 
 
-def weight_kernel(spans, a, *refs):
-    out, at = refs[-1], 0
-    for b, (first, last) in zip(refs, spans, strict=False):
-        width = last - first
-        out[:, at : at + width] = tn_dot(a[...], b[:, first:last]).astype(BF16)
-        at += width
-
-
-def weight_product(a, *parts):
+def weight_kernel(plan, a, *refs):
+    for out, parts in zip(refs[-len(plan) :], plan, strict=True):
+        at = 0
+        for i, first, last in parts:
+            width = last - first
+            out[:, at : at + width] = tn_dot(a[...], refs[i][:, first:last]).astype(BF16)
+            at += width
+
+
+def weight_products(a, sources, plan):
     rows, left = a.shape
-    spans = [span for _, span in parts]
-    right = sum(last - first for first, last in spans)
+    widths = [sum(last - first for _, first, last in parts) for parts in plan]
     size = next(t for t in (256, 128, left) if left % t == 0)
     return pl.pallas_call(
-        functools.partial(weight_kernel, spans),
+        functools.partial(weight_kernel, plan),
         grid=(left // size,),
-        out_shape=jax.ShapeDtypeStruct((left, right), BF16),
+        out_shape=[jax.ShapeDtypeStruct((left, width), BF16) for width in widths],
         in_specs=[pl.BlockSpec((rows, size), lambda i: (0, i))]
-        + [pl.BlockSpec(b.shape, lambda i: (0, 0)) for b, _ in parts],
-        out_specs=pl.BlockSpec((size, right), lambda i: (i, 0)),
+        + [pl.BlockSpec(b.shape, lambda i: (0, 0)) for b in sources],
+        out_specs=[pl.BlockSpec((size, width), lambda i: (i, 0)) for width in widths],
         compiler_params=pltpu.CompilerParams(vmem_limit_bytes=62 << 20),
-    )(a, *[b for b, _ in parts])
+    )(a, *sources)
 
 
 def tok_scatter(full, dim):
@@ -1889,11 +1996,11 @@
     column = ch_index * width
     chans = decay_param.shape[0]
     gates, gate_width = w_rgate.shape[0], w_rgate.shape[1]
-    layer_in, cotangent = to_major(layer_in), to_major(cotangent)
+    layer_in = to_major(layer_in)
     pos = positions.reshape(SEGS, rows // SEGS)
     (
         normed, scale_in, gate_pre, ext, conv, rate, igate, lru, branch, cot, vectors, dense_r,
-        dense_i, pos_tall,
+        dense_i, pos_tall, cotangent,
     ) = front(
         layer_in, norm_gain[None], pos, w_branch, w_gelu, conv_w, conv_b, b_rgate, b_igate,
         decay_param, w_rgate.reshape(-1, gate_width), w_igate.reshape(-1, gate_width),
@@ -1904,13 +2011,13 @@
     )
     count = lax.axis_size("tok")
     total, units = cot.shape[1], hidden.shape[1]
-    cut = units // 3
-    wdown_full = weight_product(hidden, (cot, (0, total)))
+    cut = units // 2
+    (wdown_full,) = weight_products(hidden, (cot,), (((0, 0, total),),))
     grad_up, wdown_full = lax.optimization_barrier((grad_up, wdown_full))
     grad_wdown = tok_scatter(wdown_full, 1)
-    wup_one = weight_product(normed_mid, (grad_up, (0, cut)))
-    grad_gate, wup_one = lax.optimization_barrier((grad_gate, wup_one))
-    wide_full = weight_product(normed_mid, (grad_gate, (0, units)), (grad_up, (cut, units)))
+    wide_full, wup_one = weight_products(
+        normed_mid, (grad_gate, grad_up), (((0, 0, units), (1, cut, units)), ((1, 0, cut),))
+    )
     wide_sum = tok_scatter(wide_full, 0)
     hidden, wide_full = lax.optimization_barrier((hidden, wide_full))
     down = rows_product(hidden, w_down)
@@ -1919,9 +2026,9 @@
         grad_gate, grad_up, w_gate, w_up, mid_full, mid_own, cot, cotangent, scale_mid,
         mlp_gain[None], wup_one, 3,
     )
-    grad_rec, grad_gate_pre, gate_parts, sums, row_term, mlp_out = recur_bwd(
+    grad_rec, grad_gate_pre, gate_parts, sums, row_term, mlp_out, wout_carry = recur_bwd(
         grad_block, w_out, gate_pre, ext, conv, rate, igate, lru, pos_tall, conv_w, dense_r,
-        dense_i, vectors, down, gate_width, 4,
+        dense_i, vectors, down, branch, gate_width, 4,
     )
     layer_out = from_major((mid_own + mlp_out).astype(BF16))
     grad_rec, layer_out = lax.optimization_barrier((grad_rec, layer_out))
@@ -1940,8 +2047,8 @@
         input_grad, small_sum, norm_gain_sum, mlp_gain_sum, taps_sum, grad_wbranch, grad_wgelu,
         grad_wout, gate_sum,
     ) = end_exchange(
-        grad_rec, grad_gate_pre, w_branch, w_gelu, stat, small, normed, branch, grad_block,
-        gate_parts, layer_in, scale_in, norm_gain[None], grad_mid_own, 5,
+        grad_rec, grad_gate_pre, w_branch, w_gelu, stat, small, normed, wout_carry, gate_parts,
+        layer_in, scale_in, norm_gain[None], grad_mid_own, 5,
     )
     (
         input_grad, grad_wbranch, grad_wgelu, grad_wout, own_norm_gain, own_mlp_gain, grad_taps,

time: 495 us -> 491 us (level)
    pallas_call x5 -> x4, Pallas kernels: 179 us -> 165 us  [the longest x1 79.2 us: end_exchange(): pl.pallas_call(functools.partial(end_kernel, ex, last, lines), out_shape=...]
    pallas_call x1, Pallas kernels: 90.8 us -> 101 us  [back_exchange(): pl.pallas_call(functools.partial(back_kernel, ex, half), out_shape=[jax.S...]
where the time goes in v4:
time: 491 us; the launch traced here: 483 us
  Pallas kernels  460 us (94%)
  between operations  14.6 us (3%)
    pallas_call x1, Pallas kernels, back_exchange(): pl.pallas_call(functools.partial(back_kernel, ex, half), out_shape=[jax.S...  101 us
    pallas_call x1, Pallas kernels, front(): pl.pallas_call(functools.partial(front_kernel, ga, late), out_shape=[jax....  88.1 us
    pallas_call x1, Pallas kernels, mid_exchange(): pl.pallas_call(functools.partial(mid_kernel, ex), out_shape=[whole, jax.S...  86.8 us
    pallas_call x1, Pallas kernels, end_exchange(): pl.pallas_call(functools.partial(end_kernel, ex, last, lines), out_shape=...  79.2 us
    pallas_call x1, Pallas kernels, recur_bwd(): pl.pallas_call(functools.partial(recur_bwd_kernel, ex, line), out_shape=[...  55.5 us
    pallas_call x2, Pallas kernels, weight_products(): pl.pallas_call(functools.partial(weight_kernel, plan), grid=(left // size...  30.4 us
    pallas_call x1, Pallas kernels, rows_product(): pl.pallas_call(rows_kernel, grid=(rows // size,), out_shape=jax.ShapeDtyp...  11.3 us
  transfers between devices with their start and end apart: 2, of which 0 were waited for; matrix products, arithmetic and copies ran while one was open for 1% of the time, Pallas kernels for 55%

profile of v4, /device:TPU:0, one launch (start us, length us, event | category | flops | bytes accessed | tf_op | source)
XLA Modules:
  0.0 482.8 jit_solution(7918277139187932773)
XLA Ops:
  7.2 0.0 reduce-scatter.5.cloned.1.call-start
  7.2 2.8 copy.40
  10.0 88.1 %shard_map.305 = (bf16[1024,2048]{1,0:T(8,128)(2,1)}, f32[1024,1]{1,0:T(8,128)}, f32[1024,640]{1,0:T(8,128)}, f32[1048,640]{1,0:T(8,128)}, f32[1024,640]{1,0:T(8...) custom-call(bf16[1024,512]{1,0:T(8,128)(2,1)} %bitcast.20, ...), custom_call_target="tpu_custom_call" | custom-call | tf_op jit(solution)/shard_map/pallas_call | solution.py:545
  98.1 86.8 %shard_map.306 = (bf16[1024,2048]{1,0:T(8,128)(2,1)}, bf16[4,2,1024,256]{3,2,1,0:T(8,128)(2,1)}, f32[1024,512]{1,0:T(8,128)}, f32[1024,1]{1,0:T(8,128)}, bf16[10...) custom-call(bf16[1024,640]{1,0:T(8,128)(2,1)} %get-tuple-element.84.branch.branch_h, ...), custom_call_target="tpu_custom_call" | custom-call | tf_op jit(solution)/shard_map/pallas_call | solution.py:1151
  184.9 11.4 %shard_map.307 = bf16[1536,2048]{1,0:T(8,128)(2,1)} custom-call(bf16[1024,1536]{1,0:T(8,128)(2,1)} %get-tuple-element.92.a, bf16[1024,2048]{1,0:T(8,128)(2,1)} %get-tuple-element.85.cot_h.refs_0_), custom_call_target="tpu_custom_call" | custom-call | tf_op jit(solution)/shard_map/pallas_call | solution.py:1896
  196.4 0.0 reduce-scatter.5.cloned.1.call-update
  196.4 0.0 reduce-scatter.3.cloned.1.call-start
  196.4 18.9 %shard_map.308 = (bf16[2048,2304]{1,0:T(8,128)(2,1)}, bf16[2048,768]{1,0:T(8,128)(2,1)}) custom-call(bf16[1024,2048]{1,0:T(8,128)(2,1)} %get-tuple-element.88.a, bf16[1024,1536]{1,0:T(8,128)(2,1)} %get-tuple-element.93.refs_0_.gg_h, bf16[1024,1536]{1,0:T(8,128)(2,1)} %get-tuple-element.90.refs_1_.gu_h), custom_call_target="tpu_custom_call" | custom-call | tf_op jit(solution)/shard_map/pallas_call | solution.py:1896
  215.4 0.0 reduce-scatter.3.cloned.1.call-update
  215.4 11.3 %shard_map.309.down = bf16[1024,2048]{1,0:T(8,128)(2,1)} custom-call(bf16[1024,1536]{1,0:T(8,128)(2,1)} %get-tuple-element.92.a, bf16[1536,2048]{1,0:T(8,128)(2,1)} %b.1), custom_call_target="tpu_custom_call" | custom-call | tf_op jit(solution)/shard_map/pallas_call | solution.py:1870
  226.7 101.3 %shard_map.310 = (bf16[1024,2048]{1,0:T(8,128)(2,1)}, f32[1024,512]{1,0:T(8,128)}, f32[8,512]{1,0:T(8,128)}, f32[256,768]{1,0:T(8,128)}) custom-call(bf16[1024,1536]{1,0:T(8,128)(2,1)} %get-tuple-element.93.refs_0_.gg_h, bf16[1024,1536]{1,0:T(8,128)(2,1)} %get-tuple-element.90.refs_1_.gu_h, bf16[2048,1536]{1,0:T(8,128)(2,1)} %wg_h.6, ...), custom_call_target="tpu_custom_call" | custom-call | tf_op jit(solution)/shard_map/pallas_call | solution.py:1420
  328.0 55.5 %shard_map.311 = (bf16[1024,640]{1,0:T(8,128)(2,1)}, bf16[1024,640]{1,0:T(8,128)(2,1)}, f32[8,160,160]{2,1,0:T(8,128)}, f32[8,640]{1,0:T(8,128)}, f32[1024,1]{1,...) custom-call(bf16[1024,2048]{1,0:T(8,128)(2,1)} %get-tuple-element.99.g_block_h, bf16[640,2048]{1,0:T(8,128)(2,1)} %w_out_h.1, ...), custom_call_target="tpu_custom_call" | custom-call | tf_op jit(solution)/shard_map/pallas_call | solution.py:816
  383.5 0.0 copy-start.2
  383.5 0.0 copy-start
  383.5 2.6 fusion
  386.1 0.0 copy-start.1
  386.1 1.3 copy.38
  387.4 0.0 copy-done.2
  387.4 0.0 copy-done
  387.5 0.8 reduce
  388.3 0.0 copy-done.1
  388.3 0.6 select_maximum_fusion.small
  388.9 79.2 %shard_map.312 = (f32[1024,512]{1,0:T(8,128)}, f32[8,640]{1,0:T(8,128)}, f32[1,512]{1,0:T(1,128)}, f32[1,512]{1,0:T(1,128)}, f32[4,640]{1,0:T(4,128)}, /*index=5...) custom-call(bf16[1024,640]{1,0:T(8,128)(2,1)} %get-tuple-element.114.g_rec, ...), custom_call_target="tpu_custom_call" | custom-call | tf_op jit(solution)/shard_map/pallas_call | solution.py:1811
  468.1 0.0 reduce-scatter.5.cloned.1.call-done.down
  468.2 0.0 reduce-scatter.3.cloned.1.call-done.wide
  468.2 7.3 %shard_map.313 = (f32[1024,512]{1,0:T(8,128)}, f32[256,640]{1,0:T(8,128)}, f32[256,640]{1,0:T(8,128)}, f32[640,256]{1,0:T(8,128)}, f32[512]{0:T(512)}, /*index=5...) custom-call(f32[1024,512]{1,0:T(8,128)} %get-tuple-element.124.input, ...), custom_call_target="tpu_custom_call" | custom-call | tf_op jit(solution)/shard_map/pallas_call | solution.py:1959
  (1 shorter events, 0.0 us)
Async XLA Ops:
  7.2 461.0 %reduce-scatter.5.cloned.1.call-start = ((), (), s32[]{:S(2)}) async-start(), calls=%async_computation.3 | async-start | bytes 7077888 | tf_op jit(solution)/shard_map/reduce_scatter | solution.py:1908
  196.4 271.8 %reduce-scatter.3.cloned.1.call-start = ((), (), s32[]{:S(2)}) async-start(), calls=%async_computation.2 | async-start | bytes 10616832 | tf_op jit(solution)/shard_map/reduce_scatter | solution.py:1908
  383.5 3.9 copy-start.2
  383.5 4.0 copy-start
  386.1 2.1 copy-start.1
Sparse Core Ops, SparseCore 0:
  196.5 83.9 reduce-scatter.4
  282.8 124.5 reduce-scatter.2

commit v5 on v4

--- a/solution.py
+++ b/solution.py
@@ -1284,13 +1284,14 @@
 
 
 def back_kernel(
-    ex, half, gg_h, gu_h, wg_h, wu_h, full_h, mid_own, cot_h, cot_own, scale, gain, source,
-    block_o, own_o, gain_o, sum_o,
+    ex, halves, gg_h, gu_h, wg_h, wu_h, full_h, mid_own, cot_h, cot_own, scale, gain, source_a, source_b,
+    block_o, own_o, gain_o, sum_a, sum_b,
     gg, gu, w_gate, w_up, full, cot, gsem, wsem, fsem, *refs,
 ):
-    held = len(half.scratch())
-    half.bind(refs[:held], source)
-    ex.bind(refs[held:])
+    held = len(halves[0].scratch())
+    for i, source in enumerate((source_a, source_b)):
+        halves[i].bind(refs[i * held : (i + 1) * held], source)
+    ex.bind(refs[2 * held :])
     n, width = ex.n, ex.width
     order = sorted(range(n), key=lambda m: -m.bit_count())
 
@@ -1325,8 +1326,9 @@
             copy.start()
     for copy in final_load(0):
         copy.start()
-    greet(ex.neighbours() + half.targets())
-    half.launch()
+    greet(ex.neighbours() + halves[0].targets())
+    for half in halves:
+        half.launch()
     gain_o[...] = jnp.zeros_like(gain_o)
 
     def first(c):
@@ -1393,40 +1395,45 @@
     stages += [functools.partial(ex.gather_pass, s) for s in range(1, ex.bits)]
     stages += [final]
     turns = ex.chunks + len(stages) - 1
-    acts = [half.join] + [functools.partial(half.step, s) for s in range(1, half.bits)]
+    acts = [(0, half.join) for half in halves]
+    for i, half in enumerate(halves):
+        for step in range(1, half.bits):
+            turn = min(2 * step + 1 + 2 * i, turns - 1)
+            acts.append((turn, functools.partial(half.step, step)))
 
     def after(t):
-        for i, act in enumerate(acts):
-
-            @pl.when(t == min(i * turns // len(acts) + i, turns - 1))
-            def _():
+        for turn, act in acts:
+
+            @pl.when(t == turn)
+            def _(act=act):
                 act()
 
     ex.run(stages, after=after)
-    half.settle(sum_o)
+    halves[0].settle(sum_a)
+    halves[1].settle(sum_b)
 
 
 def back_exchange(
-    grad_gate, grad_up, w_gate, w_up, full, mid_own, cot, cot_own, scale, gain_own, source, ident,
-    chunks=4,
+    grad_gate, grad_up, w_gate, w_up, full, mid_own, cot, cot_own, scale, gain_own, sources,
+    ident, chunks=4,
 ):
     n, count = lax.axis_size("ch"), lax.axis_size("tok")
     rows, width = mid_own.shape
     ex = Exchange(n, rows, width, chunks, True)
-    half = Halving(count, *source.shape)
+    halves = [Halving(count, *source.shape) for source in sources]
     sem = pltpu.SemaphoreType.DMA
     anywhere = pl.BlockSpec(memory_space=pl.ANY)
     vmem = pl.BlockSpec(memory_space=pltpu.VMEM)
     return pl.pallas_call(
-        functools.partial(back_kernel, ex, half),
+        functools.partial(back_kernel, ex, halves),
         out_shape=[
             jax.ShapeDtypeStruct((rows, n * width), BF16),
             jax.ShapeDtypeStruct((rows, width), F32),
             jax.ShapeDtypeStruct((8, width), F32),
-            jax.ShapeDtypeStruct((half.rows, half.columns), F32),
-        ],
-        in_specs=[anywhere] * 5 + [vmem, anywhere, vmem, vmem, vmem, anywhere],
-        out_specs=[vmem] * 4,
+        ]
+        + [jax.ShapeDtypeStruct((half.rows, half.columns), F32) for half in halves],
+        in_specs=[anywhere] * 5 + [vmem, anywhere, vmem, vmem, vmem, anywhere, anywhere],
+        out_specs=[vmem] * 5,
         scratch_shapes=[
             pltpu.VMEM(grad_gate.shape, BF16),
             pltpu.VMEM(grad_up.shape, BF16),
@@ -1436,12 +1443,12 @@
             pltpu.VMEM((ex.size, n * width), BF16),
             sem((2, chunks)), sem((2, n)), sem((2,)),
         ]
-        + half.scratch()
+        + [shape for half in halves for shape in half.scratch()]
         + ex.scratch(),
         compiler_params=pltpu.CompilerParams(
             collective_id=ident, has_side_effects=True, vmem_limit_bytes=63 << 20
         ),
-    )(grad_gate, grad_up, w_gate, w_up, full, mid_own, cot, cot_own, scale, gain_own, source)
+    )(grad_gate, grad_up, w_gate, w_up, full, mid_own, cot, cot_own, scale, gain_own, *sources)
 
 
 class Line:
@@ -1909,7 +1916,7 @@
 
 
 def close_kernel(
-    input_in, wb_in, wg_in, wo_in, small, mlp, gain, taps, gate, wide, left, down,
+    input_in, wb_in, wg_in, wo_in, small, mlp, gain, taps, gate, wide, left_a, left_b, down,
     input_o, wb_o, wg_o, wo_o, gain_o, mlp_o, taps_o, convb_o, br_o, bi_o, decay_o, wr_o, wi_o,
     wgate_o, wup_o, wdown_o, sem,
 ):
@@ -1918,13 +1925,14 @@
     for copy in copies:
         copy.start()
     units = wgate_o.shape[1]
-    cut = left.shape[1]
+    cut = left_a.shape[1]
 
     def rows(at):
         span = pl.ds(at, 16)
         wgate_o[span, :] = wide[span, :units].astype(F32)
-        wup_o[span, :cut] = left[span, :]
-        wup_o[span, cut:] = wide[span, units:].astype(F32)
+        wup_o[span, :cut] = left_a[span, :]
+        wup_o[span, cut : 2 * cut] = left_b[span, :]
+        wup_o[span, 2 * cut :] = wide[span, units:].astype(F32)
 
     over_rows(0, wgate_o.shape[0], 16, rows, 2)
 
@@ -1964,11 +1972,11 @@
             like(each, gates, block), like(each, gates, block), like(wide.shape[0], units),
             like(wide.shape[0], units), like(*down.shape),
         ],
-        in_specs=[vmem] * 12,
+        in_specs=[vmem] * 13,
         out_specs=[anywhere] * 4 + [vmem] * 12,
         scratch_shapes=[pltpu.SemaphoreType.DMA((4,))],
         compiler_params=pltpu.CompilerParams(vmem_limit_bytes=60 << 20),
-    )(input_in, wb, wg, wo, small, mlp, gain, taps, gate, wide, left, down)
+    )(input_in, wb, wg, wo, small, mlp, gain, taps, gate, wide, *left, down)
 
 
 def local(
@@ -2011,20 +2019,22 @@
     )
     count = lax.axis_size("tok")
     total, units = cot.shape[1], hidden.shape[1]
-    cut = units // 2
+    cut = units // 3
     (wdown_full,) = weight_products(hidden, (cot,), (((0, 0, total),),))
     grad_up, wdown_full = lax.optimization_barrier((grad_up, wdown_full))
     grad_wdown = tok_scatter(wdown_full, 1)
-    wide_full, wup_one = weight_products(
-        normed_mid, (grad_gate, grad_up), (((0, 0, units), (1, cut, units)), ((1, 0, cut),))
+    wide_full, *wup_parts = weight_products(
+        normed_mid,
+        (grad_gate, grad_up),
+        (((0, 0, units), (1, 2 * cut, units)), ((1, 0, cut),), ((1, cut, 2 * cut),)),
     )
     wide_sum = tok_scatter(wide_full, 0)
     hidden, wide_full = lax.optimization_barrier((hidden, wide_full))
     down = rows_product(hidden, w_down)
     grad_gate, down = lax.optimization_barrier((grad_gate, down))
-    grad_block, grad_mid_own, gain_sum, wup_left = back_exchange(
+    grad_block, grad_mid_own, gain_sum, *wup_left = back_exchange(
         grad_gate, grad_up, w_gate, w_up, mid_full, mid_own, cot, cotangent, scale_mid,
-        mlp_gain[None], wup_one, 3,
+        mlp_gain[None], wup_parts, 3,
     )
     grad_rec, grad_gate_pre, gate_parts, sums, row_term, mlp_out, wout_carry = recur_bwd(
         grad_block, w_out, gate_pre, ext, conv, rate, igate, lru, pos_tall, conv_w, dense_r,

time: 491 us -> 486 us (0.990)
  Pallas kernels: 460 us -> 455 us
    pallas_call x1, Pallas kernels: 101 us -> 84.9 us  [back_exchange(): pl.pallas_call(functools.partial(back_kernel, ex, halves), out_shape=[jax...]
    pallas_call x1, Pallas kernels: 79.2 us -> 91.7 us  [end_exchange(): pl.pallas_call(functools.partial(end_kernel, ex, last, lines), out_shape=...]
where the time goes in v5:
time: 486 us; the launch traced here: 478 us
  Pallas kernels  455 us (94%)
  between operations  14.6 us (3%)
    pallas_call x1, Pallas kernels, end_exchange(): pl.pallas_call(functools.partial(end_kernel, ex, last, lines), out_shape=...  91.7 us
    pallas_call x1, Pallas kernels, front(): pl.pallas_call(functools.partial(front_kernel, ga, late), out_shape=[jax....  88.2 us
    pallas_call x1, Pallas kernels, mid_exchange(): pl.pallas_call(functools.partial(mid_kernel, ex), out_shape=[whole, jax.S...  86.9 us
    pallas_call x1, Pallas kernels, back_exchange(): pl.pallas_call(functools.partial(back_kernel, ex, halves), out_shape=[jax...  84.9 us
    pallas_call x1, Pallas kernels, recur_bwd(): pl.pallas_call(functools.partial(recur_bwd_kernel, ex, line), out_shape=[...  54 us
    pallas_call x2, Pallas kernels, weight_products(): pl.pallas_call(functools.partial(weight_kernel, plan), grid=(left // size...  30.3 us
    pallas_call x1, Pallas kernels, rows_product(): pl.pallas_call(rows_kernel, grid=(rows // size,), out_shape=jax.ShapeDtyp...  11.3 us
  transfers between devices with their start and end apart: 2, of which 0 were waited for; matrix products, arithmetic and copies ran while one was open for 1% of the time, Pallas kernels for 55%

profile of v5, /device:TPU:0, one launch (start us, length us, event | category | flops | bytes accessed | tf_op | source)
XLA Modules:
  0.0 477.5 jit_solution(9535949824953810753)
XLA Ops:
  7.2 0.0 reduce-scatter.5.cloned.1.call-start
  7.2 2.8 copy.40
  10.0 88.2 %shard_map.305 = (bf16[1024,2048]{1,0:T(8,128)(2,1)}, f32[1024,1]{1,0:T(8,128)}, f32[1024,640]{1,0:T(8,128)}, f32[1048,640]{1,0:T(8,128)}, f32[1024,640]{1,0:T(8...) custom-call(bf16[1024,512]{1,0:T(8,128)(2,1)} %bitcast.20, ...), custom_call_target="tpu_custom_call" | custom-call | tf_op jit(solution)/shard_map/pallas_call | solution.py:545
  98.2 86.9 %shard_map.306 = (bf16[1024,2048]{1,0:T(8,128)(2,1)}, bf16[4,2,1024,256]{3,2,1,0:T(8,128)(2,1)}, f32[1024,512]{1,0:T(8,128)}, f32[1024,1]{1,0:T(8,128)}, bf16[10...) custom-call(bf16[1024,640]{1,0:T(8,128)(2,1)} %get-tuple-element.86.branch.branch_h, ...), custom_call_target="tpu_custom_call" | custom-call | tf_op jit(solution)/shard_map/pallas_call | solution.py:1151
  185.2 11.4 %shard_map.307 = bf16[1536,2048]{1,0:T(8,128)(2,1)} custom-call(bf16[1024,1536]{1,0:T(8,128)(2,1)} %get-tuple-element.94.a, bf16[1024,2048]{1,0:T(8,128)(2,1)} %get-tuple-element.87.cot_h.refs_0_), custom_call_target="tpu_custom_call" | custom-call | tf_op jit(solution)/shard_map/pallas_call | solution.py:1903
  196.6 0.0 reduce-scatter.5.cloned.1.call-update
  196.6 0.0 reduce-scatter.3.cloned.1.call-start
  196.6 18.9 %shard_map.308 = (bf16[2048,2048]{1,0:T(8,128)(2,1)}, bf16[2048,512]{1,0:T(8,128)(2,1)}, bf16[2048,512]{1,0:T(8,128)(2,1)}) custom-call(bf16[1024,2048]{1,0:T(8,128)(2,1)} %get-tuple-element.90.a, bf16[1024,1536]{1,0:T(8,128)(2,1)} %get-tuple-element.95.refs_0_.gg_h, bf16[1024,1536]{1,0:T(8,128)(2,1)} %get-tuple-element.92.refs_1_.gu_h), custom_call_target="tpu_custom_call" | custom-call | tf_op jit(solution)/shard_map/pallas_call | solution.py:1903
  215.5 0.0 reduce-scatter.3.cloned.1.call-update
  215.5 11.3 %shard_map.309.down = bf16[1024,2048]{1,0:T(8,128)(2,1)} custom-call(bf16[1024,1536]{1,0:T(8,128)(2,1)} %get-tuple-element.94.a, bf16[1536,2048]{1,0:T(8,128)(2,1)} %b.1), custom_call_target="tpu_custom_call" | custom-call | tf_op jit(solution)/shard_map/pallas_call | solution.py:1877
  226.8 84.9 %shard_map.310 = (bf16[1024,2048]{1,0:T(8,128)(2,1)}, f32[1024,512]{1,0:T(8,128)}, f32[8,512]{1,0:T(8,128)}, f32[256,512]{1,0:T(8,128)}, f32[256,512]{1,0:T(8,128)}) custom-call(bf16[1024,1536]{1,0:T(8,128)(2,1)} %get-tuple-element.95.refs_0_.gg_h, bf16[1024,1536]{1,0:T(8,128)(2,1)} %get-tuple-element.92.refs_1_.gu_h, bf16[2048,1536]{1,0:T(8,128)(2,1)} %wg_h.6, ...), custom_call_target="tpu_custom_call" | custom-call | tf_op jit(solution)/shard_map/pallas_call | solution.py:1427
  311.7 54.0 %shard_map.311 = (bf16[1024,640]{1,0:T(8,128)(2,1)}, bf16[1024,640]{1,0:T(8,128)(2,1)}, f32[8,160,160]{2,1,0:T(8,128)}, f32[8,640]{1,0:T(8,128)}, f32[1024,1]{1,...) custom-call(bf16[1024,2048]{1,0:T(8,128)(2,1)} %get-tuple-element.102.g_block_h, ...), custom_call_target="tpu_custom_call" | custom-call | tf_op jit(solution)/shard_map/pallas_call | solution.py:816
  365.7 0.0 copy-start.2
  365.8 0.0 copy-start
  365.8 2.6 fusion
  368.4 0.0 copy-start.1
  368.4 1.3 copy.38
  369.7 0.0 copy-done.2
  369.7 0.0 copy-done
  369.7 0.8 reduce
  370.5 0.0 copy-done.1
  370.5 0.6 select_maximum_fusion.small
  371.2 91.7 %shard_map.312 = (f32[1024,512]{1,0:T(8,128)}, f32[8,640]{1,0:T(8,128)}, f32[1,512]{1,0:T(1,128)}, f32[1,512]{1,0:T(1,128)}, f32[4,640]{1,0:T(4,128)}, /*index=5...) custom-call(bf16[1024,640]{1,0:T(8,128)(2,1)} %get-tuple-element.117.g_rec, ...), custom_call_target="tpu_custom_call" | custom-call | tf_op jit(solution)/shard_map/pallas_call | solution.py:1818
  462.9 0.0 reduce-scatter.5.cloned.1.call-done.down
  462.9 0.0 reduce-scatter.3.cloned.1.call-done.wide
  462.9 7.3 %shard_map.313 = (f32[1024,512]{1,0:T(8,128)}, f32[256,640]{1,0:T(8,128)}, f32[256,640]{1,0:T(8,128)}, f32[640,256]{1,0:T(8,128)}, f32[512]{0:T(512)}, /*index=5...) custom-call(f32[1024,512]{1,0:T(8,128)} %get-tuple-element.127.input, ...), custom_call_target="tpu_custom_call" | custom-call | tf_op jit(solution)/shard_map/pallas_call | solution.py:1967
  (1 shorter events, 0.0 us)
Async XLA Ops:
  7.2 455.7 %reduce-scatter.5.cloned.1.call-start = ((), (), s32[]{:S(2)}) async-start(), calls=%async_computation.3 | async-start | bytes 7077888 | tf_op jit(solution)/shard_map/reduce_scatter | solution.py:1915
  196.6 266.3 %reduce-scatter.3.cloned.1.call-start = ((), (), s32[]{:S(2)}) async-start(), calls=%async_computation.2 | async-start | bytes 9437184 | tf_op jit(solution)/shard_map/reduce_scatter | solution.py:1915
  365.7 3.9 copy-start.2
  365.8 4.0 copy-start
  368.4 2.1 copy-start.1
Sparse Core Ops, SparseCore 0:
  196.7 93.0 reduce-scatter.4
  292.1 121.0 reduce-scatter.2
